TPU v7x, 32 devices: a whole 2x2x4 slice. The times are simulated.
32 devices in a mesh: parts: 2 (over y), tile: 4 (over z), tm: 2 (over x), layer: 2 (over core).
Axes of the slice: x: 2, y: 2, z: 4, core: 2. Of those that a mesh axis runs over, the one named last changes fastest.
Arguments:
- u_start: float32 [4, 8, 64, 256], P(('parts', 'tm'), 'layer', 'tile'), parts along dimension 0, may hold values from -4 to 4
- flux: float32 [4, 64, 256], P(('parts', 'tm'), 'tile'), parts along dimension 0, may hold values from 0.003 to 0.03
- zone_of_cell: int32 [8, 64, 256], P('layer', 'tile'), may hold values from 0 to 15
- zone_row: int32 [16], replicated, may hold values from 0 to 7
- plane_rate: float32 [8], replicated, may hold values from 0.015 to 0.07
- thick_rate: float32 [8], replicated, may hold values from 0.02 to 0.1
- soften: float32 [8], replicated, may hold values from 0.05 to 0.15
Outputs:
- u_next: float32 [4, 8, 64, 256], P(('parts', 'tm'), 'layer', 'tile'), parts along dimension 0
There are 2 independent parts, one for each index of `parts`. A program takes and returns all parts, laid end to end along the dimension named above; an argument that names none is the same for every part. Nothing has to cross between parts.
All inputs are finite; a program needn't handle non-finite values.
Results may differ from a plain program's by a relative error of at most 0.0001.
Values sent between devices are 32-bit elements; how exact they have to be, the bound alone decides.
No kernel may reach another device: no remote copies, remote signals or barrier semaphores. Data moves between devices by JAX's collectives and lax.ppermute only.
A program may use at most 64 MiB of HBM per device.

v0:
```python
import jax
import jax.numpy as jnp
from jax import lax
from jax.sharding import PartitionSpec as P

FINE_STEPS = 8
COARSE_STEPS = 2


def with_halo(block, sides, width):
    for axis, dim in sides:
        count = lax.axis_size(axis)
        forward = [(i, i + 1) for i in range(count - 1)]
        backward = [(target, source) for source, target in forward]
        low = lax.ppermute(
            lax.slice_in_dim(block, block.shape[dim] - width, None, axis=dim), axis, forward
        )
        high = lax.ppermute(lax.slice_in_dim(block, 0, width, axis=dim), axis, backward)
        block = jnp.concatenate([low, block, high], axis=dim)
    return block


def shifted(value, axis, steps):
    count = lax.axis_size(axis)
    initial, last = (max(0, -steps), min(count, count - steps))
    return lax.ppermute(value, axis, [(source, source + steps) for source in range(initial, last)])


def edge_masks(start, count, total):
    positions = start + jnp.arange(count, dtype=jnp.int32)
    return ((positions > 0).astype(jnp.float32), (positions < total - 1).astype(jnp.float32))


def restrict_cells(field):
    depth, width, length = field.shape
    return field.reshape(depth // 2, 2, width // 2, 2, length // 2, 2).mean(axis=(1, 3, 5))


def restrict_surface(field):
    width, length = field.shape
    return field.reshape(width // 2, 2, length // 2, 2).mean(axis=(1, 3))


def prolong_cells(field):
    return jnp.repeat(jnp.repeat(jnp.repeat(field, 2, axis=0), 2, axis=1), 2, axis=2)


def diffuse(padded, plane_pad, thick_pad, soft_pad, z_low, z_high, x_low, x_high, source):
    k_plane = plane_pad * (1.0 + soft_pad * padded)
    k_thick = thick_pad * (1.0 + soft_pad * padded)
    center = padded[1:-1, 1:-1]
    c_plane = k_plane[1:-1, 1:-1]
    c_thick = k_thick[1:-1, 1:-1]
    gain = (
        0.5 * (c_thick + k_thick[:-2, 1:-1]) * (padded[:-2, 1:-1] - center) * z_low[:, None, None]
    )
    gain = (
        gain
        + 0.5 * (c_thick + k_thick[2:, 1:-1]) * (padded[2:, 1:-1] - center) * z_high[:, None, None]
    )
    gain = (
        gain
        + 0.5 * (c_plane + k_plane[1:-1, :-2]) * (padded[1:-1, :-2] - center) * x_low[None, :, None]
    )
    gain = (
        gain
        + 0.5 * (c_plane + k_plane[1:-1, 2:]) * (padded[1:-1, 2:] - center) * x_high[None, :, None]
    )
    flow = 0.5 * (c_plane[..., 1:] + c_plane[..., :-1]) * (center[..., 1:] - center[..., :-1])
    zeros_col = jnp.zeros(center.shape[:2] + (1,), jnp.float32)
    gain = (
        gain
        + jnp.concatenate([flow, zeros_col], axis=-1)
        - jnp.concatenate([zeros_col, flow], axis=-1)
    )
    return center + gain + source


def lookup_cells(zones, zone_row, plane_rate, thick_rate, soften):
    table_rows = plane_rate.shape[0]
    pick = (zone_row[:, None] == jnp.arange(table_rows, dtype=jnp.int32)[None, :]).astype(
        jnp.float32
    )
    zone_plane = jnp.sum(pick * plane_rate[None, :], axis=1)
    zone_thick = jnp.sum(pick * thick_rate[None, :], axis=1)
    zone_soft = jnp.sum(pick * soften[None, :], axis=1)
    cell_plane = jnp.zeros(zones.shape, jnp.float32)
    cell_thick = jnp.zeros(zones.shape, jnp.float32)
    cell_soft = jnp.zeros(zones.shape, jnp.float32)
    for zone_index in range(zone_row.shape[0]):
        inside = zones == zone_index
        cell_plane = jnp.where(inside, zone_plane[zone_index], cell_plane)
        cell_thick = jnp.where(inside, zone_thick[zone_index], cell_thick)
        cell_soft = jnp.where(inside, zone_soft[zone_index], cell_soft)
    return (cell_plane, cell_thick, cell_soft)


def on_device(u_start, flux, zone_of_cell, zone_row, plane_rate, thick_rate, soften):
    depth, width, length = zone_of_cell.shape
    tile_pos = lax.axis_index("tile")
    layer_pos = lax.axis_index("layer")
    width_all = width * lax.axis_size("tile")
    depth_all = depth * lax.axis_size("layer")
    fine_reach = 1
    heat_flux = flux[0]
    top_layer = (layer_pos * depth + jnp.arange(depth, dtype=jnp.int32) == 0).astype(jnp.float32)[
        :, None, None
    ]
    fine_source = top_layer * heat_flux[None]
    cell_plane, cell_thick, cell_soft = lookup_cells(
        zone_of_cell, zone_row, plane_rate, thick_rate, soften
    )
    fields = [cell_plane, cell_thick, cell_soft]
    coef_pad = with_halo(jnp.stack(fields), (("tile", 2), ("layer", 1)), fine_reach)
    plane_p, thick_p, soft_p = (coef_pad[0], coef_pad[1], coef_pad[2])
    fine_state = u_start[0]
    z_low, z_high = edge_masks(layer_pos * depth, depth, depth_all)
    x_low, x_high = edge_masks(tile_pos * width, width, width_all)
    for step_index in range(FINE_STEPS):
        padded = with_halo(fine_state, (("tile", 1), ("layer", 0)), 1)
        fine_state = diffuse(
            padded, plane_p, thick_p, soft_p, z_low, z_high, x_low, x_high, fine_source
        )
    u_own = u_start[0]
    c_depth = depth // 2
    c_width = width // 2
    c_total_depth = depth_all // 2
    c_total_width = width_all // 2
    coarse_top = (layer_pos * c_depth + jnp.arange(c_depth, dtype=jnp.int32) == 0).astype(
        jnp.float32
    )[:, None, None]
    coarse_source = 2.0 * coarse_top * restrict_surface(heat_flux)[None]
    coarse_coef = jnp.stack(
        [
            restrict_cells(cell_plane),
            restrict_cells(cell_thick),
            restrict_cells(cell_soft),
            coarse_source,
        ]
    )
    reach = COARSE_STEPS
    coarse_pad = with_halo(coarse_coef, (("tile", 2), ("layer", 1)), reach)

    def coarse_advance(state):
        offset = reach - 1
        region = coarse_pad[:, offset : offset + c_depth + 2, offset : offset + c_width + 2]
        inner_source = coarse_pad[3, reach : reach + c_depth, reach : reach + c_width]
        cz_low, cz_high = edge_masks(layer_pos * c_depth, c_depth, c_total_depth)
        cx_low, cx_high = edge_masks(tile_pos * c_width, c_width, c_total_width)
        for step_index in range(COARSE_STEPS):
            padded = with_halo(state, (("tile", 1), ("layer", 0)), 1)
            state = diffuse(
                padded,
                region[0],
                region[1],
                region[2],
                cz_low,
                cz_high,
                cx_low,
                cx_high,
                inner_source,
            )
        return state

    correction = fine_state - prolong_cells(coarse_advance(restrict_cells(u_own)))
    chain_pos = lax.axis_index("tm")
    rounds = lax.axis_size("tm") - 1

    def round_full(round_index, current):
        arrived = shifted(
            prolong_cells(coarse_advance(restrict_cells(current))) + correction, "tm", 1
        )
        return jnp.where(chain_pos == 0, current, arrived)

    settled = lax.fori_loop(0, rounds, round_full, u_own)
    coarse_start = restrict_cells(settled)
    result = prolong_cells(coarse_advance(coarse_start)) + correction
    return result[None]


def solution(mesh):
    return jax.shard_map(
        on_device,
        mesh=mesh,
        in_specs=(
            P(("parts", "tm"), "layer", "tile", None),
            P(("parts", "tm"), "tile", None),
            P("layer", "tile", None),
            P(),
            P(),
            P(),
            P(),
        ),
        out_specs=P(("parts", "tm"), "layer", "tile", None),
        check_vma=False,
    )
```

profile of v0, /device:TPU:0, one launch (start us, length us, event | category | flops | bytes accessed | tf_op | source)
XLA Modules:
  0.0 244.6 jit_solution(2061023713251855127)
XLA Ops:
  0.0 6.3 %reshape.127 = f32[2,2,8,2,128,2]{5,4,3,2,1,0:T(8,128)} reshape(f32[1,4,16,256]{3,2,1,0:T(8,128)} %param.7) | data formatting | bytes 131072 | tf_op jit(solution)/shard_map/while/body/eval_jaxpr/reshape | solution.py:36
  13.1 10.1 %select_select_fusion.2 = (f32[4,16,256]{2,1,0:T(8,128)S(1)}, pred[4,16,256]{2,1,0:T(8,128)(4,1)S(1)}, pred[4,16,256]{2,1,0:T(8,128)(4,1)S(1)}, pred[4,16,256]{2...) fusion(f32[]{:T(128)} %bitcast.16, f32[]{:T(128)} %bitcast.15, ...), kind=kLoop, calls=%fused_computation.359 | loop fusion | flops 524288 | bytes 393280 | tf_op jit(solution)/shard_map/jit(_where)/select_n | solution.py:92
  23.2 10.2 %select_select_fusion = f32[4,16,256]{2,1,0:T(8,128)S(1)} fusion(pred[4,16,256]{2,1,0:T(8,128)(4,1)S(1)} %get-tuple-element.50, pred[4,16,256]{2,1,0:T(8,128)(4,1)S(1)} %get-tuple-element.49, pred[4,16,256]{2,1,0:T(8,128)(4,1)S(1)} %get-tuple-element.48, pred[4,16,256]{2,1,0:T(8,128)(4,1)S(1)} %get-tuple-element.47, ...), kind=kLoop, calls=%fused_computation.357 | loop fusion | flops 262144 | bytes 327744 | tf_op jit(solution)/shard_map/jit(_where)/select_n | solution.py:94
  33.4 5.6 %reshape.130 = f32[2,2,8,2,128,2]{5,4,3,2,1,0:T(8,128)} reshape(f32[4,16,256]{2,1,0:T(8,128)S(1)} %select_select_fusion) | data formatting | bytes 131072 | tf_op jit(solution)/shard_map/reshape | solution.py:36
  42.2 10.0 %select_select_fusion.1 = f32[4,16,256]{2,1,0:T(8,128)S(1)} fusion(pred[4,16,256]{2,1,0:T(8,128)(4,1)S(1)} %get-tuple-element.50, pred[4,16,256]{2,1,0:T(8,128)(4,1)S(1)} %get-tuple-element.49, pred[4,16,256]{2,1,0:T(8,128)(4,1)S(1)} %get-tuple-element.48, pred[4,16,256]{2,1,0:T(8,128)(4,1)S(1)} %get-tuple-element.47, ...), kind=kLoop, calls=%fused_computation.358 | loop fusion | flops 262144 | bytes 327744 | tf_op jit(solution)/shard_map/jit(_where)/select_n | solution.py:93
  52.2 5.6 %reshape.129 = f32[2,2,8,2,128,2]{5,4,3,2,1,0:T(8,128)} reshape(f32[4,16,256]{2,1,0:T(8,128)S(1)} %select_select_fusion.1) | data formatting | bytes 131072 | tf_op jit(solution)/shard_map/reshape | solution.py:36
  60.3 5.6 %reshape.128 = f32[2,2,8,2,128,2]{5,4,3,2,1,0:T(8,128)} reshape(f32[4,16,256]{2,1,0:T(8,128)S(1)} %get-tuple-element.32) | data formatting | bytes 131072 | tf_op jit(solution)/shard_map/reshape | solution.py:36
  69.8 6.2 %collective-permute-start = (f32[4,2,2,128]{3,2,1,0:T(2,128)S(1)}, f32[4,2,2,128]{3,2,1,0:T(2,128)S(1)}, u32[]{:S(2)}, u32[]{:S(2)}) collective-permute-start(f32[4,2,2,128]{3,2,1,0:T(2,128)S(1)} %get-tuple-element.111), channel_id=1, source_target_pairs={{0,4},{4,8},{8,12},{1,5},{5,9},{9,13},{2,6},{6,10},{10,14},{3,7},{... | collective-permute-start | bytes 24584 | tf_op jit(solution)/shard_map/ppermute | solution.py:15
  77.4 4.6 %collective-permute-start.12 = (f32[3,4,1,256]{3,1,2,0:T(4,128)S(1)}, f32[3,4,1,256]{3,1,2,0:T(4,128)S(1)}, u32[]{:S(2)}, u32[]{:S(2)}) collective-permute-start(f32[3,4,1,256]{3,1,2,0:T(4,128)S(1)} %copy.291), channel_id=1, source_target_pairs={{0,4},{4,8},{8,12},{1,5},{5,9},{9,13},{2,6},{6,10},{10,14},{3,7},{... | collective-permute-start | bytes 36872 | tf_op jit(solution)/shard_map/ppermute | solution.py:15
  83.4 4.5 %collective-permute-start.16 = (f32[4,1,256]{2,1,0:T(1,128)S(1)}, f32[4,1,256]{2,1,0:T(1,128)S(1)}, u32[]{:S(2)}, u32[]{:S(2)}) collective-permute-start(f32[4,1,256]{2,1,0:T(1,128)S(1)} %get-tuple-element.109), channel_id=1, source_target_pairs={{0,4},{4,8},{8,12},{1,5},{5,9},{9,13},{2,6},{6,10},{10,14},{3,7},{... | collective-permute-start | bytes 12296 | tf_op jit(solution)/shard_map/ppermute | solution.py:15
  89.3 3.0 %collective-permute-start.14 = (f32[3,1,18,256]{3,2,1,0:T(8,128)S(1)}, f32[3,1,18,256]{3,2,1,0:T(8,128)S(1)}, u32[]{:S(2)}, u32[]{:S(2)}) collective-permute-start(f32[3,1,18,256]{3,2,1,0:T(8,128)S(1)} %get-tuple-element.75), channel_id=1, source_target_pairs={{0,1},{2,3},{4,5},{6,7},{8,9},{10,11},{12,13},{14,15},{16,17},{18,... | collective-permute-start | bytes 165896 | tf_op jit(solution)/shard_map/ppermute | solution.py:15
  93.7 3.0 %collective-permute-start.18 = (f32[1,18,256]{2,1,0:T(8,128)S(1)}, f32[1,18,256]{2,1,0:T(8,128)S(1)}, u32[]{:S(2)}, u32[]{:S(2)}) collective-permute-start(f32[1,18,256]{2,1,0:T(8,128)S(1)} %get-tuple-element.93), channel_id=1, source_target_pairs={{0,1},{2,3},{4,5},{6,7},{8,9},{10,11},{12,13},{14,15},{16,17},{18,... | collective-permute-start | bytes 55304 | tf_op jit(solution)/shard_map/ppermute | solution.py:15
  99.2 4.6 %collective-permute-start.20 = (f32[4,1,256]{2,1,0:T(1,128)S(1)}, f32[4,1,256]{2,1,0:T(1,128)S(1)}, u32[]{:S(2)}, u32[]{:S(2)}) collective-permute-start(f32[4,1,256]{2,1,0:T(1,128)S(1)} %get-tuple-element.107), channel_id=1, source_target_pairs={{0,4},{4,8},{8,12},{1,5},{5,9},{9,13},{2,6},{6,10},{10,14},{3,7},{... | collective-permute-start | bytes 12296 | tf_op jit(solution)/shard_map/ppermute | solution.py:15
  103.7 3.9 %collective-permute-start.4 = (f32[2,1,128]{2,1,0:T(1,128)S(1)}, f32[2,1,128]{2,1,0:T(1,128)S(1)}, u32[]{:S(2)}, u32[]{:S(2)}) collective-permute-start(f32[2,1,128]{2,1,0:T(1,128)S(1)} %get-tuple-element.127), channel_id=1, source_target_pairs={{0,4},{4,8},{8,12},{1,5},{5,9},{9,13},{2,6},{6,10},{10,14},{3,7},{... | collective-permute-start | bytes 3080 | tf_op jit(solution)/shard_map/while/body/eval_jaxpr/ppermute | solution.py:15
  109.0 3.0 %collective-permute-start.22 = (f32[1,18,256]{2,1,0:T(8,128)S(1)}, f32[1,18,256]{2,1,0:T(8,128)S(1)}, u32[]{:S(2)}, u32[]{:S(2)}) collective-permute-start(f32[1,18,256]{2,1,0:T(8,128)S(1)} %get-tuple-element.91), channel_id=1, source_target_pairs={{0,1},{2,3},{4,5},{6,7},{8,9},{10,11},{12,13},{14,15},{16,17},{18,... | collective-permute-start | bytes 55304 | tf_op jit(solution)/shard_map/ppermute | solution.py:15
  114.5 4.5 %collective-permute-start.24 = (f32[4,1,256]{2,1,0:T(1,128)S(1)}, f32[4,1,256]{2,1,0:T(1,128)S(1)}, u32[]{:S(2)}, u32[]{:S(2)}) collective-permute-start(f32[4,1,256]{2,1,0:T(1,128)S(1)} %get-tuple-element.105), channel_id=1, source_target_pairs={{0,4},{4,8},{8,12},{1,5},{5,9},{9,13},{2,6},{6,10},{10,14},{3,7},{... | collective-permute-start | bytes 12296 | tf_op jit(solution)/shard_map/ppermute | solution.py:15
  124.7 3.0 %collective-permute-start.26 = (f32[1,18,256]{2,1,0:T(8,128)S(1)}, f32[1,18,256]{2,1,0:T(8,128)S(1)}, u32[]{:S(2)}, u32[]{:S(2)}) collective-permute-start(f32[1,18,256]{2,1,0:T(8,128)S(1)} %get-tuple-element.89), channel_id=1, source_target_pairs={{0,1},{2,3},{4,5},{6,7},{8,9},{10,11},{12,13},{14,15},{16,17},{18,... | collective-permute-start | bytes 55304 | tf_op jit(solution)/shard_map/ppermute | solution.py:15
  129.1 3.0 %collective-permute-start.2 = (f32[4,2,12,128]{3,2,1,0:T(8,128)S(1)}, f32[4,2,12,128]{3,2,1,0:T(8,128)S(1)}, u32[]{:S(2)}, u32[]{:S(2)}) collective-permute-start(f32[4,2,12,128]{3,2,1,0:T(8,128)S(1)} %pad_maximum_fusion.71), channel_id=1, source_target_pairs={{0,1},{2,3},{4,5},{6,7},{8,9},{10,11},{12,13},{14,15},{16,17},{18,... | collective-permute-start | bytes 147464 | tf_op jit(solution)/shard_map/ppermute | solution.py:15
  133.8 4.5 %collective-permute-start.28 = (f32[4,1,256]{2,1,0:T(1,128)S(1)}, f32[4,1,256]{2,1,0:T(1,128)S(1)}, u32[]{:S(2)}, u32[]{:S(2)}) collective-permute-start(f32[4,1,256]{2,1,0:T(1,128)S(1)} %get-tuple-element.103), channel_id=1, source_target_pairs={{0,4},{4,8},{8,12},{1,5},{5,9},{9,13},{2,6},{6,10},{10,14},{3,7},{... | collective-permute-start | bytes 12296 | tf_op jit(solution)/shard_map/ppermute | solution.py:15
  141.0 3.0 %collective-permute-start.30 = (f32[1,18,256]{2,1,0:T(8,128)S(1)}, f32[1,18,256]{2,1,0:T(8,128)S(1)}, u32[]{:S(2)}, u32[]{:S(2)}) collective-permute-start(f32[1,18,256]{2,1,0:T(8,128)S(1)} %get-tuple-element.87), channel_id=1, source_target_pairs={{0,1},{2,3},{4,5},{6,7},{8,9},{10,11},{12,13},{14,15},{16,17},{18,... | collective-permute-start | bytes 55304 | tf_op jit(solution)/shard_map/ppermute | solution.py:15
  146.4 4.8 %collective-permute-start.32 = (f32[4,1,256]{2,1,0:T(1,128)S(1)}, f32[4,1,256]{2,1,0:T(1,128)S(1)}, u32[]{:S(2)}, u32[]{:S(2)}) collective-permute-start(f32[4,1,256]{2,1,0:T(1,128)S(1)} %get-tuple-element.101), channel_id=1, source_target_pairs={{0,4},{4,8},{8,12},{1,5},{5,9},{9,13},{2,6},{6,10},{10,14},{3,7},{... | collective-permute-start | bytes 12296 | tf_op jit(solution)/shard_map/ppermute | solution.py:15
  153.9 3.0 %collective-permute-start.34 = (f32[1,18,256]{2,1,0:T(8,128)S(1)}, f32[1,18,256]{2,1,0:T(8,128)S(1)}, u32[]{:S(2)}, u32[]{:S(2)}) collective-permute-start(f32[1,18,256]{2,1,0:T(8,128)S(1)} %get-tuple-element.85), channel_id=1, source_target_pairs={{0,1},{2,3},{4,5},{6,7},{8,9},{10,11},{12,13},{14,15},{16,17},{18,... | collective-permute-start | bytes 55304 | tf_op jit(solution)/shard_map/ppermute | solution.py:15
  159.3 4.8 %collective-permute-start.36 = (f32[4,1,256]{2,1,0:T(1,128)S(1)}, f32[4,1,256]{2,1,0:T(1,128)S(1)}, u32[]{:S(2)}, u32[]{:S(2)}) collective-permute-start(f32[4,1,256]{2,1,0:T(1,128)S(1)} %get-tuple-element.99), channel_id=1, source_target_pairs={{0,4},{4,8},{8,12},{1,5},{5,9},{9,13},{2,6},{6,10},{10,14},{3,7},{... | collective-permute-start | bytes 12296 | tf_op jit(solution)/shard_map/ppermute | solution.py:15
  165.6 4.6 %collective-permute-start.8 = (f32[2,1,128]{2,1,0:T(1,128)S(1)}, f32[2,1,128]{2,1,0:T(1,128)S(1)}, u32[]{:S(2)}, u32[]{:S(2)}) collective-permute-start(f32[2,1,128]{2,1,0:T(1,128)S(1)} %get-tuple-element.125), channel_id=1, source_target_pairs={{0,4},{4,8},{8,12},{1,5},{5,9},{9,13},{2,6},{6,10},{10,14},{3,7},{... | collective-permute-start | bytes 3080 | tf_op jit(solution)/shard_map/while/body/eval_jaxpr/ppermute | solution.py:15
  171.5 3.0 %collective-permute-start.38 = (f32[1,18,256]{2,1,0:T(8,128)S(1)}, f32[1,18,256]{2,1,0:T(8,128)S(1)}, u32[]{:S(2)}, u32[]{:S(2)}) collective-permute-start(f32[1,18,256]{2,1,0:T(8,128)S(1)} %get-tuple-element.83), channel_id=1, source_target_pairs={{0,1},{2,3},{4,5},{6,7},{8,9},{10,11},{12,13},{14,15},{16,17},{18,... | collective-permute-start | bytes 55304 | tf_op jit(solution)/shard_map/ppermute | solution.py:15
  177.0 4.5 %collective-permute-start.40 = (f32[4,1,256]{2,1,0:T(1,128)S(1)}, f32[4,1,256]{2,1,0:T(1,128)S(1)}, u32[]{:S(2)}, u32[]{:S(2)}) collective-permute-start(f32[4,1,256]{2,1,0:T(1,128)S(1)} %get-tuple-element.97), channel_id=1, source_target_pairs={{0,4},{4,8},{8,12},{1,5},{5,9},{9,13},{2,6},{6,10},{10,14},{3,7},{... | collective-permute-start | bytes 12296 | tf_op jit(solution)/shard_map/ppermute | solution.py:15
  187.2 3.0 %collective-permute-start.42 = (f32[1,18,256]{2,1,0:T(8,128)S(1)}, f32[1,18,256]{2,1,0:T(8,128)S(1)}, u32[]{:S(2)}, u32[]{:S(2)}) collective-permute-start(f32[1,18,256]{2,1,0:T(8,128)S(1)} %get-tuple-element.81), channel_id=1, source_target_pairs={{0,1},{2,3},{4,5},{6,7},{8,9},{10,11},{12,13},{14,15},{16,17},{18,... | collective-permute-start | bytes 55304 | tf_op jit(solution)/shard_map/ppermute | solution.py:15
  192.7 4.6 %collective-permute-start.44 = (f32[4,1,256]{2,1,0:T(1,128)S(1)}, f32[4,1,256]{2,1,0:T(1,128)S(1)}, u32[]{:S(2)}, u32[]{:S(2)}) collective-permute-start(f32[4,1,256]{2,1,0:T(1,128)S(1)} %get-tuple-element.95), channel_id=1, source_target_pairs={{0,4},{4,8},{8,12},{1,5},{5,9},{9,13},{2,6},{6,10},{10,14},{3,7},{... | collective-permute-start | bytes 12296 | tf_op jit(solution)/shard_map/ppermute | solution.py:15
  204.0 3.8 %collective-permute-start.48 = (f32[4,16,256]{2,1,0:T(8,128)S(1)}, f32[4,16,256]{2,1,0:T(8,128)S(1)}, u32[]{:S(2)}, u32[]{:S(2)}) collective-permute-start(f32[4,16,256]{2,1,0:T(8,128)S(1)} %get-tuple-element.22), channel_id=1, source_target_pairs={{0,2},{1,3},{4,6},{5,7},{8,10},{9,11},{12,14},{13,15},{16,18},{17,... | collective-permute-start | bytes 196616 | tf_op jit(solution)/shard_map/while/body/eval_jaxpr/ppermute | solution.py:26
  209.8 5.6 %reshape.134 = f32[2,2,8,2,128,2]{5,4,3,2,1,0:T(8,128)} reshape(f32[4,16,256]{2,1,0:T(8,128)S(1)} %broadcast_select_fusion) | data formatting | bytes 131072 | tf_op jit(solution)/shard_map/reshape | solution.py:36
  219.2 4.8 %collective-permute-start.49 = (f32[2,1,128]{2,1,0:T(1,128)S(1)}, f32[2,1,128]{2,1,0:T(1,128)S(1)}, u32[]{:S(2)}, u32[]{:S(2)}) collective-permute-start(f32[2,1,128]{2,1,0:T(1,128)S(1)} %get-tuple-element.123), channel_id=1, source_target_pairs={{0,4},{4,8},{8,12},{1,5},{5,9},{9,13},{2,6},{6,10},{10,14},{3,7},{... | collective-permute-start | bytes 3080 | tf_op jit(solution)/shard_map/ppermute | solution.py:15
  232.0 4.8 %collective-permute-start.53 = (f32[2,1,128]{2,1,0:T(1,128)S(1)}, f32[2,1,128]{2,1,0:T(1,128)S(1)}, u32[]{:S(2)}, u32[]{:S(2)}) collective-permute-start(f32[2,1,128]{2,1,0:T(1,128)S(1)} %get-tuple-element.121), channel_id=1, source_target_pairs={{0,4},{4,8},{8,12},{1,5},{5,9},{9,13},{2,6},{6,10},{10,14},{3,7},{... | collective-permute-start | bytes 3080 | tf_op jit(solution)/shard_map/ppermute | solution.py:15
  (213 shorter events, 87.5 us)
Async XLA Ops:
  9.0 100.0 %collective-permute-start.5 = (f32[2,1,128]{2,1,0:T(1,128)S(1)}, f32[2,1,128]{2,1,0:T(1,128)S(1)}, u32[]{:S(2)}, u32[]{:S(2)}) collective-permute-start(f32[2,1,128]{2,1,0:T(1,128)S(1)} %get-tuple-element.128), channel_id=1, source_target_pairs={{4,0},{8,4},{12,8},{5,1},{9,5},{13,9},{6,2},{10,6},{14,10},{7,3},{... | collective-permute-start | bytes 3080 | tf_op jit(solution)/shard_map/while/body/eval_jaxpr/ppermute | solution.py:18
  68.5 56.2 %collective-permute-start.1 = (f32[4,2,2,128]{3,2,1,0:T(2,128)S(1)}, f32[4,2,2,128]{3,2,1,0:T(2,128)S(1)}, u32[]{:S(2)}, u32[]{:S(2)}) collective-permute-start(f32[4,2,2,128]{3,2,1,0:T(2,128)S(1)} %get-tuple-element.112), channel_id=1, source_target_pairs={{4,0},{8,4},{12,8},{5,1},{9,5},{13,9},{6,2},{10,6},{14,10},{7,3},{... | collective-permute-start | bytes 24584 | tf_op jit(solution)/shard_map/ppermute | solution.py:18
  69.8 57.9 %collective-permute-start = (f32[4,2,2,128]{3,2,1,0:T(2,128)S(1)}, f32[4,2,2,128]{3,2,1,0:T(2,128)S(1)}, u32[]{:S(2)}, u32[]{:S(2)}) collective-permute-start(f32[4,2,2,128]{3,2,1,0:T(2,128)S(1)} %get-tuple-element.111), channel_id=1, source_target_pairs={{0,4},{4,8},{8,12},{1,5},{5,9},{9,13},{2,6},{6,10},{10,14},{3,7},{... | collective-permute-start | bytes 24584 | tf_op jit(solution)/shard_map/ppermute | solution.py:15
  76.1 6.0 %collective-permute-start.13 = (f32[3,4,1,256]{3,1,2,0:T(4,128)S(1)}, f32[3,4,1,256]{3,1,2,0:T(4,128)S(1)}, u32[]{:S(2)}, u32[]{:S(2)}) collective-permute-start(f32[3,4,1,256]{3,1,2,0:T(4,128)S(1)} %copy.292), channel_id=1, source_target_pairs={{4,0},{8,4},{12,8},{5,1},{9,5},{13,9},{6,2},{10,6},{14,10},{7,3},{... | collective-permute-start | bytes 36872 | tf_op jit(solution)/shard_map/ppermute | solution.py:18
  77.4 6.0 %collective-permute-start.12 = (f32[3,4,1,256]{3,1,2,0:T(4,128)S(1)}, f32[3,4,1,256]{3,1,2,0:T(4,128)S(1)}, u32[]{:S(2)}, u32[]{:S(2)}) collective-permute-start(f32[3,4,1,256]{3,1,2,0:T(4,128)S(1)} %copy.291), channel_id=1, source_target_pairs={{0,4},{4,8},{8,12},{1,5},{5,9},{9,13},{2,6},{6,10},{10,14},{3,7},{... | collective-permute-start | bytes 36872 | tf_op jit(solution)/shard_map/ppermute | solution.py:15
  82.0 5.9 %collective-permute-start.17 = (f32[4,1,256]{2,1,0:T(1,128)S(1)}, f32[4,1,256]{2,1,0:T(1,128)S(1)}, u32[]{:S(2)}, u32[]{:S(2)}) collective-permute-start(f32[4,1,256]{2,1,0:T(1,128)S(1)} %get-tuple-element.110), channel_id=1, source_target_pairs={{4,0},{8,4},{12,8},{5,1},{9,5},{13,9},{6,2},{10,6},{14,10},{7,3},{... | collective-permute-start | bytes 12296 | tf_op jit(solution)/shard_map/ppermute | solution.py:18
  83.4 5.9 %collective-permute-start.16 = (f32[4,1,256]{2,1,0:T(1,128)S(1)}, f32[4,1,256]{2,1,0:T(1,128)S(1)}, u32[]{:S(2)}, u32[]{:S(2)}) collective-permute-start(f32[4,1,256]{2,1,0:T(1,128)S(1)} %get-tuple-element.109), channel_id=1, source_target_pairs={{0,4},{4,8},{8,12},{1,5},{5,9},{9,13},{2,6},{6,10},{10,14},{3,7},{... | collective-permute-start | bytes 12296 | tf_op jit(solution)/shard_map/ppermute | solution.py:15
  99.2 8.5 %collective-permute-start.20 = (f32[4,1,256]{2,1,0:T(1,128)S(1)}, f32[4,1,256]{2,1,0:T(1,128)S(1)}, u32[]{:S(2)}, u32[]{:S(2)}) collective-permute-start(f32[4,1,256]{2,1,0:T(1,128)S(1)} %get-tuple-element.107), channel_id=1, source_target_pairs={{0,4},{4,8},{8,12},{1,5},{5,9},{9,13},{2,6},{6,10},{10,14},{3,7},{... | collective-permute-start | bytes 12296 | tf_op jit(solution)/shard_map/ppermute | solution.py:15
  103.7 8.3 %collective-permute-start.4 = (f32[2,1,128]{2,1,0:T(1,128)S(1)}, f32[2,1,128]{2,1,0:T(1,128)S(1)}, u32[]{:S(2)}, u32[]{:S(2)}) collective-permute-start(f32[2,1,128]{2,1,0:T(1,128)S(1)} %get-tuple-element.127), channel_id=1, source_target_pairs={{0,4},{4,8},{8,12},{1,5},{5,9},{9,13},{2,6},{6,10},{10,14},{3,7},{... | collective-permute-start | bytes 3080 | tf_op jit(solution)/shard_map/while/body/eval_jaxpr/ppermute | solution.py:15
  113.2 7.2 %collective-permute-start.25 = (f32[4,1,256]{2,1,0:T(1,128)S(1)}, f32[4,1,256]{2,1,0:T(1,128)S(1)}, u32[]{:S(2)}, u32[]{:S(2)}) collective-permute-start(f32[4,1,256]{2,1,0:T(1,128)S(1)} %get-tuple-element.106), channel_id=1, source_target_pairs={{4,0},{8,4},{12,8},{5,1},{9,5},{13,9},{6,2},{10,6},{14,10},{7,3},{... | collective-permute-start | bytes 12296 | tf_op jit(solution)/shard_map/ppermute | solution.py:18
  114.5 8.9 %collective-permute-start.24 = (f32[4,1,256]{2,1,0:T(1,128)S(1)}, f32[4,1,256]{2,1,0:T(1,128)S(1)}, u32[]{:S(2)}, u32[]{:S(2)}) collective-permute-start(f32[4,1,256]{2,1,0:T(1,128)S(1)} %get-tuple-element.105), channel_id=1, source_target_pairs={{0,4},{4,8},{8,12},{1,5},{5,9},{9,13},{2,6},{6,10},{10,14},{3,7},{... | collective-permute-start | bytes 12296 | tf_op jit(solution)/shard_map/ppermute | solution.py:15
  119.0 25.0 %collective-permute-start.7 = (f32[1,10,128]{2,1,0:T(8,128)S(1)}, f32[1,10,128]{2,1,0:T(8,128)S(1)}, u32[]{:S(2)}, u32[]{:S(2)}) collective-permute-start(f32[1,10,128]{2,1,0:T(8,128)S(1)} %get-tuple-element.120), channel_id=1, source_target_pairs={{1,0},{3,2},{5,4},{7,6},{9,8},{11,10},{13,12},{15,14},{17,16},{19,... | collective-permute-start | bytes 15368 | tf_op jit(solution)/shard_map/while/body/eval_jaxpr/ppermute | solution.py:18
  120.4 23.7 %collective-permute-start.6 = (f32[1,10,128]{2,1,0:T(8,128)S(1)}, f32[1,10,128]{2,1,0:T(8,128)S(1)}, u32[]{:S(2)}, u32[]{:S(2)}) collective-permute-start(f32[1,10,128]{2,1,0:T(8,128)S(1)} %get-tuple-element.119), channel_id=1, source_target_pairs={{0,1},{2,3},{4,5},{6,7},{8,9},{10,11},{12,13},{14,15},{16,17},{18,... | collective-permute-start | bytes 15368 | tf_op jit(solution)/shard_map/while/body/eval_jaxpr/ppermute | solution.py:15
  124.7 7.4 %collective-permute-start.26 = (f32[1,18,256]{2,1,0:T(8,128)S(1)}, f32[1,18,256]{2,1,0:T(8,128)S(1)}, u32[]{:S(2)}, u32[]{:S(2)}) collective-permute-start(f32[1,18,256]{2,1,0:T(8,128)S(1)} %get-tuple-element.89), channel_id=1, source_target_pairs={{0,1},{2,3},{4,5},{6,7},{8,9},{10,11},{12,13},{14,15},{16,17},{18,... | collective-permute-start | bytes 55304 | tf_op jit(solution)/shard_map/ppermute | solution.py:15
  127.8 6.0 %collective-permute-start.3 = (f32[4,2,12,128]{3,2,1,0:T(8,128)S(1)}, f32[4,2,12,128]{3,2,1,0:T(8,128)S(1)}, u32[]{:S(2)}, u32[]{:S(2)}) collective-permute-start(f32[4,2,12,128]{3,2,1,0:T(8,128)S(1)} %pad_maximum_fusion.71), channel_id=1, source_target_pairs={{1,0},{3,2},{5,4},{7,6},{9,8},{11,10},{13,12},{15,14},{17,16},{19,... | collective-permute-start | bytes 147464 | tf_op jit(solution)/shard_map/ppermute | solution.py:18
  129.1 9.2 %collective-permute-start.2 = (f32[4,2,12,128]{3,2,1,0:T(8,128)S(1)}, f32[4,2,12,128]{3,2,1,0:T(8,128)S(1)}, u32[]{:S(2)}, u32[]{:S(2)}) collective-permute-start(f32[4,2,12,128]{3,2,1,0:T(8,128)S(1)} %pad_maximum_fusion.71), channel_id=1, source_target_pairs={{0,1},{2,3},{4,5},{6,7},{8,9},{10,11},{12,13},{14,15},{16,17},{18,... | collective-permute-start | bytes 147464 | tf_op jit(solution)/shard_map/ppermute | solution.py:15
  132.5 5.9 %collective-permute-start.29 = (f32[4,1,256]{2,1,0:T(1,128)S(1)}, f32[4,1,256]{2,1,0:T(1,128)S(1)}, u32[]{:S(2)}, u32[]{:S(2)}) collective-permute-start(f32[4,1,256]{2,1,0:T(1,128)S(1)} %get-tuple-element.104), channel_id=1, source_target_pairs={{4,0},{8,4},{12,8},{5,1},{9,5},{13,9},{6,2},{10,6},{14,10},{7,3},{... | collective-permute-start | bytes 12296 | tf_op jit(solution)/shard_map/ppermute | solution.py:18
  145.1 6.2 %collective-permute-start.33 = (f32[4,1,256]{2,1,0:T(1,128)S(1)}, f32[4,1,256]{2,1,0:T(1,128)S(1)}, u32[]{:S(2)}, u32[]{:S(2)}) collective-permute-start(f32[4,1,256]{2,1,0:T(1,128)S(1)} %get-tuple-element.102), channel_id=1, source_target_pairs={{4,0},{8,4},{12,8},{5,1},{9,5},{13,9},{6,2},{10,6},{14,10},{7,3},{... | collective-permute-start | bytes 12296 | tf_op jit(solution)/shard_map/ppermute | solution.py:18
  146.4 6.1 %collective-permute-start.32 = (f32[4,1,256]{2,1,0:T(1,128)S(1)}, f32[4,1,256]{2,1,0:T(1,128)S(1)}, u32[]{:S(2)}, u32[]{:S(2)}) collective-permute-start(f32[4,1,256]{2,1,0:T(1,128)S(1)} %get-tuple-element.101), channel_id=1, source_target_pairs={{0,4},{4,8},{8,12},{1,5},{5,9},{9,13},{2,6},{6,10},{10,14},{3,7},{... | collective-permute-start | bytes 12296 | tf_op jit(solution)/shard_map/ppermute | solution.py:15
  158.0 12.2 %collective-permute-start.37 = (f32[4,1,256]{2,1,0:T(1,128)S(1)}, f32[4,1,256]{2,1,0:T(1,128)S(1)}, u32[]{:S(2)}, u32[]{:S(2)}) collective-permute-start(f32[4,1,256]{2,1,0:T(1,128)S(1)} %get-tuple-element.100), channel_id=1, source_target_pairs={{4,0},{8,4},{12,8},{5,1},{9,5},{13,9},{6,2},{10,6},{14,10},{7,3},{... | collective-permute-start | bytes 12296 | tf_op jit(solution)/shard_map/ppermute | solution.py:18
  159.3 10.9 %collective-permute-start.36 = (f32[4,1,256]{2,1,0:T(1,128)S(1)}, f32[4,1,256]{2,1,0:T(1,128)S(1)}, u32[]{:S(2)}, u32[]{:S(2)}) collective-permute-start(f32[4,1,256]{2,1,0:T(1,128)S(1)} %get-tuple-element.99), channel_id=1, source_target_pairs={{0,4},{4,8},{8,12},{1,5},{5,9},{9,13},{2,6},{6,10},{10,14},{3,7},{... | collective-permute-start | bytes 12296 | tf_op jit(solution)/shard_map/ppermute | solution.py:15
  164.2 10.4 %collective-permute-start.9 = (f32[2,1,128]{2,1,0:T(1,128)S(1)}, f32[2,1,128]{2,1,0:T(1,128)S(1)}, u32[]{:S(2)}, u32[]{:S(2)}) collective-permute-start(f32[2,1,128]{2,1,0:T(1,128)S(1)} %get-tuple-element.126), channel_id=1, source_target_pairs={{4,0},{8,4},{12,8},{5,1},{9,5},{13,9},{6,2},{10,6},{14,10},{7,3},{... | collective-permute-start | bytes 3080 | tf_op jit(solution)/shard_map/while/body/eval_jaxpr/ppermute | solution.py:18
  165.6 8.9 %collective-permute-start.8 = (f32[2,1,128]{2,1,0:T(1,128)S(1)}, f32[2,1,128]{2,1,0:T(1,128)S(1)}, u32[]{:S(2)}, u32[]{:S(2)}) collective-permute-start(f32[2,1,128]{2,1,0:T(1,128)S(1)} %get-tuple-element.125), channel_id=1, source_target_pairs={{0,4},{4,8},{8,12},{1,5},{5,9},{9,13},{2,6},{6,10},{10,14},{3,7},{... | collective-permute-start | bytes 3080 | tf_op jit(solution)/shard_map/while/body/eval_jaxpr/ppermute | solution.py:15
  175.7 10.2 %collective-permute-start.41 = (f32[4,1,256]{2,1,0:T(1,128)S(1)}, f32[4,1,256]{2,1,0:T(1,128)S(1)}, u32[]{:S(2)}, u32[]{:S(2)}) collective-permute-start(f32[4,1,256]{2,1,0:T(1,128)S(1)} %get-tuple-element.98), channel_id=1, source_target_pairs={{4,0},{8,4},{12,8},{5,1},{9,5},{13,9},{6,2},{10,6},{14,10},{7,3},{... | collective-permute-start | bytes 12296 | tf_op jit(solution)/shard_map/ppermute | solution.py:18
  177.0 8.9 %collective-permute-start.40 = (f32[4,1,256]{2,1,0:T(1,128)S(1)}, f32[4,1,256]{2,1,0:T(1,128)S(1)}, u32[]{:S(2)}, u32[]{:S(2)}) collective-permute-start(f32[4,1,256]{2,1,0:T(1,128)S(1)} %get-tuple-element.97), channel_id=1, source_target_pairs={{0,4},{4,8},{8,12},{1,5},{5,9},{9,13},{2,6},{6,10},{10,14},{3,7},{... | collective-permute-start | bytes 12296 | tf_op jit(solution)/shard_map/ppermute | solution.py:15
  181.6 8.7 %collective-permute-start.11 = (f32[1,10,128]{2,1,0:T(8,128)S(1)}, f32[1,10,128]{2,1,0:T(8,128)S(1)}, u32[]{:S(2)}, u32[]{:S(2)}) collective-permute-start(f32[1,10,128]{2,1,0:T(8,128)S(1)} %get-tuple-element.118), channel_id=1, source_target_pairs={{1,0},{3,2},{5,4},{7,6},{9,8},{11,10},{13,12},{15,14},{17,16},{19,... | collective-permute-start | bytes 15368 | tf_op jit(solution)/shard_map/while/body/eval_jaxpr/ppermute | solution.py:18
  182.9 7.4 %collective-permute-start.10 = (f32[1,10,128]{2,1,0:T(8,128)S(1)}, f32[1,10,128]{2,1,0:T(8,128)S(1)}, u32[]{:S(2)}, u32[]{:S(2)}) collective-permute-start(f32[1,10,128]{2,1,0:T(8,128)S(1)} %get-tuple-element.117), channel_id=1, source_target_pairs={{0,1},{2,3},{4,5},{6,7},{8,9},{10,11},{12,13},{14,15},{16,17},{18,... | collective-permute-start | bytes 15368 | tf_op jit(solution)/shard_map/while/body/eval_jaxpr/ppermute | solution.py:15
  191.4 5.9 %collective-permute-start.45 = (f32[4,1,256]{2,1,0:T(1,128)S(1)}, f32[4,1,256]{2,1,0:T(1,128)S(1)}, u32[]{:S(2)}, u32[]{:S(2)}) collective-permute-start(f32[4,1,256]{2,1,0:T(1,128)S(1)} %get-tuple-element.96), channel_id=1, source_target_pairs={{4,0},{8,4},{12,8},{5,1},{9,5},{13,9},{6,2},{10,6},{14,10},{7,3},{... | collective-permute-start | bytes 12296 | tf_op jit(solution)/shard_map/ppermute | solution.py:18
  217.9 6.1 %collective-permute-start.50 = (f32[2,1,128]{2,1,0:T(1,128)S(1)}, f32[2,1,128]{2,1,0:T(1,128)S(1)}, u32[]{:S(2)}, u32[]{:S(2)}) collective-permute-start(f32[2,1,128]{2,1,0:T(1,128)S(1)} %get-tuple-element.124), channel_id=1, source_target_pairs={{4,0},{8,4},{12,8},{5,1},{9,5},{13,9},{6,2},{10,6},{14,10},{7,3},{... | collective-permute-start | bytes 3080 | tf_op jit(solution)/shard_map/ppermute | solution.py:18
  219.2 6.1 %collective-permute-start.49 = (f32[2,1,128]{2,1,0:T(1,128)S(1)}, f32[2,1,128]{2,1,0:T(1,128)S(1)}, u32[]{:S(2)}, u32[]{:S(2)}) collective-permute-start(f32[2,1,128]{2,1,0:T(1,128)S(1)} %get-tuple-element.123), channel_id=1, source_target_pairs={{0,4},{4,8},{8,12},{1,5},{5,9},{9,13},{2,6},{6,10},{10,14},{3,7},{... | collective-permute-start | bytes 3080 | tf_op jit(solution)/shard_map/ppermute | solution.py:15
  230.7 6.1 %collective-permute-start.54 = (f32[2,1,128]{2,1,0:T(1,128)S(1)}, f32[2,1,128]{2,1,0:T(1,128)S(1)}, u32[]{:S(2)}, u32[]{:S(2)}) collective-permute-start(f32[2,1,128]{2,1,0:T(1,128)S(1)} %get-tuple-element.122), channel_id=1, source_target_pairs={{4,0},{8,4},{12,8},{5,1},{9,5},{13,9},{6,2},{10,6},{14,10},{7,3},{... | collective-permute-start | bytes 3080 | tf_op jit(solution)/shard_map/ppermute | solution.py:18
  232.0 6.1 %collective-permute-start.53 = (f32[2,1,128]{2,1,0:T(1,128)S(1)}, f32[2,1,128]{2,1,0:T(1,128)S(1)}, u32[]{:S(2)}, u32[]{:S(2)}) collective-permute-start(f32[2,1,128]{2,1,0:T(1,128)S(1)} %get-tuple-element.121), channel_id=1, source_target_pairs={{0,4},{4,8},{8,12},{1,5},{5,9},{9,13},{2,6},{6,10},{10,14},{3,7},{... | collective-permute-start | bytes 3080 | tf_op jit(solution)/shard_map/ppermute | solution.py:15
  (32 other events, 172.1 us)
where the time goes:
time: 248 us; the launch traced here: 245 us
  starting transfers between devices  148 us (60%)
  other arithmetic  47.3 us (19%)
  local copies, waits for them, and re-layouts  32.9 us (13%)
  waiting for transfers between devices  14.7 us (6%)
    ppermute x28, starting transfers between devices, with_halo(): lax.ppermute(lax.slice_in_dim(block, block.shape[dim] - width, None, axis...  108 us
    ppermute x28, starting transfers between devices, with_halo(): lax.ppermute(lax.slice_in_dim(block, 0, width, axis=dim), axis, backward)  36.4 us
    reshape x5, local copies, waits for them, and re-layouts, restrict_cells(): field.reshape(depth // 2, 2, width // 2, 2, length // 2, 2)  28.6 us
    reduce_sum x5, other arithmetic, restrict_cells(): field.reshape(depth // 2, 2, width // 2, 2, length // 2, 2)  12.8 us
    ppermute x28, waiting for transfers between devices, with_halo(): lax.ppermute(lax.slice_in_dim(block, block.shape[dim] - width, None, axis...  12.7 us
    select_n x1, other arithmetic, lookup_cells(): cell_soft = jnp.where(inside, zone_soft[zone_index], cell_soft)  10.2 us
    select_n x1, other arithmetic, lookup_cells(): cell_plane = jnp.where(inside, zone_plane[zone_index], cell_plane)  10.1 us
    select_n x1, other arithmetic, lookup_cells(): cell_thick = jnp.where(inside, zone_thick[zone_index], cell_thick)  10 us
  transfers between devices with their start and end apart: 57, of which 15 were waited for; matrix products, arithmetic and copies ran while one was open for 25% of the time, Pallas kernels for 0%

commit v1 on v0

v1 whole, which is shorter than its diff:
```python
import functools

import jax
import jax.numpy as jnp
from jax import lax
from jax.experimental import pallas as pl
from jax.experimental.pallas import tpu as pltpu
from jax.sharding import PartitionSpec as P

FINE_STEPS = 8
COARSE_STEPS = 2
LANES = 128
EDGE = 2 * COARSE_STEPS
HALO = FINE_STEPS + EDGE
VMEM_BYTES = 16 * 2**20
VMEM = pl.BlockSpec(memory_space=pltpu.VMEM)


def iota(shape, dim):
    return lax.broadcasted_iota(jnp.int32, shape, dim)


def pick(table, index):
    return jnp.take_along_axis(table, index, axis=1, mode="promise_in_bounds")


def split_lanes(row):
    rows = row.shape[0]
    lane = iota((rows, LANES), 1)
    low = lane < LANES // 2
    even = (2 * lane) % LANES
    first, second = row[:, :LANES], row[:, LANES:]
    return jnp.concatenate(
        [
            jnp.where(low, pick(first, even), pick(second, even)),
            jnp.where(low, pick(first, even + 1), pick(second, even + 1)),
        ],
        axis=1,
    )


def join_lanes(row):
    rows = row.shape[0]
    lane = iota((rows, LANES), 1)
    is_even = lane % 2 == 0
    half = lane // 2
    even, odd = row[:, :LANES], row[:, LANES:]
    return jnp.concatenate(
        [
            jnp.where(is_even, pick(even, half), pick(odd, half)),
            jnp.where(is_even, pick(even, half + LANES // 2), pick(odd, half + LANES // 2)),
        ],
        axis=1,
    )


def prepare_kernel(u_ref, u_other, zone_ref, zone_other, flux_ref, local_ref, send_ref):
    width = u_ref.shape[1]
    core = lax.axis_index("layer")

    def fill(order, mirror):
        for i in range(width):
            row = width - 1 - i if mirror else i
            for at, pair in ((0, (u_ref, u_other)), (width, (zone_ref, zone_other))):
                low, high = (pair[k] for k in order)
                slab = jnp.concatenate([low[:, row, :], high[:, row, :]], axis=0)
                slab = split_lanes(slab.astype(jnp.float32))
                local_ref[at + i] = slab
                if i < HALO:
                    send_ref[(HALO if at else 0) + i] = slab
        flux = split_lanes(flux_ref[...])
        for i in range(width):
            row = width - 1 - i if mirror else i
            local_ref[2 * width + i // 8, i % 8 : i % 8 + 1, :] = flux[row : row + 1]
            send_ref[2 * HALO + i // 8, i % 8 : i % 8 + 1, :] = flux[row : row + 1]

    pl.when(core == 0)(lambda: fill((0, 1), False))
    pl.when(core == 1)(lambda: fill((1, 0), True))


def pair_sum(value):
    layers = value.shape[0]
    even = iota(value.shape, 0) % 2 == 0
    return value + jnp.where(even, pltpu.roll(value, layers - 1, 0), pltpu.roll(value, 1, 0))


def halves(value):
    return value[:, :LANES] + value[:, LANES:]


def step_row(v, low, high, k_plane, k_thick, source, y_flow, layer_gap):
    layers = v.shape[0]
    inside = iota(v.shape, 0) < layers - layer_gap
    shift = layers - layer_gap
    up_v, up_k = pltpu.roll(v, shift, 0), pltpu.roll(k_thick, shift, 0)
    flow = jnp.where(inside, (k_thick + up_k) * (up_v - v), 0.0)
    return v + source + (high - low) + y_flow(v, k_plane) + (flow - pltpu.roll(flow, layer_gap, 0))


def fine_y(v, k):
    va, vb, ka, kb = v[:, :LANES], v[:, LANES:], k[:, :LANES], k[:, LANES:]
    inner = (ka + kb) * (vb - va)
    next_v, next_k = pltpu.roll(va, LANES - 1, 1), pltpu.roll(ka, LANES - 1, 1)
    outer = jnp.where(iota(va.shape, 1) < LANES - 1, (kb + next_k) * (next_v - vb), 0.0)
    return jnp.concatenate([inner - pltpu.roll(outer, 1, 1), outer - inner], axis=1)


def coarse_y(v, k):
    next_v, next_k = pltpu.roll(v, LANES - 1, 1), pltpu.roll(k, LANES - 1, 1)
    flow = jnp.where(iota(v.shape, 1) < LANES - 1, (k + next_k) * (next_v - v), 0.0)
    return flow - pltpu.roll(flow, 1, 1)


def outer_mask(core):
    tile, tiles = lax.axis_index("tile"), lax.axis_size("tile")
    at_edge = jnp.where(core == 0, tile == 0, tile == tiles - 1)
    return jnp.where(at_edge, 0.0, 1.0).astype(jnp.float32)


def propagate_kernel(
    local_ref, recv_ref, table_ref, rest_ref, share_ref, coarse_ref, v_ref, coef_ref, source_ref
):
    rows = v_ref.shape[0]
    width = rows - HALO
    layers = local_ref.shape[1]
    mask = outer_mask(lax.axis_index("layer"))
    tables = [jnp.broadcast_to(table_ref[k : k + 1, :], (layers, LANES)) for k in range(5)]
    top = iota((layers, 2 * LANES), 0) == 0
    top_pair = iota((layers, LANES), 0) < 2

    def flux_row(j):
        ref, at, i = (
            (recv_ref, 2 * HALO, HALO - 1 - j) if j < HALO else (local_ref, 2 * width, j - HALO)
        )
        return ref[at + i // 8, i % 8 : i % 8 + 1, :]

    fields = []
    for j in range(rows):
        if j < HALO:
            v, zone = recv_ref[HALO - 1 - j], recv_ref[2 * HALO - 1 - j]
        else:
            v, zone = local_ref[j - HALO], local_ref[width + j - HALO]
        zone = zone.astype(jnp.int32)
        coefs = [
            jnp.concatenate([pick(t, zone[:, :LANES]), pick(t, zone[:, LANES:])], axis=1)
            for t in tables
        ]
        v_ref[j] = v
        for k in range(4):
            coef_ref[k, j] = coefs[k]
        flux = flux_row(j)
        source_ref[j] = jnp.where(top, flux, 0.0)
        if j >= HALO - EDGE:
            here = [halves(x) for x in (coefs[0], coefs[2], coefs[4], v)] + [halves(flux)]
            if j % 2 == 0:
                fields = here
            else:
                at = (j - (HALO - EDGE)) // 2
                for k in range(4):
                    coarse_ref[k, at] = 0.125 * pair_sum(fields[k] + here[k])
                coarse_ref[4, at] = jnp.where(top_pair, 0.5 * (fields[4] + here[4]), 0.0)

    for step in range(1, FINE_STEPS + 1):
        v_next = v_ref[step - 1]
        k_next = coef_ref[0, step - 1] + coef_ref[1, step - 1] * v_next
        high = None
        for j in range(step - 1, rows - step):
            v, k_plane, low = v_next, k_next, high
            v_next = v_ref[j + 1]
            k_next = coef_ref[0, j + 1] + coef_ref[1, j + 1] * v_next
            high = (k_plane + k_next) * (v_next - v)
            if j == HALO - 1:
                high = high * mask
            if j >= step:
                k_thick = coef_ref[2, j] + coef_ref[3, j] * v
                v_ref[j] = step_row(v, low, high, k_plane, k_thick, source_ref[j], fine_y, 1)

    even = iota((layers, LANES), 0) % 2 == 0
    start = HALO - EDGE
    restricted = []
    for j in range(start, HALO + width // 2, 2):
        restricted.append(0.125 * pair_sum(halves(v_ref[j]) + halves(v_ref[j + 1])))
    for i in range(0, len(restricted), 2):
        rest_ref[i // 2] = jnp.where(even, restricted[i], restricted[i + 1])
    for i in range(width // 2):
        share_ref[2 * i] = v_ref[HALO + i][:, :LANES]
        share_ref[2 * i + 1] = v_ref[HALO + i][:, LANES:]
    for k in range(5):
        for i in range(COARSE_STEPS):
            share_ref[width + k * COARSE_STEPS + i] = coarse_ref[k, i]


def coarse_fields(mine_ref, coarse_ref, other_ref, width):
    def row(k, j):
        known = width // 2 + COARSE_STEPS
        if j < known:
            return coarse_ref[k, j]
        return other_ref[width + k * COARSE_STEPS + width // 2 + 2 * COARSE_STEPS - 1 - j]

    return row


def coarse_propagate(state, field, masks):
    count = len(state)
    flux = {j: field(4, j) for j in range(1, count - 1)}
    plane = [field(0, j) for j in range(count)]
    thick = [field(1, j) for j in range(count)]
    soft = [field(2, j) for j in range(count)]
    for step in range(1, COARSE_STEPS + 1):
        k_plane = {
            j: plane[j] * (1.0 + soft[j] * state[j]) for j in range(step - 1, count - step + 1)
        }
        flows = {}
        for j in range(step - 1, count - step):
            flow = (k_plane[j] + k_plane[j + 1]) * (state[j + 1] - state[j])
            flows[j] = flow * masks[j] if j in masks else flow
        fresh = list(state)
        for j in range(step, count - step):
            k_thick = thick[j] * (1.0 + soft[j] * state[j])
            fresh[j] = step_row(
                state[j], flows[j - 1], flows[j], k_plane[j], k_thick, flux[j], coarse_y, 2
            )
        state = fresh
    return state[COARSE_STEPS : count - COARSE_STEPS]


def edge_factors(rows):
    core = lax.axis_index("layer")
    return {
        COARSE_STEPS - 1: outer_mask(core),
        rows - COARSE_STEPS - 1: outer_mask(1 - core),
    }


def expand(slab):
    layers = slab.shape[0]
    even = iota(slab.shape, 0) % 2 == 0
    return [
        jnp.where(even, slab, pltpu.roll(slab, 1, 0)),
        jnp.where(even, pltpu.roll(slab, layers - 1, 0), slab),
    ]


def read_state(state_ref, rows):
    if state_ref.shape[0] == rows:
        return [state_ref[j] for j in range(rows)]
    half = state_ref.shape[0] // 2
    mine = sum((expand(state_ref[i]) for i in range(half)), [])
    other = sum((expand(state_ref[half + i]) for i in range(half)), [])
    return mine + other[::-1]


def output_kernel(state_ref, coarse_ref, share_ref, other_ref, out_ref):
    depth, width = out_ref.shape[1:3]
    core = lax.axis_index("layer")
    rows = width // 2 + 2 * COARSE_STEPS
    field = coarse_fields(share_ref, coarse_ref, other_ref, width)
    masks = edge_factors(rows)
    own = [field(3, j) for j in range(rows)]
    first = lax.axis_index("tm") == 0
    state = [jnp.where(first, a, b) for a, b in zip(own, read_state(state_ref, rows))]
    moved = coarse_propagate(state, field, masks)
    base = coarse_propagate(own, field, masks)

    def write(mirror):
        for j in range(0, width, 2):
            gain = moved[j // 2] - base[j // 2]
            slabs = []
            for i in (j, j + 1):
                ref, at = (share_ref, i) if i < width // 2 else (other_ref, width - 1 - i)
                slab = jnp.concatenate([ref[2 * at] + gain, ref[2 * at + 1] + gain], axis=1)
                slabs.append(slab[depth:] if mirror else slab[:depth])
            both = join_lanes(jnp.concatenate(slabs, axis=0))
            for i in (0, 1):
                row = width - 1 - (j + i) if mirror else j + i
                out_ref[0, :, row, :] = both[depth * i : depth * (i + 1)]

    pl.when(core == 0)(lambda: write(False))
    pl.when(core == 1)(lambda: write(True))


def advance_kernel(state_ref, coarse_ref, share_ref, other_ref, next_ref):
    width = 2 * next_ref.shape[0]
    rows = width // 2 + 2 * COARSE_STEPS
    field = coarse_fields(share_ref, coarse_ref, other_ref, width)
    masks = edge_factors(rows)
    own = [field(3, j) for j in range(rows)]
    first = lax.axis_index("tm") == 0
    state = [jnp.where(first, a, b) for a, b in zip(own, read_state(state_ref, rows))]
    moved = coarse_propagate(state, field, masks)
    base = coarse_propagate(own, field, masks)
    for j in range(width // 2):
        pair = []
        for i in (2 * j, 2 * j + 1):
            ref, at = (share_ref, i) if i < width // 2 else (other_ref, width - 1 - i)
            pair.append(ref[2 * at] + ref[2 * at + 1])
        next_ref[j] = moved[j] - base[j] + 0.125 * pair_sum(pair[0] + pair[1])


def layer_swap(value):
    return lax.ppermute(value, "layer", [(0, 1), (1, 0)])


def swap_pairs(pairs):
    return [edge for a, b in pairs for edge in ((a, b), (b, a))]


def tile_swap(value):
    tiles, slices = lax.axis_size("tile"), lax.axis_size("tm")
    at = lambda tile, time, core: (tile * slices + time) * 2 + core
    pairs = [
        (at(t, m, 0), at(t - 1, m, 1)) for t in range(1, tiles) for m in range(slices)
    ]
    for m in range(0, slices - 1, 2):
        pairs.append((at(0, m, 0), at(0, m + 1, 0)))
        pairs.append((at(tiles - 1, m, 1), at(tiles - 1, m + 1, 1)))
    return lax.ppermute(value, ("tile", "tm", "layer"), swap_pairs(pairs))


def time_swap(value, parity):
    slices = lax.axis_size("tm")
    at = lambda time, core: time * 2 + core
    pairs = [
        (at(m, c), at(m + 1, c)) for m in range(parity, slices - 1, 2) for c in range(2)
    ]
    used = {d for pair in pairs for d in pair}
    pairs += [(at(m, 0), at(m, 1)) for m in range(slices) if at(m, 0) not in used]
    return lax.ppermute(value, ("tm", "layer"), swap_pairs(pairs))


def zone_tables(zone_row, plane_rate, thick_rate, soften):
    table_rows = plane_rate.shape[0]
    hit = (zone_row[:, None] == jnp.arange(table_rows, dtype=jnp.int32)[None, :]).astype(
        jnp.float32
    )
    plane, thick, soft = (
        jnp.sum(hit * rate[None, :], axis=1) for rate in (plane_rate, thick_rate, soften)
    )
    tables = jnp.stack(
        [0.5 * plane, 0.5 * plane * soft, 0.5 * thick, 0.5 * thick * soft, soft]
    )
    return jnp.pad(tables, ((0, 8 - tables.shape[0]), (0, LANES - tables.shape[1])))


def on_device(u_start, flux, zone_of_cell, zone_row, plane_rate, thick_rate, soften):
    depth, width, length = zone_of_cell.shape
    layers = depth * lax.axis_size("layer")
    f32 = jnp.float32
    slabs = lambda *lead: jax.ShapeDtypeStruct((*lead, layers, LANES), f32)
    wide = lambda *lead: jax.ShapeDtypeStruct((*lead, layers, length), f32)
    call = functools.partial(
        pl.pallas_call, compiler_params=pltpu.CompilerParams(vmem_limit_bytes=VMEM_BYTES)
    )
    specs = lambda count: [VMEM] * count

    own = u_start[0]
    tables = zone_tables(zone_row, plane_rate, thick_rate, soften)
    own_other = layer_swap(own)
    zone_other = layer_swap(zone_of_cell)
    flux_slabs = width // 8
    local, send = call(
        prepare_kernel,
        out_shape=(wide(2 * width + flux_slabs), wide(2 * HALO + flux_slabs)),
        in_specs=specs(5),
        out_specs=(VMEM, VMEM),
        name="prepare",
    )(own, own_other, zone_of_cell, zone_other, flux[0])
    recv = tile_swap(send)

    rows = HALO + width
    edge_rows = width // 2 + EDGE
    rest, share, coarse = call(
        propagate_kernel,
        out_shape=(
            slabs(edge_rows // 4),
            slabs(width + 5 * COARSE_STEPS),
            slabs(5, (width + EDGE) // 2),
        ),
        in_specs=specs(3),
        out_specs=(VMEM, VMEM, VMEM),
        scratch_shapes=[
            pltpu.VMEM((rows, layers, length), f32),
            pltpu.VMEM((4, rows, layers, length), f32),
            pltpu.VMEM((rows, layers, length), f32),
        ],
        name="propagate",
    )(local, recv, tables)

    state = jnp.concatenate([rest, layer_swap(rest)], axis=0)
    other = layer_swap(share)
    slices = lax.axis_size("tm")
    position = lax.axis_index("tm")
    for turn in range(slices - 1):
        if turn == 0:
            state = time_swap(state, 0)
            continue
        ended = call(
            advance_kernel,
            out_shape=slabs(width // 2),
            in_specs=specs(4),
            out_specs=VMEM,
            name="advance",
        )(state, coarse, share, other)
        outer = tile_swap(ended[:COARSE_STEPS])
        inner = layer_swap(outer)
        full = jnp.concatenate([outer[::-1], ended, inner], axis=0)
        arrived = time_swap(full, turn % 2)
        if state.shape != full.shape:
            state = call(
                lambda s, o: [o.__setitem__(j, r) for j, r in enumerate(read_state(s, o.shape[0]))]
                and None,
                out_shape=slabs(full.shape[0]),
                in_specs=specs(1),
                out_specs=VMEM,
                name="unfold",
            )(state)
        state = jnp.where(position == turn + 1, arrived, state)
    return call(
        output_kernel,
        out_shape=jax.ShapeDtypeStruct((1, depth, width, length), f32),
        in_specs=specs(4),
        out_specs=VMEM,
        name="output",
    )(state, coarse, share, other)


def solution(mesh):
    return jax.shard_map(
        on_device,
        mesh=mesh,
        in_specs=(
            P(("parts", "tm"), "layer", "tile", None),
            P(("parts", "tm"), "tile", None),
            P("layer", "tile", None),
            P(),
            P(),
            P(),
            P(),
        ),
        out_specs=P(("parts", "tm"), "layer", "tile", None),
        check_vma=False,
    )
```

time: 248 us -> 19.5 us (0.08); the launches traced: 245 us -> 19.3 us
  starting transfers between devices: 148 us -> 5.9 us
  other arithmetic: 47.3 us -> 0.75 us
  local copies, waits for them, and re-layouts: 32.9 us -> 2.51 us
  waiting for transfers between devices: 14.7 us -> 6.82 us
  Pallas kernels: 0 us -> 3.24 us
    ppermute x57 -> x6, starting transfers between devices: 148 us -> 5.9 us  [the longest x1 2.71 us: tile_swap(): return lax.ppermute(value, ('tile', 'tm', 'layer'), swap_pairs(pairs))]
    select_n x4 -> x0, other arithmetic: 30.3 us -> none  [the longest x1 10.2 us: lookup_cells(): cell_soft = jnp.where(inside, zone_soft[zone_index], cell_soft)]
    reshape x9 -> x0, local copies, waits for them, and re-layouts: 29.2 us -> none  [the longest x5 28.6 us: restrict_cells(): field.reshape(depth // 2, 2, width // 2, 2, length // 2, 2)]
    reduce_sum x7 -> x1, other arithmetic: 13.1 us -> 0.74 us  [zone_tables(): jnp.sum(hit * rate[None, :], axis=1)]
    ppermute x57 -> x6, waiting for transfers between devices: 14.7 us -> 6.82 us  [the longest x1 3.79 us: tile_swap(): return lax.ppermute(value, ('tile', 'tm', 'layer'), swap_pairs(pairs))]
    pallas_call x0 -> x3, Pallas kernels: none -> 3.24 us  [the longest x1 1.75 us: on_device(): call(propagate_kernel, out_shape=(slabs(edge_rows // 4), slabs(width + 5...]
  transfers between devices with their start and end apart: 57 -> 6, of which waited for: 15 -> 5; matrix products, arithmetic and copies ran while one was open for 25% -> 4% of each run, Pallas kernels for 0% -> 0%
where the time goes in v1:
time: 19.5 us; the launch traced here: 19.3 us
  waiting for transfers between devices  6.82 us (35%)
  starting transfers between devices  5.9 us (30%)
  Pallas kernels  3.24 us (17%)
  local copies, waits for them, and re-layouts  2.51 us (13%)
  other arithmetic  0.75 us (4%)
    ppermute x1, waiting for transfers between devices, tile_swap(): return lax.ppermute(value, ('tile', 'tm', 'layer'), swap_pairs(pairs))  3.79 us
    ppermute x1, starting transfers between devices, tile_swap(): return lax.ppermute(value, ('tile', 'tm', 'layer'), swap_pairs(pairs))  2.71 us
    unnamed x12, local copies, waits for them, and re-layouts  2.48 us
    ppermute x1, starting transfers between devices, time_swap(): return lax.ppermute(value, ('tm', 'layer'), swap_pairs(pairs))  2.02 us
    ppermute x1, waiting for transfers between devices, time_swap(): return lax.ppermute(value, ('tm', 'layer'), swap_pairs(pairs))  1.81 us
    pallas_call x1, Pallas kernels, on_device(): call(propagate_kernel, out_shape=(slabs(edge_rows // 4), slabs(width + 5...  1.75 us
    ppermute x4, waiting for transfers between devices, layer_swap(): return lax.ppermute(value, 'layer', [(0, 1), (1, 0)])  1.22 us
    ppermute x4, starting transfers between devices, layer_swap(): return lax.ppermute(value, 'layer', [(0, 1), (1, 0)])  1.18 us
  transfers between devices with their start and end apart: 6, of which 5 were waited for; matrix products, arithmetic and copies ran while one was open for 4% of the time, Pallas kernels for 0%

profile of v1, /device:TPU:0, one launch (start us, length us, event | category | flops | bytes accessed | tf_op | source)
XLA Modules:
  0.0 19.3 jit_solution(18006939826249866453)
XLA Ops:
  0.0 0.0 copy-start.5
  0.0 0.0 copy-start.3
  0.0 0.0 copy-start.4
  0.0 0.5 %collective-permute-start = (f32[4,16,256]{2,1,0:T(8,128)}, f32[4,16,256]{2,1,0:T(8,128)S(1)}, u32[]{:S(2)}, u32[]{:S(2)}) collective-permute-start(f32[4,16,256]{2,1,0:T(8,128)} %bitcast.13), channel_id=1, source_target_pairs={{0,1},{1,0},{2,3},{3,2},{4,5},{5,4},{6,7},{7,6},{8,9},{9,8},{10,11... | collective-permute-start | bytes 196616 | tf_op jit(solution)/shard_map/ppermute | solution.py:301
  0.5 0.1 collective-permute-start.1
  0.6 0.0 copy-done.5
  0.7 0.0 copy-done.3
  0.7 0.0 copy-done.4
  0.7 0.7 %select_reduce_fusion = (f32[16]{0:T(128)S(1)}, f32[16]{0:T(128)S(1)}, f32[16]{0:T(128)S(1)}) fusion(f32[8]{0:T(128)S(1)} %copy-done.3, s32[16]{0:T(128)S(1)} %copy-done.4, f32[8]{0:T(128)S(1)} %copy-done.5, f32[8]{0:T(128)} %param.11), kind=kLoop, calls=%fused_computation.1 | loop fusion | flops 848 | bytes 352 | tf_op jit(solution)/shard_map/reduce_sum | solution.py:337
  1.4 0.2 %collective-permute-done.u_other = f32[4,16,256]{2,1,0:T(8,128)S(1)} collective-permute-done((f32[4,16,256]{2,1,0:T(8,128)}, f32[4,16,256]{2,1,0:T(8,128)S(1)}, u32[]{:S(2)}, u32[]{:S(2)}) %collective-permute-start) | collective-permute-done | bytes 65568 | tf_op jit(solution)/shard_map/ppermute | solution.py:301
  1.6 0.4 %collective-permute-done.1.zone_other = s32[4,16,256]{2,1,0:T(8,128)S(1)} collective-permute-done((s32[4,16,256]{2,1,0:T(8,128)}, s32[4,16,256]{2,1,0:T(8,128)S(1)}, u32[]{:S(2)}, u32[]{:S(2)}) %collective-permute-start.1) | collective-permute-done | bytes 65568 | tf_op jit(solution)/shard_map/ppermute | solution.py:301
  2.0 0.0 copy-start
  2.0 0.8 %copy-done = f32[1,4,16,256]{3,2,1,0:T(8,128)S(1)} copy-done((f32[1,4,16,256]{3,2,1,0:T(8,128)S(1)}, f32[1,4,16,256]{3,2,1,0:T(8,128)}, u32[]{:S(2)}) %copy-start) | copy-done | bytes 65560
  2.8 0.0 copy-start.1
  2.8 0.8 %copy-done.1 = s32[4,16,256]{2,1,0:T(8,128)S(1)} copy-done((s32[4,16,256]{2,1,0:T(8,128)S(1)}, s32[4,16,256]{2,1,0:T(8,128)}, u32[]{:S(2)}) %copy-start.1) | copy-done | bytes 65560
  3.7 0.0 copy-start.2
  3.7 0.7 %copy-done.2 = f32[1,16,256]{2,1,0:T(8,128)S(1)} copy-done((f32[1,16,256]{2,1,0:T(8,128)S(1)}, f32[1,16,256]{2,1,0:T(8,128)}, u32[]{:S(2)}) %copy-start.2) | copy-done | bytes 16408
  4.4 0.4 %prepare.1 = (f32[34,8,256]{2,1,0:T(8,128)S(1)}, f32[26,8,256]{2,1,0:T(8,128)S(1)}) custom-call(f32[4,16,256]{2,1,0:T(8,128)S(1)} %bitcast.14, f32[4,16,256]{2,1,0:T(8,128)S(1)} %collective-permute-done.u_other, s32[4,16,256]{2,1,0:T(8,128)S(1)} %copy-done.1, s32[4,16,256]{2,1,0:T(8,128)S(1)} %collective-permute-done.1.zone_other, f32[16,256]{1,0:T(8,128)S(1)} %bitcast.15), custom_call_target="tpu_custom_call" | custom-call | tf_op jit(solution)/shard_map/prepare/pallas_call | solution.py:361
  4.8 2.7 %collective-permute-start.2 = (f32[26,8,256]{2,1,0:T(8,128)S(1)}, f32[26,8,256]{2,1,0:T(8,128)S(1)}, u32[]{:S(2)}, u32[]{:S(2)}) collective-permute-start(f32[26,8,256]{2,1,0:T(8,128)S(1)} %get-tuple-element.11), channel_id=1, source_target_pairs={{4,1},{1,4},{6,3},{3,6},{8,5},{5,8},{10,7},{7,10},{12,9},{9,12},{1... | collective-permute-start | bytes 638984 | tf_op jit(solution)/shard_map/ppermute | solution.py:317
  7.5 3.8 %collective-permute-done.2.recv_ref = f32[26,8,256]{2,1,0:T(8,128)S(1)} collective-permute-done((f32[26,8,256]{2,1,0:T(8,128)S(1)}, f32[26,8,256]{2,1,0:T(8,128)S(1)}, u32[]{:S(2)}, u32[]{:S(2)}) %collective-permute-start.2) | collective-permute-done | bytes 213024 | tf_op jit(solution)/shard_map/ppermute | solution.py:317
  11.3 1.8 %propagate.1 = (f32[3,8,128]{2,1,0:T(8,128)S(1)}, f32[26,8,128]{2,1,0:T(8,128)S(1)}, f32[5,10,8,128]{3,2,1,0:T(8,128)S(1)}) custom-call(f32[34,8,256]{2,1,0:T(8,128)S(1)} %get-tuple-element.10.local_ref, f32[26,8,256]{2,1,0:T(8,128)S(1)} %collective-permute-done.2.recv_ref, f32[8,128]{1,0:T(8,128)S(1)} %pad.4.table_ref), custom_call_target="tpu_custom_call" | custom-call | tf_op jit(solution)/shard_map/propagate/pallas_call | solution.py:372
  13.1 0.2 collective-permute-start.3
  13.2 0.4 %collective-permute-start.5 = (f32[26,8,128]{2,1,0:T(8,128)S(1)}, f32[26,8,128]{2,1,0:T(8,128)S(1)}, u32[]{:S(2)}, u32[]{:S(2)}) collective-permute-start(f32[26,8,128]{2,1,0:T(8,128)S(1)} %get-tuple-element.14.share_ref), channel_id=1, source_target_pairs={{0,1},{1,0},{2,3},{3,2},{4,5},{5,4},{6,7},{7,6},{8,9},{9,8},{10,11... | collective-permute-start | bytes 319496 | tf_op jit(solution)/shard_map/ppermute | solution.py:301
  13.6 0.7 %collective-permute-done.3 = f32[3,8,128]{2,1,0:T(8,128)S(1)} collective-permute-done((f32[3,8,128]{2,1,0:T(8,128)S(1)}, f32[3,8,128]{2,1,0:T(8,128)S(1)}, u32[]{:S(2)}, u32[]{:S(2)}) %collective-permute-start.3) | collective-permute-done | bytes 12320 | tf_op jit(solution)/shard_map/ppermute | solution.py:301
  14.3 2.0 %collective-permute-start.4 = (f32[6,8,128]{2,1,0:T(8,128)S(1)}, f32[6,8,128]{2,1,0:T(8,128)S(1)}, u32[]{:S(2)}, u32[]{:S(2)}) collective-permute-start(f32[6,8,128]{2,1,0:T(8,128)S(1)} %pad_maximum_fusion), channel_id=1, source_target_pairs={{0,2},{2,0},{1,3},{3,1},{4,6},{6,4},{5,7},{7,5},{8,10},{10,8},{9,1... | collective-permute-start | bytes 73736 | tf_op jit(solution)/shard_map/ppermute | solution.py:328
  16.3 1.8 %collective-permute-done.4.state_ref = f32[6,8,128]{2,1,0:T(8,128)S(1)} collective-permute-done((f32[6,8,128]{2,1,0:T(8,128)S(1)}, f32[6,8,128]{2,1,0:T(8,128)S(1)}, u32[]{:S(2)}, u32[]{:S(2)}) %collective-permute-start.4) | collective-permute-done | bytes 24608 | tf_op jit(solution)/shard_map/ppermute | solution.py:328
  18.1 0.0 collective-permute-done.5.other_ref
  18.1 1.1 %output.1 = f32[1,4,16,256]{3,2,1,0:T(8,128)} custom-call(f32[6,8,128]{2,1,0:T(8,128)S(1)} %collective-permute-done.4.state_ref, f32[5,10,8,128]{3,2,1,0:T(8,128)S(1)} %get-tuple-element.13.coarse_ref, f32[26,8,128]{2,1,0:T(8,128)S(1)} %get-tuple-element.14.share_ref, f32[26,8,128]{2,1,0:T(8,128)S(1)} %collective-permute-done.5.other_ref), custom_call_target="tpu_custom_call" | custom-call | tf_op jit(solution)/shard_map/output/pallas_call | solution.py:418
  (5 shorter events, 0.0 us)
Async XLA Ops:
  0.0 0.7 %copy-start.5 = (f32[8]{0:T(128)S(1)}, f32[8]{0:T(128)}, u32[]{:S(2)}) copy-start(f32[8]{0:T(128)} %param.13) | copy-start | bytes 100
  0.0 0.7 %copy-start.3 = (f32[8]{0:T(128)S(1)}, f32[8]{0:T(128)}, u32[]{:S(2)}) copy-start(f32[8]{0:T(128)} %param.12) | copy-start | bytes 100
  0.0 0.7 %copy-start.4 = (s32[16]{0:T(128)S(1)}, s32[16]{0:T(128)}, u32[]{:S(2)}) copy-start(s32[16]{0:T(128)} %param.10) | copy-start | bytes 196
  0.0 1.6 %collective-permute-start = (f32[4,16,256]{2,1,0:T(8,128)}, f32[4,16,256]{2,1,0:T(8,128)S(1)}, u32[]{:S(2)}, u32[]{:S(2)}) collective-permute-start(f32[4,16,256]{2,1,0:T(8,128)} %bitcast.13), channel_id=1, source_target_pairs={{0,1},{1,0},{2,3},{3,2},{4,5},{5,4},{6,7},{7,6},{8,9},{9,8},{10,11... | collective-permute-start | bytes 196616 | tf_op jit(solution)/shard_map/ppermute | solution.py:301
  0.5 1.5 %collective-permute-start.1 = (s32[4,16,256]{2,1,0:T(8,128)}, s32[4,16,256]{2,1,0:T(8,128)S(1)}, u32[]{:S(2)}, u32[]{:S(2)}) collective-permute-start(s32[4,16,256]{2,1,0:T(8,128)} %zone_ref.1), channel_id=1, source_target_pairs={{0,1},{1,0},{2,3},{3,2},{4,5},{5,4},{6,7},{7,6},{8,9},{9,8},{10,11... | collective-permute-start | bytes 196616 | tf_op jit(solution)/shard_map/ppermute | solution.py:301
  2.0 0.8 %copy-start = (f32[1,4,16,256]{3,2,1,0:T(8,128)S(1)}, f32[1,4,16,256]{3,2,1,0:T(8,128)}, u32[]{:S(2)}) copy-start(f32[1,4,16,256]{3,2,1,0:T(8,128)} %param.7) | copy-start | bytes 196612
  2.8 0.8 %copy-start.1 = (s32[4,16,256]{2,1,0:T(8,128)S(1)}, s32[4,16,256]{2,1,0:T(8,128)}, u32[]{:S(2)}) copy-start(s32[4,16,256]{2,1,0:T(8,128)} %zone_ref.1) | copy-start | bytes 196612
  3.7 0.7 %copy-start.2 = (f32[1,16,256]{2,1,0:T(8,128)S(1)}, f32[1,16,256]{2,1,0:T(8,128)}, u32[]{:S(2)}) copy-start(f32[1,16,256]{2,1,0:T(8,128)} %param.8) | copy-start | bytes 49156
  4.8 6.5 %collective-permute-start.2 = (f32[26,8,256]{2,1,0:T(8,128)S(1)}, f32[26,8,256]{2,1,0:T(8,128)S(1)}, u32[]{:S(2)}, u32[]{:S(2)}) collective-permute-start(f32[26,8,256]{2,1,0:T(8,128)S(1)} %get-tuple-element.11), channel_id=1, source_target_pairs={{4,1},{1,4},{6,3},{3,6},{8,5},{5,8},{10,7},{7,10},{12,9},{9,12},{1... | collective-permute-start | bytes 638984 | tf_op jit(solution)/shard_map/ppermute | solution.py:317
  13.1 1.2 %collective-permute-start.3 = (f32[3,8,128]{2,1,0:T(8,128)S(1)}, f32[3,8,128]{2,1,0:T(8,128)S(1)}, u32[]{:S(2)}, u32[]{:S(2)}) collective-permute-start(f32[3,8,128]{2,1,0:T(8,128)S(1)} %get-tuple-element.12), channel_id=1, source_target_pairs={{0,1},{1,0},{2,3},{3,2},{4,5},{5,4},{6,7},{7,6},{8,9},{9,8},{10,11... | collective-permute-start | bytes 36872 | tf_op jit(solution)/shard_map/ppermute | solution.py:301
  13.2 4.9 %collective-permute-start.5 = (f32[26,8,128]{2,1,0:T(8,128)S(1)}, f32[26,8,128]{2,1,0:T(8,128)S(1)}, u32[]{:S(2)}, u32[]{:S(2)}) collective-permute-start(f32[26,8,128]{2,1,0:T(8,128)S(1)} %get-tuple-element.14.share_ref), channel_id=1, source_target_pairs={{0,1},{1,0},{2,3},{3,2},{4,5},{5,4},{6,7},{7,6},{8,9},{9,8},{10,11... | collective-permute-start | bytes 319496 | tf_op jit(solution)/shard_map/ppermute | solution.py:301
  14.3 3.8 %collective-permute-start.4 = (f32[6,8,128]{2,1,0:T(8,128)S(1)}, f32[6,8,128]{2,1,0:T(8,128)S(1)}, u32[]{:S(2)}, u32[]{:S(2)}) collective-permute-start(f32[6,8,128]{2,1,0:T(8,128)S(1)} %pad_maximum_fusion), channel_id=1, source_target_pairs={{0,2},{2,0},{1,3},{3,1},{4,6},{6,4},{5,7},{7,5},{8,10},{10,8},{9,1... | collective-permute-start | bytes 73736 | tf_op jit(solution)/shard_map/ppermute | solution.py:328

commit v2 on v1

v2 whole, which is shorter than its diff:
```python
import jax
import jax.numpy as jnp
from jax import lax
from jax.experimental import pallas as pl
from jax.experimental.pallas import tpu as pltpu
from jax.sharding import PartitionSpec as P

FINE_STEPS = 8
COARSE_STEPS = 2
LANES = 128
EDGE = 2 * COARSE_STEPS
HALO = FINE_STEPS + EDGE
VMEM_BYTES = 16 * 2**20
VMEM = pl.BlockSpec(memory_space=pltpu.VMEM)


def iota(shape, dim):
    return lax.broadcasted_iota(jnp.int32, shape, dim)


def pick(table, index):
    return jnp.take_along_axis(table, index, axis=1, mode="promise_in_bounds")


def split_lanes(row):
    rows = row.shape[0]
    lane = iota((rows, LANES), 1)
    low = lane < LANES // 2
    even = (2 * lane) % LANES
    first, second = row[:, :LANES], row[:, LANES:]
    return jnp.concatenate(
        [
            jnp.where(low, pick(first, even), pick(second, even)),
            jnp.where(low, pick(first, even + 1), pick(second, even + 1)),
        ],
        axis=1,
    )


def join_lanes(row):
    rows = row.shape[0]
    lane = iota((rows, LANES), 1)
    is_even = lane % 2 == 0
    half = lane // 2
    even, odd = row[:, :LANES], row[:, LANES:]
    return jnp.concatenate(
        [
            jnp.where(is_even, pick(even, half), pick(odd, half)),
            jnp.where(is_even, pick(even, half + LANES // 2), pick(odd, half + LANES // 2)),
        ],
        axis=1,
    )


def pack_rows(core, u_ref, zone_ref, head_ref, tail_ref, flux_ref=None):
    depth, width = u_ref.shape[:2]

    def fill(mirror):
        for i in range(width):
            row = width - 1 - i if mirror else i
            slab = jnp.concatenate(
                [u_ref[:, row, :], zone_ref[:, row, :].astype(jnp.float32)], axis=0
            )
            slab = split_lanes(slab)
            if i < HALO:
                head_ref[i] = slab
            else:
                tail_ref[i - HALO] = slab
        if flux_ref is not None:
            flux = split_lanes(flux_ref[...])
            for i in range(width):
                row = width - 1 - i if mirror else i
                head_ref[HALO + i // 8, i % 8 : i % 8 + 1, :] = flux[row : row + 1]

    pl.when(core == 0)(lambda: fill(False))
    pl.when(core == 1)(lambda: fill(True))


def pack_own_kernel(
    u_hbm,
    zone_hbm,
    flux_hbm,
    row_hbm,
    plane_hbm,
    thick_hbm,
    soft_hbm,
    head_ref,
    tail_ref,
    table_ref,
    u_ref,
    zone_ref,
    flux_ref,
    row_ref,
    plane_ref,
    thick_ref,
    soft_ref,
    sems,
):
    sources = (u_hbm, zone_hbm, flux_hbm, row_hbm, plane_hbm, thick_hbm, soft_hbm)
    targets = (u_ref, zone_ref, flux_ref, row_ref, plane_ref, thick_ref, soft_ref)
    copies = [
        pltpu.make_async_copy(source, target, sems.at[k])
        for k, (source, target) in enumerate(zip(sources, targets))
    ]
    for copy in copies:
        copy.start()
    for copy in copies[3:]:
        copy.wait()
    lane = iota(table_ref.shape, 1)
    plane = thick = soft = jnp.zeros(table_ref.shape, jnp.float32)
    for zone in range(row_ref.shape[0]):
        at, here = row_ref[zone], lane == zone
        plane = jnp.where(here, 0.5 * plane_ref[at], plane)
        thick = jnp.where(here, 0.5 * thick_ref[at], thick)
        soft = jnp.where(here, soft_ref[at], soft)
    table_ref[0:1] = plane[:1]
    table_ref[1:2] = (plane * soft)[:1]
    table_ref[2:3] = thick[:1]
    table_ref[3:4] = (thick * soft)[:1]
    table_ref[4:8] = soft[:4]
    for copy in copies[:3]:
        copy.wait()
    pack_rows(lax.axis_index("layer"), u_ref, zone_ref, head_ref, tail_ref, flux_ref)


def pack_other_kernel(u_ref, zone_ref, head_ref, tail_ref):
    pack_rows(lax.axis_index("layer"), u_ref, zone_ref, head_ref, tail_ref)


def join_layers(low, high):
    depth = low.shape[0] // 2
    return (
        jnp.concatenate([low[:depth], high[:depth]], axis=0),
        jnp.concatenate([low[depth:], high[depth:]], axis=0),
    )


def pair_sum(value):
    layers = value.shape[0]
    even = iota(value.shape, 0) % 2 == 0
    return value + jnp.where(even, pltpu.roll(value, layers - 1, 0), pltpu.roll(value, 1, 0))


def halves(value):
    return value[:, :LANES] + value[:, LANES:]


def step_row(v, low, high, k_plane, k_thick, source, y_flow, layer_gap):
    layers = v.shape[0]
    inside = iota(v.shape, 0) < layers - layer_gap
    shift = layers - layer_gap
    up_v, up_k = pltpu.roll(v, shift, 0), pltpu.roll(k_thick, shift, 0)
    flow = jnp.where(inside, (k_thick + up_k) * (up_v - v), 0.0)
    return v + source + (high - low) + y_flow(v, k_plane) + (flow - pltpu.roll(flow, layer_gap, 0))


def fine_y(v, k):
    va, vb, ka, kb = v[:, :LANES], v[:, LANES:], k[:, :LANES], k[:, LANES:]
    inner = (ka + kb) * (vb - va)
    next_v, next_k = pltpu.roll(va, LANES - 1, 1), pltpu.roll(ka, LANES - 1, 1)
    outer = jnp.where(iota(va.shape, 1) < LANES - 1, (kb + next_k) * (next_v - vb), 0.0)
    return jnp.concatenate([inner - pltpu.roll(outer, 1, 1), outer - inner], axis=1)


def coarse_y(v, k):
    next_v, next_k = pltpu.roll(v, LANES - 1, 1), pltpu.roll(k, LANES - 1, 1)
    flow = jnp.where(iota(v.shape, 1) < LANES - 1, (k + next_k) * (next_v - v), 0.0)
    return flow - pltpu.roll(flow, 1, 1)


def outer_mask(core):
    tile, tiles = lax.axis_index("tile"), lax.axis_size("tile")
    at_edge = jnp.where(core == 0, tile == 0, tile == tiles - 1)
    return jnp.where(at_edge, 0.0, 1.0).astype(jnp.float32)


def look_up(table_ref, zone):
    zone = zone.astype(jnp.int32)
    halves_of = (zone[:, :LANES], zone[:, LANES:])
    tables = [jnp.broadcast_to(table_ref[k : k + 1, :], halves_of[0].shape) for k in range(5)]
    return [jnp.concatenate([pick(t, z) for z in halves_of], axis=1) for t in tables]


def flux_row(head_ref, i):
    return head_ref[HALO + i // 8, i % 8 : i % 8 + 1, :]


def to_source(flux, layers):
    return jnp.where(iota((layers, flux.shape[1]), 0) == 0, flux, 0.0)


def to_coarse(coarse_ref, at, rows):
    sums = []
    for coefs, v, flux in rows:
        sums.append([halves(x) for x in (coefs[0], coefs[2], coefs[4], v, flux)])
    first, second = sums
    for k in range(4):
        coarse_ref[k, at] = 0.125 * pair_sum(first[k] + second[k])
    pair = iota(coarse_ref.shape[2:], 0) < 2
    coarse_ref[4, at] = jnp.where(pair, 0.5 * (first[4] + second[4]), 0.0)


def fine_sweep(step, rows, load_v, store_v, load_coef, source, mask):
    v_next = load_v(rows[0] - 1)
    k_next = load_coef(0, rows[0] - 1) + load_coef(1, rows[0] - 1) * v_next
    high = None
    for j in (rows[0] - 1, *rows):
        v, k_plane, low = v_next, k_next, high
        v_next = load_v(j + 1)
        k_next = load_coef(0, j + 1) + load_coef(1, j + 1) * v_next
        high = (k_plane + k_next) * (v_next - v)
        if j == HALO - 1:
            high = high * mask
        if j >= rows[0]:
            k_thick = load_coef(2, j) + load_coef(3, j) * v
            store_v(j, step_row(v, low, high, k_plane, k_thick, source(j), fine_y, 1))


def interior_kernel(
    own_ref, own_tail, other_ref, other_tail, table_ref, edge_ref, coef_out, coarse_ref, v_ref, coef_ref
):
    width, layers = v_ref.shape[:2]
    core = lax.axis_index("layer")

    def gather(order):
        rows = []
        for i in range(width):
            slabs = [
                ref[i] if i < HALO else tail[i - HALO]
                for ref, tail in ((own_ref, own_tail), (other_ref, other_tail))
            ]
            v, zone = join_layers(*(slabs[k] for k in order))
            coefs = look_up(table_ref, zone)
            v_ref[i] = v
            for k in range(4):
                coef_ref[k, i] = coefs[k]
                if i < coef_out.shape[1]:
                    coef_out[k, i] = coefs[k]
            rows.append((coefs, v, flux_row(own_ref, i)))
            if i % 2:
                to_coarse(coarse_ref, i // 2, rows)
                rows = []

    pl.when(core == 0)(lambda: gather((0, 1)))
    pl.when(core == 1)(lambda: gather((1, 0)))
    for level in range(FINE_STEPS):
        if level:
            fine_sweep(
                level,
                range(HALO + level, HALO + width - level),
                lambda j: v_ref[j - HALO],
                lambda j, value: v_ref.__setitem__(j - HALO, value),
                lambda k, j: coef_ref[k, j - HALO],
                lambda j: to_source(flux_row(own_ref, j - HALO), layers),
                None,
            )
        for i in range(2):
            edge_ref[level, i] = v_ref[level + i]


def edge_kernel(
    recv_ref,
    recv_other,
    own_ref,
    table_ref,
    edge_ref,
    own_coef,
    rest_ref,
    share_ref,
    coarse_ref,
    v_ref,
    coef_ref,
):
    layers = v_ref.shape[1]
    half = v_ref.shape[0] - HALO
    core = lax.axis_index("layer")
    mask = outer_mask(core)

    def gather(order):
        rows = []
        for j in range(HALO):
            i = HALO - 1 - j
            slabs = (recv_ref[i], recv_other[i])
            v, zone = join_layers(*(slabs[k] for k in order))
            coefs = look_up(table_ref, zone)
            v_ref[j] = v
            for k in range(4):
                coef_ref[k, j] = coefs[k]
            rows.append((coefs, v, flux_row(recv_ref, i)))
            if j % 2:
                if j >= HALO - EDGE:
                    to_coarse(coarse_ref, (j - (HALO - EDGE)) // 2, rows)
                rows = []

    pl.when(core == 0)(lambda: gather((1, 0)))
    pl.when(core == 1)(lambda: gather((0, 1)))

    def source(j):
        flux = flux_row(own_ref, j - HALO) if j >= HALO else flux_row(recv_ref, HALO - 1 - j)
        return to_source(flux, layers)

    for step in range(1, FINE_STEPS + 1):
        reach = HALO + step - 1
        fine_sweep(
            step,
            range(step, HALO + step),
            lambda j: edge_ref[step - 1, j - reach] if j >= reach else v_ref[j],
            lambda j, value: v_ref.__setitem__(j, value),
            lambda k, j: own_coef[k, j - HALO] if j >= HALO else coef_ref[k, j],
            source,
            mask,
        )

    even = iota((layers, LANES), 0) % 2 == 0
    restricted = []
    for j in range(HALO - EDGE, HALO + half, 2):
        restricted.append(0.125 * pair_sum(halves(v_ref[j]) + halves(v_ref[j + 1])))
    for i in range(0, len(restricted), 2):
        rest_ref[i // 2] = jnp.where(even, restricted[i], restricted[i + 1])
    for i in range(half):
        share_ref[2 * i] = v_ref[HALO + i][:, :LANES]
        share_ref[2 * i + 1] = v_ref[HALO + i][:, LANES:]
    for k in range(5):
        for i in range(COARSE_STEPS):
            share_ref[2 * half + k * COARSE_STEPS + i] = coarse_ref[k, i]


def coarse_fields(coarse_ref, outer_ref, other_ref):
    own = coarse_ref.shape[1]

    def row(k, j):
        if j < COARSE_STEPS:
            return outer_ref[k, j]
        if j < COARSE_STEPS + own:
            return coarse_ref[k, j - COARSE_STEPS]
        return other_ref[2 * own + k * COARSE_STEPS + own + 2 * COARSE_STEPS - 1 - j]

    return row


def coarse_propagate(state, field, masks):
    count = len(state)
    flux = {j: field(4, j) for j in range(1, count - 1)}
    plane = [field(0, j) for j in range(count)]
    thick = [field(1, j) for j in range(count)]
    soft = [field(2, j) for j in range(count)]
    for step in range(1, COARSE_STEPS + 1):
        k_plane = {
            j: plane[j] * (1.0 + soft[j] * state[j]) for j in range(step - 1, count - step + 1)
        }
        flows = {}
        for j in range(step - 1, count - step):
            flow = (k_plane[j] + k_plane[j + 1]) * (state[j + 1] - state[j])
            flows[j] = flow * masks[j] if j in masks else flow
        fresh = list(state)
        for j in range(step, count - step):
            k_thick = thick[j] * (1.0 + soft[j] * state[j])
            fresh[j] = step_row(
                state[j], flows[j - 1], flows[j], k_plane[j], k_thick, flux[j], coarse_y, 2
            )
        state = fresh
    return state[COARSE_STEPS : count - COARSE_STEPS]


def edge_factors(rows):
    core = lax.axis_index("layer")
    return {
        COARSE_STEPS - 1: outer_mask(core),
        rows - COARSE_STEPS - 1: outer_mask(1 - core),
    }


def expand(slab):
    layers = slab.shape[0]
    even = iota(slab.shape, 0) % 2 == 0
    return [
        jnp.where(even, slab, pltpu.roll(slab, 1, 0)),
        jnp.where(even, pltpu.roll(slab, layers - 1, 0), slab),
    ]


def read_state(refs):
    if len(refs) == 1:
        return [refs[0][j] for j in range(refs[0].shape[0])]
    mine, other = (sum((expand(ref[i]) for i in range(ref.shape[0])), []) for ref in refs)
    return mine + other[::-1]


def unfold_kernel(mine_ref, other_ref, state_ref):
    for j, row in enumerate(read_state((mine_ref, other_ref))):
        state_ref[j] = row


def propagated(refs, state_refs=None):
    field = coarse_fields(*refs)
    rows = refs[0].shape[1] + 2 * COARSE_STEPS
    state = [field(3, j) for j in range(rows)]
    if state_refs:
        first = lax.axis_index("tm") == 0
        state = [jnp.where(first, a, b) for a, b in zip(state, read_state(state_refs))]
    return coarse_propagate(state, field, edge_factors(rows))


def base_kernel(coarse_ref, outer_ref, share_ref, other_ref, base_ref):
    depth, width = base_ref.shape[:2]
    core = lax.axis_index("layer")
    base = propagated((coarse_ref, outer_ref, other_ref))

    def write(mirror):
        for j in range(0, width, 2):
            slabs = []
            for i in (j, j + 1):
                ref, at = (share_ref, i) if i < width // 2 else (other_ref, width - 1 - i)
                slab = jnp.concatenate(
                    [ref[2 * at] - base[j // 2], ref[2 * at + 1] - base[j // 2]], axis=1
                )
                slabs.append(slab[depth:] if mirror else slab[:depth])
            both = join_lanes(jnp.concatenate(slabs, axis=0))
            for i in (0, 1):
                row = width - 1 - (j + i) if mirror else j + i
                base_ref[:, row, :] = both[depth * i : depth * (i + 1)]

    pl.when(core == 0)(lambda: write(False))
    pl.when(core == 1)(lambda: write(True))


def output_kernel(*refs):
    *state_refs, coarse_ref, outer_ref, other_ref, base_ref, out_ref = refs
    depth, width = base_ref.shape[:2]
    core = lax.axis_index("layer")
    moved = propagated((coarse_ref, outer_ref, other_ref), state_refs)
    half = iota(moved[0].shape, 1) // 2

    def write(mirror):
        for j, row in enumerate(moved):
            gain = jnp.concatenate([pick(row, half), pick(row, half + LANES // 2)], axis=1)
            gain = gain[depth:] if mirror else gain[:depth]
            for i in (2 * j, 2 * j + 1):
                at = width - 1 - i if mirror else i
                out_ref[0, :, at, :] = base_ref[:, at, :] + gain

    pl.when(core == 0)(lambda: write(False))
    pl.when(core == 1)(lambda: write(True))


def advance_kernel(state_ref, coarse_ref, outer_ref, share_ref, other_ref, next_ref):
    own = next_ref.shape[0]
    refs = (coarse_ref, outer_ref, other_ref)
    moved, base = propagated(refs, (state_ref,)), propagated(refs)
    for j in range(own):
        pair = []
        for i in (2 * j, 2 * j + 1):
            ref, at = (share_ref, i) if i < own else (other_ref, 2 * own - 1 - i)
            pair.append(ref[2 * at] + ref[2 * at + 1])
        next_ref[j] = moved[j] - base[j] + 0.125 * pair_sum(pair[0] + pair[1])


def layer_swap(value):
    return lax.ppermute(value, "layer", [(0, 1), (1, 0)])


def swap_pairs(pairs):
    return [edge for a, b in pairs for edge in ((a, b), (b, a))]


def tile_swap(value):
    tiles, slices = lax.axis_size("tile"), lax.axis_size("tm")
    at = lambda tile, time, core: (tile * slices + time) * 2 + core
    pairs = [
        (at(t, m, 0), at(t - 1, m, 1)) for t in range(1, tiles) for m in range(slices)
    ]
    for m in range(0, slices - 1, 2):
        pairs.append((at(0, m, 0), at(0, m + 1, 0)))
        pairs.append((at(tiles - 1, m, 1), at(tiles - 1, m + 1, 1)))
    return lax.ppermute(value, ("tile", "tm", "layer"), swap_pairs(pairs))


def time_swap(value, parity):
    slices = lax.axis_size("tm")
    at = lambda time, core: time * 2 + core
    pairs = [
        (at(m, c), at(m + 1, c)) for m in range(parity, slices - 1, 2) for c in range(2)
    ]
    used = {d for pair in pairs for d in pair}
    pairs += [(at(m, 0), at(m, 1)) for m in range(slices) if at(m, 0) not in used]
    return lax.ppermute(value, ("tm", "layer"), swap_pairs(pairs))


def cross_swap(value):
    slices = lax.axis_size("tm")
    pairs = [(m * 2 + c, m * 2 + 3 - c) for m in range(0, slices - 1, 2) for c in range(2)]
    return lax.ppermute(value, ("tm", "layer"), swap_pairs(pairs))


def on_device(u_start, flux, zone_of_cell, zone_row, plane_rate, thick_rate, soften):
    depth, width, length = zone_of_cell.shape
    layers = depth * lax.axis_size("layer")
    half = width // 2
    f32 = jnp.float32
    slabs = lambda *lead: jax.ShapeDtypeStruct((*lead, layers, LANES), f32)
    wide = lambda *lead: jax.ShapeDtypeStruct((*lead, layers, length), f32)

    def call(kernel, out_shape, *operands, name, scratch=(), memory=pltpu.VMEM):
        return pl.pallas_call(
            kernel,
            out_shape=out_shape,
            in_specs=[pl.BlockSpec(memory_space=memory)] * len(operands),
            out_specs=jax.tree.map(lambda _: VMEM, out_shape),
            scratch_shapes=scratch,
            compiler_params=pltpu.CompilerParams(vmem_limit_bytes=VMEM_BYTES),
            name=name,
        )(*operands)

    u_own = u_start[0]
    u_other, zone_other = layer_swap(u_own), layer_swap(zone_of_cell)
    own, own_tail, tables = call(
        pack_own_kernel,
        (wide(HALO + width // 8), wide(width - HALO), jax.ShapeDtypeStruct((8, LANES), f32)),
        *(u_own, zone_of_cell, flux[0], zone_row, plane_rate, thick_rate, soften),
        name="pack_own",
        scratch=[
            pltpu.VMEM(u_own.shape, f32),
            pltpu.VMEM(zone_of_cell.shape, jnp.int32),
            pltpu.VMEM(flux.shape[1:], f32),
            pltpu.SMEM(zone_row.shape, jnp.int32),
            *[pltpu.SMEM(plane_rate.shape, f32)] * 3,
            pltpu.SemaphoreType.DMA((7,)),
        ],
        memory=pltpu.HBM,
    )
    recv = tile_swap(own)
    other, other_tail = call(
        pack_other_kernel,
        (wide(HALO), wide(width - HALO)),
        *(u_other, zone_other),
        name="pack_other",
    )
    recv_other = tile_swap(other)

    levels, own_coef, coarse = call(
        interior_kernel,
        (wide(FINE_STEPS, 2), wide(4, FINE_STEPS + 1), slabs(5, half)),
        *(own, own_tail, other, other_tail, tables),
        name="interior",
        scratch=[
            pltpu.VMEM((width, layers, length), f32),
            pltpu.VMEM((4, width, layers, length), f32),
        ],
    )
    rest, share, outer = call(
        edge_kernel,
        (
            slabs((half + EDGE) // 4),
            slabs(2 * half + 5 * COARSE_STEPS),
            slabs(5, COARSE_STEPS),
        ),
        *(recv, recv_other, own, tables, levels, own_coef),
        name="edge",
        scratch=[
            pltpu.VMEM((HALO + half, layers, length), f32),
            pltpu.VMEM((4, HALO, layers, length), f32),
        ],
    )

    slices = lax.axis_size("tm")
    position = lax.axis_index("tm")
    state = [rest, rest]
    if slices > 1:
        state = [time_swap(rest, 0), cross_swap(rest)]
    other_share = layer_swap(share)
    base = call(
        base_kernel,
        jax.ShapeDtypeStruct((depth, width, length), f32),
        *(coarse, outer, share, other_share),
        name="base",
    )
    if slices > 2:
        full = slabs(half + 2 * COARSE_STEPS)
        state = [call(unfold_kernel, full, *state, name="unfold")]
    for turn in range(1, slices - 1):
        ended = call(
            advance_kernel,
            slabs(half),
            *(*state, coarse, outer, share, other_share),
            name="advance",
        )
        low = tile_swap(ended[:COARSE_STEPS])
        high = layer_swap(low)
        arrived = time_swap(jnp.concatenate([low[::-1], ended, high], axis=0), turn % 2)
        state = [jnp.where(position == turn + 1, arrived, state[0])]
    return call(
        output_kernel,
        jax.ShapeDtypeStruct((1, depth, width, length), f32),
        *(*state, coarse, outer, other_share, base),
        name="output",
    )


def solution(mesh):
    return jax.shard_map(
        on_device,
        mesh=mesh,
        in_specs=(
            P(("parts", "tm"), "layer", "tile", None),
            P(("parts", "tm"), "tile", None),
            P("layer", "tile", None),
            P(),
            P(),
            P(),
            P(),
        ),
        out_specs=P(("parts", "tm"), "layer", "tile", None),
        check_vma=False,
    )
```

time: 19.5 us -> 19.3 us (0.990)
  Pallas kernels: 3.24 us -> 5.81 us
  waiting for transfers between devices: 6.82 us -> 5.03 us
  other arithmetic: 0.75 us -> 0 us
  starting transfers between devices: 5.9 us -> 5.64 us
    pallas_call x3 -> x6, Pallas kernels: 3.24 us -> 5.81 us  [call(): pl.pallas_call(kernel, out_shape=out_shape, in_specs=[pl.BlockSpec(memory...]
    ppermute x4 -> x3, waiting for transfers between devices: 1.22 us -> 0.01 us  [layer_swap(): return lax.ppermute(value, 'layer', [(0, 1), (1, 0)])]
    ppermute x1, starting transfers between devices: 2.02 us -> 1.1 us  [time_swap(): return lax.ppermute(value, ('tm', 'layer'), swap_pairs(pairs))]
    ppermute x0 -> x1, starting transfers between devices: none -> 0.76 us  [cross_swap(): return lax.ppermute(value, ('tm', 'layer'), swap_pairs(pairs))]
    reduce_sum x1 -> x0, other arithmetic: 0.74 us -> none  [zone_tables(): jnp.sum(hit * rate[None, :], axis=1)]
    ppermute x1 -> x2, waiting for transfers between devices: 3.79 us -> 3.12 us  [tile_swap(): return lax.ppermute(value, ('tile', 'tm', 'layer'), swap_pairs(pairs))]
    ppermute x4 -> x3, starting transfers between devices: 1.18 us -> 0.68 us  [layer_swap(): return lax.ppermute(value, 'layer', [(0, 1), (1, 0)])]
    ppermute x0 -> x1, waiting for transfers between devices: none -> 0.46 us  [cross_swap(): return lax.ppermute(value, ('tm', 'layer'), swap_pairs(pairs))]
  transfers between devices with their start and end apart: 6 -> 7, of which waited for: 5 -> 4; matrix products, arithmetic and copies ran while one was open for 4% -> 0% of each run, Pallas kernels for 0% -> 17%
where the time goes in v2:
time: 19.3 us; the launch traced here: 19 us
  Pallas kernels  5.81 us (30%)
  starting transfers between devices  5.64 us (29%)
  waiting for transfers between devices  5.03 us (26%)
  local copies, waits for them, and re-layouts  2.49 us (13%)
    pallas_call x6, Pallas kernels, call(): pl.pallas_call(kernel, out_shape=out_shape, in_specs=[pl.BlockSpec(memory...  5.81 us
    ppermute x2, waiting for transfers between devices, tile_swap(): return lax.ppermute(value, ('tile', 'tm', 'layer'), swap_pairs(pairs))  3.12 us
    ppermute x2, starting transfers between devices, tile_swap(): return lax.ppermute(value, ('tile', 'tm', 'layer'), swap_pairs(pairs))  3.1 us
    unnamed x14, local copies, waits for them, and re-layouts  2.49 us
    ppermute x1, waiting for transfers between devices, time_swap(): return lax.ppermute(value, ('tm', 'layer'), swap_pairs(pairs))  1.44 us
    ppermute x1, starting transfers between devices, time_swap(): return lax.ppermute(value, ('tm', 'layer'), swap_pairs(pairs))  1.1 us
    ppermute x1, starting transfers between devices, cross_swap(): return lax.ppermute(value, ('tm', 'layer'), swap_pairs(pairs))  0.76 us
    ppermute x3, starting transfers between devices, layer_swap(): return lax.ppermute(value, 'layer', [(0, 1), (1, 0)])  0.68 us
  transfers between devices with their start and end apart: 7, of which 4 were waited for; matrix products, arithmetic and copies ran while one was open for 0% of the time, Pallas kernels for 17%

profile of v2, /device:TPU:0, one launch (start us, length us, event | category | flops | bytes accessed | tf_op | source)
XLA Modules:
  0.0 19.0 jit_solution(7052543009543025479)
XLA Ops:
  0.0 0.0 copy-start.6
  0.0 0.0 copy-start.3
  0.0 0.0 copy-start.4
  0.0 0.0 copy-start.5
  0.0 0.5 %collective-permute-start.1 = (f32[4,16,256]{2,1,0:T(8,128)}, f32[4,16,256]{2,1,0:T(8,128)S(1)}, u32[]{:S(2)}, u32[]{:S(2)}) collective-permute-start(f32[4,16,256]{2,1,0:T(8,128)} %bitcast.2), channel_id=1, source_target_pairs={{0,1},{1,0},{2,3},{3,2},{4,5},{5,4},{6,7},{7,6},{8,9},{9,8},{10,11... | collective-permute-start | bytes 196616 | tf_op jit(solution)/shard_map/ppermute | solution.py:459
  0.5 0.1 collective-permute-start.2
  0.6 0.0 copy-done.6
  0.7 0.0 copy-done.3
  0.7 0.0 copy-done.4
  0.7 0.0 copy-done.5
  0.7 0.0 copy-start
  0.7 0.8 %copy-done = f32[1,4,16,256]{3,2,1,0:T(8,128)S(1)} copy-done((f32[1,4,16,256]{3,2,1,0:T(8,128)S(1)}, f32[1,4,16,256]{3,2,1,0:T(8,128)}, u32[]{:S(2)}) %copy-start) | copy-done | bytes 65560
  1.5 0.8 %copy-done.1 = s32[4,16,256]{2,1,0:T(8,128)S(1)} copy-done((s32[4,16,256]{2,1,0:T(8,128)S(1)}, s32[4,16,256]{2,1,0:T(8,128)}, u32[]{:S(2)}) %copy-start.1) | copy-done | bytes 65560
  2.4 0.7 %copy-done.2 = f32[1,16,256]{2,1,0:T(8,128)S(1)} copy-done((f32[1,16,256]{2,1,0:T(8,128)S(1)}, f32[1,16,256]{2,1,0:T(8,128)}, u32[]{:S(2)}) %copy-start.2) | copy-done | bytes 16408
  3.1 1.1 %pack_own.1 = (f32[14,8,256]{2,1,0:T(8,128)S(1)}, f32[4,8,256]{2,1,0:T(8,128)S(1)}, f32[8,128]{1,0:T(8,128)S(1)}) custom-call(f32[4,16,256]{2,1,0:T(8,128)S(1)} %bitcast.3, s32[4,16,256]{2,1,0:T(8,128)S(1)} %copy-done.1, f32[16,256]{1,0:T(8,128)S(1)} %bitcast.4, s32[16]{0:T(128)S(1)} %copy-done.3, f32[8]{0:T(128)S(1)} %copy-done.4, f32[8]{0:T(128)S(1)} %copy-done.5, ...), custom_call_target="tpu_custom_call" | custom-call | tf_op jit(solution)/shard_map/pack_own/pallas_call | solution.py:504
  4.2 3.0 %collective-permute-start = (f32[14,8,256]{2,1,0:T(8,128)S(1)}, f32[14,8,256]{2,1,0:T(8,128)S(1)}, u32[]{:S(2)}, u32[]{:S(2)}) collective-permute-start(f32[14,8,256]{2,1,0:T(8,128)S(1)} %get-tuple-element.16.own_ref), channel_id=1, source_target_pairs={{4,1},{1,4},{6,3},{3,6},{8,5},{5,8},{10,7},{7,10},{12,9},{9,12},{1... | collective-permute-start | bytes 344072 | tf_op jit(solution)/shard_map/ppermute | solution.py:475
  7.2 0.0 collective-permute-done.1.u_ref
  7.2 0.0 collective-permute-done.2.zone_ref
  7.2 0.2 %pack_other.1 = (f32[12,8,256]{2,1,0:T(8,128)S(1)}, f32[4,8,256]{2,1,0:T(8,128)S(1)}) custom-call(f32[4,16,256]{2,1,0:T(8,128)S(1)} %collective-permute-done.1.u_ref, s32[4,16,256]{2,1,0:T(8,128)S(1)} %collective-permute-done.2.zone_ref), custom_call_target="tpu_custom_call" | custom-call | tf_op jit(solution)/shard_map/pack_other/pallas_call | solution.py:504
  7.4 0.1 collective-permute-start.3
  7.5 1.5 %interior.1 = (f32[8,2,8,256]{3,2,1,0:T(8,128)S(1)}, f32[4,9,8,256]{3,2,1,0:T(8,128)S(1)}, f32[5,8,8,128]{3,2,1,0:T(8,128)S(1)}) custom-call(f32[14,8,256]{2,1,0:T(8,128)S(1)} %get-tuple-element.16.own_ref, f32[4,8,256]{2,1,0:T(8,128)S(1)} %get-tuple-element.19.own_tail, f32[12,8,256]{2,1,0:T(8,128)S(1)} %get-tuple-element.17.other_ref, ...), custom_call_target="tpu_custom_call" | custom-call | tf_op jit(solution)/shard_map/interior/pallas_call | solution.py:504
  9.0 1.0 %collective-permute-done.recv_ref = f32[14,8,256]{2,1,0:T(8,128)S(1)} collective-permute-done((f32[14,8,256]{2,1,0:T(8,128)S(1)}, f32[14,8,256]{2,1,0:T(8,128)S(1)}, u32[]{:S(2)}, u32[]{:S(2)}) %collective-permute-start) | collective-permute-done | bytes 114720 | tf_op jit(solution)/shard_map/ppermute | solution.py:475
  9.9 2.1 %collective-permute-done.3.recv_other = f32[12,8,256]{2,1,0:T(8,128)S(1)} collective-permute-done((f32[12,8,256]{2,1,0:T(8,128)S(1)}, f32[12,8,256]{2,1,0:T(8,128)S(1)}, u32[]{:S(2)}, u32[]{:S(2)}) %collective-permute-start.3) | collective-permute-done | bytes 98336 | tf_op jit(solution)/shard_map/ppermute | solution.py:475
  12.1 1.6 %edge.1 = (f32[3,8,128]{2,1,0:T(8,128)S(1)}, f32[26,8,128]{2,1,0:T(8,128)S(1)}, f32[5,2,8,128]{3,2,1,0:T(8,128)S(1)}) custom-call(f32[14,8,256]{2,1,0:T(8,128)S(1)} %collective-permute-done.recv_ref, f32[12,8,256]{2,1,0:T(8,128)S(1)} %collective-permute-done.3.recv_other, f32[14,8,256]{2,1,0:T(8,128)S(1)} %get-tuple-element.16.own_ref, ...), custom_call_target="tpu_custom_call" | custom-call | tf_op jit(solution)/shard_map/edge/pallas_call | solution.py:504
  13.7 0.1 collective-permute-start.6
  13.8 1.1 %collective-permute-start.4 = (f32[3,8,128]{2,1,0:T(8,128)S(1)}, f32[3,8,128]{2,1,0:T(8,128)S(1)}, u32[]{:S(2)}, u32[]{:S(2)}) collective-permute-start(f32[3,8,128]{2,1,0:T(8,128)S(1)} %get-tuple-element.23), channel_id=1, source_target_pairs={{0,2},{2,0},{1,3},{3,1},{4,6},{6,4},{5,7},{7,5},{8,10},{10,8},{9,1... | collective-permute-start | bytes 36872 | tf_op jit(solution)/shard_map/ppermute | solution.py:486
  14.9 0.8 %collective-permute-start.5 = (f32[3,8,128]{2,1,0:T(8,128)S(1)}, f32[3,8,128]{2,1,0:T(8,128)S(1)}, u32[]{:S(2)}, u32[]{:S(2)}) collective-permute-start(f32[3,8,128]{2,1,0:T(8,128)S(1)} %get-tuple-element.23), channel_id=1, source_target_pairs={{0,3},{3,0},{1,2},{2,1},{4,7},{7,4},{5,6},{6,5},{8,11},{11,8},{9,1... | collective-permute-start | bytes 36872 | tf_op jit(solution)/shard_map/ppermute | solution.py:492
  15.6 0.0 collective-permute-done.6.other_ref.refs_4_
  15.6 0.4 %base.1.refs_5_ = f32[4,16,256]{2,1,0:T(8,128)S(1)} custom-call(f32[5,8,8,128]{3,2,1,0:T(8,128)S(1)} %get-tuple-element.24.coarse_ref.refs_2_, f32[5,2,8,128]{3,2,1,0:T(8,128)S(1)} %get-tuple-element.25.outer_ref.refs_3_, f32[26,8,128]{2,1,0:T(8,128)S(1)} %get-tuple-element.26.share_ref, f32[26,8,128]{2,1,0:T(8,128)S(1)} %collective-permute-done.6.other_ref.refs_4_), custom_call_target="tpu_custom_call" | custom-call | tf_op jit(solution)/shard_map/base/pallas_call | solution.py:504
  16.1 1.4 %collective-permute-done.4.refs_0_ = f32[3,8,128]{2,1,0:T(8,128)S(1)} collective-permute-done((f32[3,8,128]{2,1,0:T(8,128)S(1)}, f32[3,8,128]{2,1,0:T(8,128)S(1)}, u32[]{:S(2)}, u32[]{:S(2)}) %collective-permute-start.4) | collective-permute-done | bytes 12320 | tf_op jit(solution)/shard_map/ppermute | solution.py:486
  17.5 0.5 %collective-permute-done.5.refs_1_ = f32[3,8,128]{2,1,0:T(8,128)S(1)} collective-permute-done((f32[3,8,128]{2,1,0:T(8,128)S(1)}, f32[3,8,128]{2,1,0:T(8,128)S(1)}, u32[]{:S(2)}, u32[]{:S(2)}) %collective-permute-start.5) | collective-permute-done | bytes 12320 | tf_op jit(solution)/shard_map/ppermute | solution.py:492
  18.0 1.1 %output.1 = f32[1,4,16,256]{3,2,1,0:T(8,128)} custom-call(f32[3,8,128]{2,1,0:T(8,128)S(1)} %collective-permute-done.4.refs_0_, f32[3,8,128]{2,1,0:T(8,128)S(1)} %collective-permute-done.5.refs_1_, f32[5,8,8,128]{3,2,1,0:T(8,128)S(1)} %get-tuple-element.24.coarse_ref.refs_2_, f32[5,2,8,128]{3,2,1,0:T(8,128)S(1)} %get-tuple-element.25.outer_ref.refs_3_, ...), custom_call_target="tpu_custom_call" | custom-call | tf_op jit(solution)/shard_map/output/pallas_call | solution.py:504
  (2 shorter events, 0.0 us)
Async XLA Ops:
  0.0 0.7 %copy-start.6 = (f32[8]{0:T(128)S(1)}, f32[8]{0:T(128)}, u32[]{:S(2)}) copy-start(f32[8]{0:T(128)} %soft_hbm.1) | copy-start | bytes 100
  0.0 0.7 %copy-start.3 = (s32[16]{0:T(128)S(1)}, s32[16]{0:T(128)}, u32[]{:S(2)}) copy-start(s32[16]{0:T(128)} %row_hbm.1) | copy-start | bytes 196
  0.0 0.7 %copy-start.4 = (f32[8]{0:T(128)S(1)}, f32[8]{0:T(128)}, u32[]{:S(2)}) copy-start(f32[8]{0:T(128)} %plane_hbm.1) | copy-start | bytes 100
  0.0 0.7 %copy-start.5 = (f32[8]{0:T(128)S(1)}, f32[8]{0:T(128)}, u32[]{:S(2)}) copy-start(f32[8]{0:T(128)} %thick_hbm.1) | copy-start | bytes 100
  0.0 7.2 %collective-permute-start.1 = (f32[4,16,256]{2,1,0:T(8,128)}, f32[4,16,256]{2,1,0:T(8,128)S(1)}, u32[]{:S(2)}, u32[]{:S(2)}) collective-permute-start(f32[4,16,256]{2,1,0:T(8,128)} %bitcast.2), channel_id=1, source_target_pairs={{0,1},{1,0},{2,3},{3,2},{4,5},{5,4},{6,7},{7,6},{8,9},{9,8},{10,11... | collective-permute-start | bytes 196616 | tf_op jit(solution)/shard_map/ppermute | solution.py:459
  0.5 6.6 %collective-permute-start.2 = (s32[4,16,256]{2,1,0:T(8,128)}, s32[4,16,256]{2,1,0:T(8,128)S(1)}, u32[]{:S(2)}, u32[]{:S(2)}) collective-permute-start(s32[4,16,256]{2,1,0:T(8,128)} %zone_hbm.1), channel_id=1, source_target_pairs={{0,1},{1,0},{2,3},{3,2},{4,5},{5,4},{6,7},{7,6},{8,9},{9,8},{10,11... | collective-permute-start | bytes 196616 | tf_op jit(solution)/shard_map/ppermute | solution.py:459
  0.7 0.8 %copy-start = (f32[1,4,16,256]{3,2,1,0:T(8,128)S(1)}, f32[1,4,16,256]{3,2,1,0:T(8,128)}, u32[]{:S(2)}) copy-start(f32[1,4,16,256]{3,2,1,0:T(8,128)} %param.7) | copy-start | bytes 196612
  1.5 0.8 %copy-start.1 = (s32[4,16,256]{2,1,0:T(8,128)S(1)}, s32[4,16,256]{2,1,0:T(8,128)}, u32[]{:S(2)}) copy-start(s32[4,16,256]{2,1,0:T(8,128)} %zone_hbm.1) | copy-start | bytes 196612
  2.4 0.7 %copy-start.2 = (f32[1,16,256]{2,1,0:T(8,128)S(1)}, f32[1,16,256]{2,1,0:T(8,128)}, u32[]{:S(2)}) copy-start(f32[1,16,256]{2,1,0:T(8,128)} %param.8) | copy-start | bytes 49156
  4.2 5.8 %collective-permute-start = (f32[14,8,256]{2,1,0:T(8,128)S(1)}, f32[14,8,256]{2,1,0:T(8,128)S(1)}, u32[]{:S(2)}, u32[]{:S(2)}) collective-permute-start(f32[14,8,256]{2,1,0:T(8,128)S(1)} %get-tuple-element.16.own_ref), channel_id=1, source_target_pairs={{4,1},{1,4},{6,3},{3,6},{8,5},{5,8},{10,7},{7,10},{12,9},{9,12},{1... | collective-permute-start | bytes 344072 | tf_op jit(solution)/shard_map/ppermute | solution.py:475
  7.4 4.7 %collective-permute-start.3 = (f32[12,8,256]{2,1,0:T(8,128)S(1)}, f32[12,8,256]{2,1,0:T(8,128)S(1)}, u32[]{:S(2)}, u32[]{:S(2)}) collective-permute-start(f32[12,8,256]{2,1,0:T(8,128)S(1)} %get-tuple-element.17.other_ref), channel_id=1, source_target_pairs={{4,1},{1,4},{6,3},{3,6},{8,5},{5,8},{10,7},{7,10},{12,9},{9,12},{1... | collective-permute-start | bytes 294920 | tf_op jit(solution)/shard_map/ppermute | solution.py:475
  13.7 1.9 %collective-permute-start.6 = (f32[26,8,128]{2,1,0:T(8,128)S(1)}, f32[26,8,128]{2,1,0:T(8,128)S(1)}, u32[]{:S(2)}, u32[]{:S(2)}) collective-permute-start(f32[26,8,128]{2,1,0:T(8,128)S(1)} %get-tuple-element.26.share_ref), channel_id=1, source_target_pairs={{0,1},{1,0},{2,3},{3,2},{4,5},{5,4},{6,7},{7,6},{8,9},{9,8},{10,11... | collective-permute-start | bytes 319496 | tf_op jit(solution)/shard_map/ppermute | solution.py:459
  13.8 3.8 %collective-permute-start.4 = (f32[3,8,128]{2,1,0:T(8,128)S(1)}, f32[3,8,128]{2,1,0:T(8,128)S(1)}, u32[]{:S(2)}, u32[]{:S(2)}) collective-permute-start(f32[3,8,128]{2,1,0:T(8,128)S(1)} %get-tuple-element.23), channel_id=1, source_target_pairs={{0,2},{2,0},{1,3},{3,1},{4,6},{6,4},{5,7},{7,5},{8,10},{10,8},{9,1... | collective-permute-start | bytes 36872 | tf_op jit(solution)/shard_map/ppermute | solution.py:486
  14.9 3.1 %collective-permute-start.5 = (f32[3,8,128]{2,1,0:T(8,128)S(1)}, f32[3,8,128]{2,1,0:T(8,128)S(1)}, u32[]{:S(2)}, u32[]{:S(2)}) collective-permute-start(f32[3,8,128]{2,1,0:T(8,128)S(1)} %get-tuple-element.23), channel_id=1, source_target_pairs={{0,3},{3,0},{1,2},{2,1},{4,7},{7,4},{5,6},{6,5},{8,11},{11,8},{9,1... | collective-permute-start | bytes 36872 | tf_op jit(solution)/shard_map/ppermute | solution.py:492

commit v3 on v2

--- a/solution.py
+++ b/solution.py
@@ -52,8 +52,11 @@
     )
 
 
-def pack_rows(core, u_ref, zone_ref, head_ref, tail_ref, flux_ref=None):
-    depth, width = u_ref.shape[:2]
+def pack_kernel(
+    u_hbm, zone_hbm, flux_hbm, head_ref, tail_ref, turned_ref, u_ref, zone_ref, flux_ref, sems
+):
+    copies = start_copies((u_hbm, zone_hbm, flux_hbm), (u_ref, zone_ref, flux_ref), sems)
+    width = u_ref.shape[1]
 
     def fill(mirror):
         for i in range(width):
@@ -62,69 +65,42 @@
                 [u_ref[:, row, :], zone_ref[:, row, :].astype(jnp.float32)], axis=0
             )
             slab = split_lanes(slab)
+            turned_ref[width - 1 - i] = slab
             if i < HALO:
                 head_ref[i] = slab
             else:
                 tail_ref[i - HALO] = slab
-        if flux_ref is not None:
-            flux = split_lanes(flux_ref[...])
-            for i in range(width):
-                row = width - 1 - i if mirror else i
-                head_ref[HALO + i // 8, i % 8 : i % 8 + 1, :] = flux[row : row + 1]
-
-    pl.when(core == 0)(lambda: fill(False))
-    pl.when(core == 1)(lambda: fill(True))
-
-
-def pack_own_kernel(
-    u_hbm,
-    zone_hbm,
-    flux_hbm,
-    row_hbm,
-    plane_hbm,
-    thick_hbm,
-    soft_hbm,
-    head_ref,
-    tail_ref,
-    table_ref,
-    u_ref,
-    zone_ref,
-    flux_ref,
-    row_ref,
-    plane_ref,
-    thick_ref,
-    soft_ref,
-    sems,
-):
-    sources = (u_hbm, zone_hbm, flux_hbm, row_hbm, plane_hbm, thick_hbm, soft_hbm)
-    targets = (u_ref, zone_ref, flux_ref, row_ref, plane_ref, thick_ref, soft_ref)
+        flux = split_lanes(flux_ref[...])
+        for i in range(width):
+            row = width - 1 - i if mirror else i
+            head_ref[HALO + i // 8, i % 8 : i % 8 + 1, :] = flux[row : row + 1]
+
+    for copy in copies:
+        copy.wait()
+    core = lax.axis_index("layer")
+    pl.when(core == 0)(lambda: fill(True))
+    pl.when(core == 1)(lambda: fill(False))
+
+
+def start_copies(sources, targets, sems):
     copies = [
         pltpu.make_async_copy(source, target, sems.at[k])
         for k, (source, target) in enumerate(zip(sources, targets))
     ]
     for copy in copies:
         copy.start()
-    for copy in copies[3:]:
-        copy.wait()
-    lane = iota(table_ref.shape, 1)
-    plane = thick = soft = jnp.zeros(table_ref.shape, jnp.float32)
+    return copies
+
+
+def fill_tables(table_ref, row_ref, plane_ref, thick_ref, soft_ref):
+    lane = iota((1, LANES), 1)
+    tables = [jnp.zeros((1, LANES), jnp.float32)] * 3
     for zone in range(row_ref.shape[0]):
-        at, here = row_ref[zone], lane == zone
-        plane = jnp.where(here, 0.5 * plane_ref[at], plane)
-        thick = jnp.where(here, 0.5 * thick_ref[at], thick)
-        soft = jnp.where(here, soft_ref[at], soft)
-    table_ref[0:1] = plane[:1]
-    table_ref[1:2] = (plane * soft)[:1]
-    table_ref[2:3] = thick[:1]
-    table_ref[3:4] = (thick * soft)[:1]
-    table_ref[4:8] = soft[:4]
-    for copy in copies[:3]:
-        copy.wait()
-    pack_rows(lax.axis_index("layer"), u_ref, zone_ref, head_ref, tail_ref, flux_ref)
-
-
-def pack_other_kernel(u_ref, zone_ref, head_ref, tail_ref):
-    pack_rows(lax.axis_index("layer"), u_ref, zone_ref, head_ref, tail_ref)
+        at = row_ref[zone]
+        values = (0.5 * plane_ref[at], 0.5 * thick_ref[at], soft_ref[at])
+        tables = [jnp.where(lane == zone, x, t) for x, t in zip(values, tables)]
+    for k in range(3):
+        table_ref[k : k + 1] = tables[k]
 
 
 def join_layers(low, high):
@@ -145,40 +121,50 @@
     return value[:, :LANES] + value[:, LANES:]
 
 
-def step_row(v, low, high, k_plane, k_thick, source, y_flow, layer_gap):
+def step_row(v, low, high, k_plane, k_thick, source, y_gain, layer_gap):
     layers = v.shape[0]
-    inside = iota(v.shape, 0) < layers - layer_gap
-    shift = layers - layer_gap
-    up_v, up_k = pltpu.roll(v, shift, 0), pltpu.roll(k_thick, shift, 0)
-    flow = jnp.where(inside, (k_thick + up_k) * (up_v - v), 0.0)
-    return v + source + (high - low) + y_flow(v, k_plane) + (flow - pltpu.roll(flow, layer_gap, 0))
+    layer = iota(v.shape, 0)
+    up, down = layers - layer_gap, layer_gap
+    from_up = jnp.where(layer < layers - layer_gap, pltpu.roll(v, up, 0) - v, 0.0)
+    from_down = jnp.where(layer >= layer_gap, pltpu.roll(v, down, 0) - v, 0.0)
+    z_gain = (k_thick + pltpu.roll(k_thick, up, 0)) * from_up
+    z_gain = z_gain + (k_thick + pltpu.roll(k_thick, down, 0)) * from_down
+    return ((v + source) + (high - low)) + (z_gain + y_gain(v, k_plane))
 
 
 def fine_y(v, k):
     va, vb, ka, kb = v[:, :LANES], v[:, LANES:], k[:, :LANES], k[:, LANES:]
+    lane = iota(va.shape, 1)
     inner = (ka + kb) * (vb - va)
-    next_v, next_k = pltpu.roll(va, LANES - 1, 1), pltpu.roll(ka, LANES - 1, 1)
-    outer = jnp.where(iota(va.shape, 1) < LANES - 1, (kb + next_k) * (next_v - vb), 0.0)
-    return jnp.concatenate([inner - pltpu.roll(outer, 1, 1), outer - inner], axis=1)
+    from_last = jnp.where(lane > 0, pltpu.roll(vb, 1, 1) - va, 0.0)
+    from_next = jnp.where(lane < LANES - 1, pltpu.roll(va, LANES - 1, 1) - vb, 0.0)
+    even = inner + (ka + pltpu.roll(kb, 1, 1)) * from_last
+    odd = (kb + pltpu.roll(ka, LANES - 1, 1)) * from_next - inner
+    return jnp.concatenate([even, odd], axis=1)
 
 
 def coarse_y(v, k):
-    next_v, next_k = pltpu.roll(v, LANES - 1, 1), pltpu.roll(k, LANES - 1, 1)
-    flow = jnp.where(iota(v.shape, 1) < LANES - 1, (k + next_k) * (next_v - v), 0.0)
-    return flow - pltpu.roll(flow, 1, 1)
+    lane = iota(v.shape, 1)
+    from_last = jnp.where(lane > 0, pltpu.roll(v, 1, 1) - v, 0.0)
+    from_next = jnp.where(lane < LANES - 1, pltpu.roll(v, LANES - 1, 1) - v, 0.0)
+    last = (k + pltpu.roll(k, 1, 1)) * from_last
+    return last + (k + pltpu.roll(k, LANES - 1, 1)) * from_next
 
 
 def outer_mask(core):
     tile, tiles = lax.axis_index("tile"), lax.axis_size("tile")
-    at_edge = jnp.where(core == 0, tile == 0, tile == tiles - 1)
+    at_edge = jnp.where(core == 1, tile == 0, tile == tiles - 1)
     return jnp.where(at_edge, 0.0, 1.0).astype(jnp.float32)
 
 
 def look_up(table_ref, zone):
     zone = zone.astype(jnp.int32)
     halves_of = (zone[:, :LANES], zone[:, LANES:])
-    tables = [jnp.broadcast_to(table_ref[k : k + 1, :], halves_of[0].shape) for k in range(5)]
-    return [jnp.concatenate([pick(t, z) for z in halves_of], axis=1) for t in tables]
+    tables = [jnp.broadcast_to(table_ref[k : k + 1, :], halves_of[0].shape) for k in range(3)]
+    plane, thick, soft = (
+        jnp.concatenate([pick(t, z) for z in halves_of], axis=1) for t in tables
+    )
+    return [plane, plane * soft, thick, thick * soft, soft]
 
 
 def flux_row(head_ref, i):
@@ -200,35 +186,55 @@
     coarse_ref[4, at] = jnp.where(pair, 0.5 * (first[4] + second[4]), 0.0)
 
 
-def fine_sweep(step, rows, load_v, store_v, load_coef, source, mask):
-    v_next = load_v(rows[0] - 1)
+def fine_step(rows, state, load_coef, source, mask):
+    v_next = state[rows[0] - 1]
     k_next = load_coef(0, rows[0] - 1) + load_coef(1, rows[0] - 1) * v_next
     high = None
+    fresh = {}
     for j in (rows[0] - 1, *rows):
         v, k_plane, low = v_next, k_next, high
-        v_next = load_v(j + 1)
+        v_next = state[j + 1]
         k_next = load_coef(0, j + 1) + load_coef(1, j + 1) * v_next
         high = (k_plane + k_next) * (v_next - v)
         if j == HALO - 1:
             high = high * mask
         if j >= rows[0]:
             k_thick = load_coef(2, j) + load_coef(3, j) * v
-            store_v(j, step_row(v, low, high, k_plane, k_thick, source(j), fine_y, 1))
+            fresh[j] = step_row(v, low, high, k_plane, k_thick, source(j), fine_y, 1)
+    return fresh
 
 
 def interior_kernel(
-    own_ref, own_tail, other_ref, other_tail, table_ref, edge_ref, coef_out, coarse_ref, v_ref, coef_ref
+    own_ref,
+    own_tail,
+    other_ref,
+    row_hbm,
+    plane_hbm,
+    thick_hbm,
+    soft_hbm,
+    edge_ref,
+    coef_out,
+    coarse_ref,
+    table_ref,
+    v_ref,
+    coef_ref,
+    row_ref,
+    plane_ref,
+    thick_ref,
+    soft_ref,
+    sems,
 ):
+    parameters = (row_ref, plane_ref, thick_ref, soft_ref)
+    for copy in start_copies((row_hbm, plane_hbm, thick_hbm, soft_hbm), parameters, sems):
+        copy.wait()
+    fill_tables(table_ref, *parameters)
     width, layers = v_ref.shape[:2]
     core = lax.axis_index("layer")
 
     def gather(order):
         rows = []
         for i in range(width):
-            slabs = [
-                ref[i] if i < HALO else tail[i - HALO]
-                for ref, tail in ((own_ref, own_tail), (other_ref, other_tail))
-            ]
+            slabs = (own_ref[i] if i < HALO else own_tail[i - HALO], other_ref[i])
             v, zone = join_layers(*(slabs[k] for k in order))
             coefs = look_up(table_ref, zone)
             v_ref[i] = v
@@ -243,19 +249,18 @@
 
     pl.when(core == 0)(lambda: gather((0, 1)))
     pl.when(core == 1)(lambda: gather((1, 0)))
+    state = {HALO + i: v_ref[i] for i in range(width)}
     for level in range(FINE_STEPS):
         if level:
-            fine_sweep(
-                level,
+            state = fine_step(
                 range(HALO + level, HALO + width - level),
-                lambda j: v_ref[j - HALO],
-                lambda j, value: v_ref.__setitem__(j - HALO, value),
+                state,
                 lambda k, j: coef_ref[k, j - HALO],
                 lambda j: to_source(flux_row(own_ref, j - HALO), layers),
                 None,
             )
         for i in range(2):
-            edge_ref[level, i] = v_ref[level + i]
+            edge_ref[level, i] = state[HALO + level + i]
 
 
 def edge_kernel(
@@ -270,6 +275,7 @@
     coarse_ref,
     v_ref,
     coef_ref,
+    source_ref,
 ):
     layers = v_ref.shape[1]
     half = v_ref.shape[0] - HALO
@@ -295,17 +301,18 @@
     pl.when(core == 0)(lambda: gather((1, 0)))
     pl.when(core == 1)(lambda: gather((0, 1)))
 
-    def source(j):
+    for j in range(HALO + FINE_STEPS):
         flux = flux_row(own_ref, j - HALO) if j >= HALO else flux_row(recv_ref, HALO - 1 - j)
-        return to_source(flux, layers)
-
+        source_ref[j] = to_source(flux, layers)
+    source = lambda j: source_ref[j]
+
+    state = {j: v_ref[j] for j in range(HALO)}
     for step in range(1, FINE_STEPS + 1):
-        reach = HALO + step - 1
-        fine_sweep(
-            step,
+        for i in range(2):
+            state[HALO + step - 1 + i] = edge_ref[step - 1, i]
+        state = fine_step(
             range(step, HALO + step),
-            lambda j: edge_ref[step - 1, j - reach] if j >= reach else v_ref[j],
-            lambda j, value: v_ref.__setitem__(j, value),
+            state,
             lambda k, j: own_coef[k, j - HALO] if j >= HALO else coef_ref[k, j],
             source,
             mask,
@@ -314,12 +321,12 @@
     even = iota((layers, LANES), 0) % 2 == 0
     restricted = []
     for j in range(HALO - EDGE, HALO + half, 2):
-        restricted.append(0.125 * pair_sum(halves(v_ref[j]) + halves(v_ref[j + 1])))
+        restricted.append(0.125 * pair_sum(halves(state[j]) + halves(state[j + 1])))
     for i in range(0, len(restricted), 2):
         rest_ref[i // 2] = jnp.where(even, restricted[i], restricted[i + 1])
     for i in range(half):
-        share_ref[2 * i] = v_ref[HALO + i][:, :LANES]
-        share_ref[2 * i + 1] = v_ref[HALO + i][:, LANES:]
+        share_ref[2 * i] = state[HALO + i][:, :LANES]
+        share_ref[2 * i + 1] = state[HALO + i][:, LANES:]
     for k in range(5):
         for i in range(COARSE_STEPS):
             share_ref[2 * half + k * COARSE_STEPS + i] = coarse_ref[k, i]
@@ -414,14 +421,14 @@
                 slab = jnp.concatenate(
                     [ref[2 * at] - base[j // 2], ref[2 * at + 1] - base[j // 2]], axis=1
                 )
-                slabs.append(slab[depth:] if mirror else slab[:depth])
+                slabs.append(slab[:depth] if mirror else slab[depth:])
             both = join_lanes(jnp.concatenate(slabs, axis=0))
             for i in (0, 1):
                 row = width - 1 - (j + i) if mirror else j + i
                 base_ref[:, row, :] = both[depth * i : depth * (i + 1)]
 
-    pl.when(core == 0)(lambda: write(False))
-    pl.when(core == 1)(lambda: write(True))
+    pl.when(core == 0)(lambda: write(True))
+    pl.when(core == 1)(lambda: write(False))
 
 
 def output_kernel(*refs):
@@ -434,13 +441,13 @@
     def write(mirror):
         for j, row in enumerate(moved):
             gain = jnp.concatenate([pick(row, half), pick(row, half + LANES // 2)], axis=1)
-            gain = gain[depth:] if mirror else gain[:depth]
+            gain = gain[:depth] if mirror else gain[depth:]
             for i in (2 * j, 2 * j + 1):
                 at = width - 1 - i if mirror else i
                 out_ref[0, :, at, :] = base_ref[:, at, :] + gain
 
-    pl.when(core == 0)(lambda: write(False))
-    pl.when(core == 1)(lambda: write(True))
+    pl.when(core == 0)(lambda: write(True))
+    pl.when(core == 1)(lambda: write(False))
 
 
 def advance_kernel(state_ref, coarse_ref, outer_ref, share_ref, other_ref, next_ref):
@@ -467,11 +474,11 @@
     tiles, slices = lax.axis_size("tile"), lax.axis_size("tm")
     at = lambda tile, time, core: (tile * slices + time) * 2 + core
     pairs = [
-        (at(t, m, 0), at(t - 1, m, 1)) for t in range(1, tiles) for m in range(slices)
+        (at(t, m, 1), at(t - 1, m, 0)) for t in range(1, tiles) for m in range(slices)
     ]
     for m in range(0, slices - 1, 2):
-        pairs.append((at(0, m, 0), at(0, m + 1, 0)))
-        pairs.append((at(tiles - 1, m, 1), at(tiles - 1, m + 1, 1)))
+        pairs.append((at(0, m, 1), at(0, m + 1, 1)))
+        pairs.append((at(tiles - 1, m, 0), at(tiles - 1, m + 1, 0)))
     return lax.ppermute(value, ("tile", "tm", "layer"), swap_pairs(pairs))
 
 
@@ -500,11 +507,16 @@
     slabs = lambda *lead: jax.ShapeDtypeStruct((*lead, layers, LANES), f32)
     wide = lambda *lead: jax.ShapeDtypeStruct((*lead, layers, length), f32)
 
-    def call(kernel, out_shape, *operands, name, scratch=(), memory=pltpu.VMEM):
+    def call(kernel, out_shape, *operands, name, scratch=(), in_hbm=()):
+        spaces = [pltpu.HBM if k in in_hbm else pltpu.VMEM for k in range(len(operands))]
+        operands = [
+            pltpu.with_memory_space_constraint(x, space) if space is pltpu.HBM else x
+            for x, space in zip(operands, spaces)
+        ]
         return pl.pallas_call(
             kernel,
             out_shape=out_shape,
-            in_specs=[pl.BlockSpec(memory_space=memory)] * len(operands),
+            in_specs=[pl.BlockSpec(memory_space=space) for space in spaces],
             out_specs=jax.tree.map(lambda _: VMEM, out_shape),
             scratch_shapes=scratch,
             compiler_params=pltpu.CompilerParams(vmem_limit_bytes=VMEM_BYTES),
@@ -512,40 +524,40 @@
         )(*operands)
 
     u_own = u_start[0]
-    u_other, zone_other = layer_swap(u_own), layer_swap(zone_of_cell)
-    own, own_tail, tables = call(
-        pack_own_kernel,
-        (wide(HALO + width // 8), wide(width - HALO), jax.ShapeDtypeStruct((8, LANES), f32)),
-        *(u_own, zone_of_cell, flux[0], zone_row, plane_rate, thick_rate, soften),
-        name="pack_own",
+    own, own_tail, turned = call(
+        pack_kernel,
+        (wide(HALO + width // 8), wide(width - HALO), wide(width)),
+        *(u_own, zone_of_cell, flux[0]),
+        name="pack",
         scratch=[
             pltpu.VMEM(u_own.shape, f32),
             pltpu.VMEM(zone_of_cell.shape, jnp.int32),
             pltpu.VMEM(flux.shape[1:], f32),
-            pltpu.SMEM(zone_row.shape, jnp.int32),
-            *[pltpu.SMEM(plane_rate.shape, f32)] * 3,
-            pltpu.SemaphoreType.DMA((7,)),
+            pltpu.SemaphoreType.DMA((3,)),
         ],
-        memory=pltpu.HBM,
-    )
-    recv = tile_swap(own)
-    other, other_tail = call(
-        pack_other_kernel,
-        (wide(HALO), wide(width - HALO)),
-        *(u_other, zone_other),
-        name="pack_other",
-    )
-    recv_other = tile_swap(other)
-
-    levels, own_coef, coarse = call(
+        in_hbm=range(3),
+    )
+    other = layer_swap(turned)
+    recv, recv_other = tile_swap(own), tile_swap(other[:HALO])
+
+    levels, own_coef, coarse, tables = call(
         interior_kernel,
-        (wide(FINE_STEPS, 2), wide(4, FINE_STEPS + 1), slabs(5, half)),
-        *(own, own_tail, other, other_tail, tables),
+        (
+            wide(FINE_STEPS, 2),
+            wide(4, FINE_STEPS + 1),
+            slabs(5, half),
+            jax.ShapeDtypeStruct((3, LANES), f32),
+        ),
+        *(own, own_tail, other, zone_row, plane_rate, thick_rate, soften),
         name="interior",
         scratch=[
             pltpu.VMEM((width, layers, length), f32),
             pltpu.VMEM((4, width, layers, length), f32),
+            pltpu.SMEM(zone_row.shape, jnp.int32),
+            *[pltpu.SMEM(plane_rate.shape, f32)] * 3,
+            pltpu.SemaphoreType.DMA((4,)),
         ],
+        in_hbm=range(3, 7),
     )
     rest, share, outer = call(
         edge_kernel,
@@ -559,6 +571,7 @@
         scratch=[
             pltpu.VMEM((HALO + half, layers, length), f32),
             pltpu.VMEM((4, HALO, layers, length), f32),
+            pltpu.VMEM((HALO + FINE_STEPS, layers, length), f32),
         ],
     )
 

time: 19.3 us -> 15.6 us (0.81)
  local copies, waits for them, and re-layouts: 2.49 us -> 0.01 us
  waiting for transfers between devices: 5.03 us -> 3.88 us
  Pallas kernels: 5.81 us -> 5.31 us
  starting transfers between devices: 5.64 us -> 6.14 us
    unnamed x14 -> x0, local copies, waits for them, and re-layouts: 2.49 us -> none
    ppermute x2, waiting for transfers between devices: 3.12 us -> 1.41 us  [tile_swap(): return lax.ppermute(value, ('tile', 'tm', 'layer'), swap_pairs(pairs))]
    ppermute x2, starting transfers between devices: 3.1 us -> 3.69 us  [tile_swap(): return lax.ppermute(value, ('tile', 'tm', 'layer'), swap_pairs(pairs))]
    pallas_call x6 -> x5, Pallas kernels: 5.81 us -> 5.31 us  [call(): pl.pallas_call(kernel, out_shape=out_shape, in_specs=[pl.BlockSpec(memory...]
    ppermute x1, starting transfers between devices: 0.76 us -> 0.31 us  [cross_swap(): return lax.ppermute(value, ('tm', 'layer'), swap_pairs(pairs))]
    ppermute x1, waiting for transfers between devices: 0.46 us -> 0.92 us  [cross_swap(): return lax.ppermute(value, ('tm', 'layer'), swap_pairs(pairs))]
    ppermute x1, starting transfers between devices: 1.1 us -> 1.56 us  [time_swap(): return lax.ppermute(value, ('tm', 'layer'), swap_pairs(pairs))]
    ppermute x3 -> x2, starting transfers between devices: 0.68 us -> 0.59 us  [layer_swap(): return lax.ppermute(value, 'layer', [(0, 1), (1, 0)])]
  transfers between devices with their start and end apart: 7 -> 6, of which waited for: 4 -> 3; matrix products, arithmetic and copies ran while one was open for 0% -> 0% of each run, Pallas kernels for 17% -> 13%
where the time goes in v3:
time: 15.6 us; the launch traced here: 15.4 us
  starting transfers between devices  6.14 us (39%)
  Pallas kernels  5.31 us (34%)
  waiting for transfers between devices  3.88 us (25%)
    pallas_call x5, Pallas kernels, call(): pl.pallas_call(kernel, out_shape=out_shape, in_specs=[pl.BlockSpec(memory...  5.31 us
    ppermute x2, starting transfers between devices, tile_swap(): return lax.ppermute(value, ('tile', 'tm', 'layer'), swap_pairs(pairs))  3.69 us
    ppermute x1, starting transfers between devices, time_swap(): return lax.ppermute(value, ('tm', 'layer'), swap_pairs(pairs))  1.56 us
    ppermute x1, waiting for transfers between devices, time_swap(): return lax.ppermute(value, ('tm', 'layer'), swap_pairs(pairs))  1.55 us
    ppermute x2, waiting for transfers between devices, tile_swap(): return lax.ppermute(value, ('tile', 'tm', 'layer'), swap_pairs(pairs))  1.41 us
    ppermute x1, waiting for transfers between devices, cross_swap(): return lax.ppermute(value, ('tm', 'layer'), swap_pairs(pairs))  0.92 us
    ppermute x2, starting transfers between devices, layer_swap(): return lax.ppermute(value, 'layer', [(0, 1), (1, 0)])  0.59 us
  transfers between devices with their start and end apart: 6, of which 3 were waited for; matrix products, arithmetic and copies ran while one was open for 0% of the time, Pallas kernels for 13%

profile of v3, /device:TPU:0, one launch (start us, length us, event | category | flops | bytes accessed | tf_op | source)
XLA Modules:
  0.0 15.4 jit_solution(14723657926226793146)
XLA Ops:
  0.0 1.1 %pack.1 = (f32[14,8,256]{2,1,0:T(8,128)S(1)}, f32[4,8,256]{2,1,0:T(8,128)S(1)}, f32[16,8,256]{2,1,0:T(8,128)S(1)}) custom-call(f32[4,16,256]{2,1,0:T(8,128)} %bitcast.2, s32[4,16,256]{2,1,0:T(8,128)} %zone_hbm.1, f32[16,256]{1,0:T(8,128)} %bitcast.3), custom_call_target="tpu_custom_call" | custom-call | tf_op jit(solution)/shard_map/pack/pallas_call | solution.py:516
  1.1 0.5 %collective-permute-start.1 = (f32[16,8,256]{2,1,0:T(8,128)S(1)}, f32[16,8,256]{2,1,0:T(8,128)S(1)}, u32[]{:S(2)}, u32[]{:S(2)}) collective-permute-start(f32[16,8,256]{2,1,0:T(8,128)S(1)} %get-tuple-element.16), channel_id=1, source_target_pairs={{0,1},{1,0},{2,3},{3,2},{4,5},{5,4},{6,7},{7,6},{8,9},{9,8},{10,11... | collective-permute-start | bytes 393224 | tf_op jit(solution)/shard_map/ppermute | solution.py:466
  1.7 2.7 %collective-permute-start = (f32[14,8,256]{2,1,0:T(8,128)S(1)}, f32[14,8,256]{2,1,0:T(8,128)S(1)}, u32[]{:S(2)}, u32[]{:S(2)}) collective-permute-start(f32[14,8,256]{2,1,0:T(8,128)S(1)} %get-tuple-element.15.own_ref), channel_id=1, source_target_pairs={{5,0},{0,5},{7,2},{2,7},{9,4},{4,9},{11,6},{6,11},{13,8},{8,13},{1... | collective-permute-start | bytes 344072 | tf_op jit(solution)/shard_map/ppermute | solution.py:482
  4.3 0.0 collective-permute-done.1.other_ref
  4.4 1.0 %collective-permute-start.2 = (f32[12,8,256]{2,1,0:T(8,128)S(1)}, f32[12,8,256]{2,1,0:T(8,128)S(1)}, u32[]{:S(2)}, u32[]{:S(2)}) collective-permute-start(f32[12,8,256]{2,1,0:T(8,128)S(1)} %slice.4), channel_id=1, source_target_pairs={{5,0},{0,5},{7,2},{2,7},{9,4},{4,9},{11,6},{6,11},{13,8},{8,13},{1... | collective-permute-start | bytes 294920 | tf_op jit(solution)/shard_map/ppermute | solution.py:482
  5.4 1.7 %interior.1 = (f32[8,2,8,256]{3,2,1,0:T(8,128)S(1)}, f32[4,9,8,256]{3,2,1,0:T(8,128)S(1)}, f32[5,8,8,128]{3,2,1,0:T(8,128)S(1)}, f32[3,128]{1,0:T(4,128)S(1)}) custom-call(f32[14,8,256]{2,1,0:T(8,128)S(1)} %get-tuple-element.15.own_ref, f32[4,8,256]{2,1,0:T(8,128)S(1)} %get-tuple-element.17.own_tail, f32[16,8,256]{2,1,0:T(8,128)S(1)} %collective-permute-done.1.other_ref, ...), custom_call_target="tpu_custom_call" | custom-call | tf_op jit(solution)/shard_map/interior/pallas_call | solution.py:516
  7.0 0.0 collective-permute-done.recv_ref
  7.0 1.4 %collective-permute-done.2.recv_other = f32[12,8,256]{2,1,0:T(8,128)S(1)} collective-permute-done((f32[12,8,256]{2,1,0:T(8,128)S(1)}, f32[12,8,256]{2,1,0:T(8,128)S(1)}, u32[]{:S(2)}, u32[]{:S(2)}) %collective-permute-start.2) | collective-permute-done | bytes 98336 | tf_op jit(solution)/shard_map/ppermute | solution.py:482
  8.5 1.2 %edge.1 = (f32[3,8,128]{2,1,0:T(8,128)S(1)}, f32[26,8,128]{2,1,0:T(8,128)S(1)}, f32[5,2,8,128]{3,2,1,0:T(8,128)S(1)}) custom-call(f32[14,8,256]{2,1,0:T(8,128)S(1)} %collective-permute-done.recv_ref, f32[12,8,256]{2,1,0:T(8,128)S(1)} %collective-permute-done.2.recv_other, f32[14,8,256]{2,1,0:T(8,128)S(1)} %get-tuple-element.15.own_ref, ...), custom_call_target="tpu_custom_call" | custom-call | tf_op jit(solution)/shard_map/edge/pallas_call | solution.py:516
  9.7 0.1 collective-permute-start.5
  9.8 1.6 %collective-permute-start.3 = (f32[3,8,128]{2,1,0:T(8,128)S(1)}, f32[3,8,128]{2,1,0:T(8,128)S(1)}, u32[]{:S(2)}, u32[]{:S(2)}) collective-permute-start(f32[3,8,128]{2,1,0:T(8,128)S(1)} %get-tuple-element.21), channel_id=1, source_target_pairs={{0,2},{2,0},{1,3},{3,1},{4,6},{6,4},{5,7},{7,5},{8,10},{10,8},{9,1... | collective-permute-start | bytes 36872 | tf_op jit(solution)/shard_map/ppermute | solution.py:493
  11.3 0.3 %collective-permute-start.4 = (f32[3,8,128]{2,1,0:T(8,128)S(1)}, f32[3,8,128]{2,1,0:T(8,128)S(1)}, u32[]{:S(2)}, u32[]{:S(2)}) collective-permute-start(f32[3,8,128]{2,1,0:T(8,128)S(1)} %get-tuple-element.21), channel_id=1, source_target_pairs={{0,3},{3,0},{1,2},{2,1},{4,7},{7,4},{5,6},{6,5},{8,11},{11,8},{9,1... | collective-permute-start | bytes 36872 | tf_op jit(solution)/shard_map/ppermute | solution.py:499
  11.6 0.0 collective-permute-done.5.other_ref.refs_4_
  11.6 0.3 %base.1.refs_5_ = f32[4,16,256]{2,1,0:T(8,128)S(1)} custom-call(f32[5,8,8,128]{3,2,1,0:T(8,128)S(1)} %get-tuple-element.22.coarse_ref.refs_2_, f32[5,2,8,128]{3,2,1,0:T(8,128)S(1)} %get-tuple-element.23.outer_ref.refs_3_, f32[26,8,128]{2,1,0:T(8,128)S(1)} %get-tuple-element.24.share_ref, f32[26,8,128]{2,1,0:T(8,128)S(1)} %collective-permute-done.5.other_ref.refs_4_), custom_call_target="tpu_custom_call" | custom-call | tf_op jit(solution)/shard_map/base/pallas_call | solution.py:516
  12.0 1.6 %collective-permute-done.3.refs_0_ = f32[3,8,128]{2,1,0:T(8,128)S(1)} collective-permute-done((f32[3,8,128]{2,1,0:T(8,128)S(1)}, f32[3,8,128]{2,1,0:T(8,128)S(1)}, u32[]{:S(2)}, u32[]{:S(2)}) %collective-permute-start.3) | collective-permute-done | bytes 12320 | tf_op jit(solution)/shard_map/ppermute | solution.py:493
  13.5 0.9 %collective-permute-done.4.refs_1_ = f32[3,8,128]{2,1,0:T(8,128)S(1)} collective-permute-done((f32[3,8,128]{2,1,0:T(8,128)S(1)}, f32[3,8,128]{2,1,0:T(8,128)S(1)}, u32[]{:S(2)}, u32[]{:S(2)}) %collective-permute-start.4) | collective-permute-done | bytes 12320 | tf_op jit(solution)/shard_map/ppermute | solution.py:499
  14.5 0.9 %output.1 = f32[1,4,16,256]{3,2,1,0:T(8,128)} custom-call(f32[3,8,128]{2,1,0:T(8,128)S(1)} %collective-permute-done.3.refs_0_, f32[3,8,128]{2,1,0:T(8,128)S(1)} %collective-permute-done.4.refs_1_, f32[5,8,8,128]{3,2,1,0:T(8,128)S(1)} %get-tuple-element.22.coarse_ref.refs_2_, f32[5,2,8,128]{3,2,1,0:T(8,128)S(1)} %get-tuple-element.23.outer_ref.refs_3_, ...), custom_call_target="tpu_custom_call" | custom-call | tf_op jit(solution)/shard_map/output/pallas_call | solution.py:516
  (1 shorter events, 0.0 us)
Async XLA Ops:
  1.1 3.2 %collective-permute-start.1 = (f32[16,8,256]{2,1,0:T(8,128)S(1)}, f32[16,8,256]{2,1,0:T(8,128)S(1)}, u32[]{:S(2)}, u32[]{:S(2)}) collective-permute-start(f32[16,8,256]{2,1,0:T(8,128)S(1)} %get-tuple-element.16), channel_id=1, source_target_pairs={{0,1},{1,0},{2,3},{3,2},{4,5},{5,4},{6,7},{7,6},{8,9},{9,8},{10,11... | collective-permute-start | bytes 393224 | tf_op jit(solution)/shard_map/ppermute | solution.py:466
  1.7 5.4 %collective-permute-start = (f32[14,8,256]{2,1,0:T(8,128)S(1)}, f32[14,8,256]{2,1,0:T(8,128)S(1)}, u32[]{:S(2)}, u32[]{:S(2)}) collective-permute-start(f32[14,8,256]{2,1,0:T(8,128)S(1)} %get-tuple-element.15.own_ref), channel_id=1, source_target_pairs={{5,0},{0,5},{7,2},{2,7},{9,4},{4,9},{11,6},{6,11},{13,8},{8,13},{1... | collective-permute-start | bytes 344072 | tf_op jit(solution)/shard_map/ppermute | solution.py:482
  4.4 4.1 %collective-permute-start.2 = (f32[12,8,256]{2,1,0:T(8,128)S(1)}, f32[12,8,256]{2,1,0:T(8,128)S(1)}, u32[]{:S(2)}, u32[]{:S(2)}) collective-permute-start(f32[12,8,256]{2,1,0:T(8,128)S(1)} %slice.4), channel_id=1, source_target_pairs={{5,0},{0,5},{7,2},{2,7},{9,4},{4,9},{11,6},{6,11},{13,8},{8,13},{1... | collective-permute-start | bytes 294920 | tf_op jit(solution)/shard_map/ppermute | solution.py:482
  9.7 1.9 %collective-permute-start.5 = (f32[26,8,128]{2,1,0:T(8,128)S(1)}, f32[26,8,128]{2,1,0:T(8,128)S(1)}, u32[]{:S(2)}, u32[]{:S(2)}) collective-permute-start(f32[26,8,128]{2,1,0:T(8,128)S(1)} %get-tuple-element.24.share_ref), channel_id=1, source_target_pairs={{0,1},{1,0},{2,3},{3,2},{4,5},{5,4},{6,7},{7,6},{8,9},{9,8},{10,11... | collective-permute-start | bytes 319496 | tf_op jit(solution)/shard_map/ppermute | solution.py:466
  9.8 3.8 %collective-permute-start.3 = (f32[3,8,128]{2,1,0:T(8,128)S(1)}, f32[3,8,128]{2,1,0:T(8,128)S(1)}, u32[]{:S(2)}, u32[]{:S(2)}) collective-permute-start(f32[3,8,128]{2,1,0:T(8,128)S(1)} %get-tuple-element.21), channel_id=1, source_target_pairs={{0,2},{2,0},{1,3},{3,1},{4,6},{6,4},{5,7},{7,5},{8,10},{10,8},{9,1... | collective-permute-start | bytes 36872 | tf_op jit(solution)/shard_map/ppermute | solution.py:493
  11.3 3.1 %collective-permute-start.4 = (f32[3,8,128]{2,1,0:T(8,128)S(1)}, f32[3,8,128]{2,1,0:T(8,128)S(1)}, u32[]{:S(2)}, u32[]{:S(2)}) collective-permute-start(f32[3,8,128]{2,1,0:T(8,128)S(1)} %get-tuple-element.21), channel_id=1, source_target_pairs={{0,3},{3,0},{1,2},{2,1},{4,7},{7,4},{5,6},{6,5},{8,11},{11,8},{9,1... | collective-permute-start | bytes 36872 | tf_op jit(solution)/shard_map/ppermute | solution.py:499

commit v4 on v3

--- a/solution.py
+++ b/solution.py
@@ -121,7 +121,7 @@
     return value[:, :LANES] + value[:, LANES:]
 
 
-def step_row(v, low, high, k_plane, k_thick, source, y_gain, layer_gap):
+def step_row(v, low, high, k_plane, k_thick, source, y_gain, layer_gap, coefs_beside=None):
     layers = v.shape[0]
     layer = iota(v.shape, 0)
     up, down = layers - layer_gap, layer_gap
@@ -129,21 +129,26 @@
     from_down = jnp.where(layer >= layer_gap, pltpu.roll(v, down, 0) - v, 0.0)
     z_gain = (k_thick + pltpu.roll(k_thick, up, 0)) * from_up
     z_gain = z_gain + (k_thick + pltpu.roll(k_thick, down, 0)) * from_down
-    return ((v + source) + (high - low)) + (z_gain + y_gain(v, k_plane))
-
-
-def fine_y(v, k):
+    return ((v + source) + (high - low)) + (z_gain + y_gain(v, k_plane, coefs_beside))
+
+
+def beside(row):
+    even, odd = row[:, :LANES], row[:, LANES:]
+    return jnp.concatenate([pltpu.roll(odd, 1, 1), pltpu.roll(even, LANES - 1, 1)], axis=1)
+
+
+def fine_y(v, k, coefs_beside):
     va, vb, ka, kb = v[:, :LANES], v[:, LANES:], k[:, :LANES], k[:, LANES:]
-    lane = iota(va.shape, 1)
+    lane = iota(v.shape, 1)
     inner = (ka + kb) * (vb - va)
-    from_last = jnp.where(lane > 0, pltpu.roll(vb, 1, 1) - va, 0.0)
-    from_next = jnp.where(lane < LANES - 1, pltpu.roll(va, LANES - 1, 1) - vb, 0.0)
-    even = inner + (ka + pltpu.roll(kb, 1, 1)) * from_last
-    odd = (kb + pltpu.roll(ka, LANES - 1, 1)) * from_next - inner
-    return jnp.concatenate([even, odd], axis=1)
-
-
-def coarse_y(v, k):
+    rate, slope = coefs_beside
+    v_beside = beside(v)
+    drop = jnp.where((lane > 0) & (lane < 2 * LANES - 1), v_beside - v, 0.0)
+    outer = (k + (rate + slope * v_beside)) * drop
+    return outer + jnp.concatenate([inner, -inner], axis=1)
+
+
+def coarse_y(v, k, _):
     lane = iota(v.shape, 1)
     from_last = jnp.where(lane > 0, pltpu.roll(v, 1, 1) - v, 0.0)
     from_next = jnp.where(lane < LANES - 1, pltpu.roll(v, LANES - 1, 1) - v, 0.0)
@@ -200,7 +205,8 @@
             high = high * mask
         if j >= rows[0]:
             k_thick = load_coef(2, j) + load_coef(3, j) * v
-            fresh[j] = step_row(v, low, high, k_plane, k_thick, source(j), fine_y, 1)
+            near = [load_coef(k, j) for k in (4, 5)]
+            fresh[j] = step_row(v, low, high, k_plane, k_thick, source(j), fine_y, 1, near)
     return fresh
 
 
@@ -231,24 +237,25 @@
     width, layers = v_ref.shape[:2]
     core = lax.axis_index("layer")
 
-    def gather(order):
+    first = core == 0
+
+    def gather():
         rows = []
         for i in range(width):
-            slabs = (own_ref[i] if i < HALO else own_tail[i - HALO], other_ref[i])
-            v, zone = join_layers(*(slabs[k] for k in order))
+            a, b = own_ref[i] if i < HALO else own_tail[i - HALO], other_ref[i]
+            v, zone = join_layers(jnp.where(first, a, b), jnp.where(first, b, a))
             coefs = look_up(table_ref, zone)
             v_ref[i] = v
-            for k in range(4):
-                coef_ref[k, i] = coefs[k]
+            for k, coef in enumerate((*coefs[:4], beside(coefs[0]), beside(coefs[1]))):
+                coef_ref[k, i] = coef
                 if i < coef_out.shape[1]:
-                    coef_out[k, i] = coefs[k]
+                    coef_out[k, i] = coef
             rows.append((coefs, v, flux_row(own_ref, i)))
             if i % 2:
                 to_coarse(coarse_ref, i // 2, rows)
                 rows = []
 
-    pl.when(core == 0)(lambda: gather((0, 1)))
-    pl.when(core == 1)(lambda: gather((1, 0)))
+    gather()
     state = {HALO + i: v_ref[i] for i in range(width)}
     for level in range(FINE_STEPS):
         if level:
@@ -282,24 +289,25 @@
     core = lax.axis_index("layer")
     mask = outer_mask(core)
 
-    def gather(order):
+    first = core == 0
+
+    def gather():
         rows = []
         for j in range(HALO):
             i = HALO - 1 - j
-            slabs = (recv_ref[i], recv_other[i])
-            v, zone = join_layers(*(slabs[k] for k in order))
+            a, b = recv_ref[i], recv_other[i]
+            v, zone = join_layers(jnp.where(first, b, a), jnp.where(first, a, b))
             coefs = look_up(table_ref, zone)
             v_ref[j] = v
-            for k in range(4):
-                coef_ref[k, j] = coefs[k]
+            for k, coef in enumerate((*coefs[:4], beside(coefs[0]), beside(coefs[1]))):
+                coef_ref[k, j] = coef
             rows.append((coefs, v, flux_row(recv_ref, i)))
             if j % 2:
                 if j >= HALO - EDGE:
                     to_coarse(coarse_ref, (j - (HALO - EDGE)) // 2, rows)
                 rows = []
 
-    pl.when(core == 0)(lambda: gather((1, 0)))
-    pl.when(core == 1)(lambda: gather((0, 1)))
+    gather()
 
     for j in range(HALO + FINE_STEPS):
         flux = flux_row(own_ref, j - HALO) if j >= HALO else flux_row(recv_ref, HALO - 1 - j)
@@ -544,7 +552,7 @@
         interior_kernel,
         (
             wide(FINE_STEPS, 2),
-            wide(4, FINE_STEPS + 1),
+            wide(6, FINE_STEPS + 1),
             slabs(5, half),
             jax.ShapeDtypeStruct((3, LANES), f32),
         ),
@@ -552,7 +560,7 @@
         name="interior",
         scratch=[
             pltpu.VMEM((width, layers, length), f32),
-            pltpu.VMEM((4, width, layers, length), f32),
+            pltpu.VMEM((6, width, layers, length), f32),
             pltpu.SMEM(zone_row.shape, jnp.int32),
             *[pltpu.SMEM(plane_rate.shape, f32)] * 3,
             pltpu.SemaphoreType.DMA((4,)),
@@ -570,7 +578,7 @@
         name="edge",
         scratch=[
             pltpu.VMEM((HALO + half, layers, length), f32),
-            pltpu.VMEM((4, HALO, layers, length), f32),
+            pltpu.VMEM((6, HALO, layers, length), f32),
             pltpu.VMEM((HALO + FINE_STEPS, layers, length), f32),
         ],
     )

time: 15.6 us -> 15.4 us (0.987)
  Pallas kernels: 5.31 us -> 5.01 us
    pallas_call x5, Pallas kernels: 5.31 us -> 5.01 us  [call(): pl.pallas_call(kernel, out_shape=out_shape, in_specs=[pl.BlockSpec(memory...]
  transfers between devices with their start and end apart: 6 -> 6, of which waited for: 3 -> 3; matrix products, arithmetic and copies ran while one was open for 0% -> 0% of each run, Pallas kernels for 13% -> 12%
where the time goes in v4:
time: 15.4 us; the launch traced here: 15.2 us
  starting transfers between devices  6.14 us (40%)
  Pallas kernels  5.01 us (33%)
  waiting for transfers between devices  4.02 us (26%)
    pallas_call x5, Pallas kernels, call(): pl.pallas_call(kernel, out_shape=out_shape, in_specs=[pl.BlockSpec(memory...  5.01 us
    ppermute x2, starting transfers between devices, tile_swap(): return lax.ppermute(value, ('tile', 'tm', 'layer'), swap_pairs(pairs))  3.69 us
    ppermute x1, starting transfers between devices, time_swap(): return lax.ppermute(value, ('tm', 'layer'), swap_pairs(pairs))  1.56 us
    ppermute x1, waiting for transfers between devices, time_swap(): return lax.ppermute(value, ('tm', 'layer'), swap_pairs(pairs))  1.55 us
    ppermute x2, waiting for transfers between devices, tile_swap(): return lax.ppermute(value, ('tile', 'tm', 'layer'), swap_pairs(pairs))  1.55 us
    ppermute x1, waiting for transfers between devices, cross_swap(): return lax.ppermute(value, ('tm', 'layer'), swap_pairs(pairs))  0.92 us
    ppermute x2, starting transfers between devices, layer_swap(): return lax.ppermute(value, 'layer', [(0, 1), (1, 0)])  0.59 us
  transfers between devices with their start and end apart: 6, of which 3 were waited for; matrix products, arithmetic and copies ran while one was open for 0% of the time, Pallas kernels for 12%

profile of v4, /device:TPU:0, one launch (start us, length us, event | category | flops | bytes accessed | tf_op | source)
XLA Modules:
  0.0 15.2 jit_solution(14158427510472319240)
XLA Ops:
  0.0 1.1 %pack.1 = (f32[14,8,256]{2,1,0:T(8,128)S(1)}, f32[4,8,256]{2,1,0:T(8,128)S(1)}, f32[16,8,256]{2,1,0:T(8,128)S(1)}) custom-call(f32[4,16,256]{2,1,0:T(8,128)} %bitcast.2, s32[4,16,256]{2,1,0:T(8,128)} %zone_hbm.1, f32[16,256]{1,0:T(8,128)} %bitcast.3), custom_call_target="tpu_custom_call" | custom-call | tf_op jit(solution)/shard_map/pack/pallas_call | solution.py:524
  1.1 0.5 %collective-permute-start.1 = (f32[16,8,256]{2,1,0:T(8,128)S(1)}, f32[16,8,256]{2,1,0:T(8,128)S(1)}, u32[]{:S(2)}, u32[]{:S(2)}) collective-permute-start(f32[16,8,256]{2,1,0:T(8,128)S(1)} %get-tuple-element.16), channel_id=1, source_target_pairs={{0,1},{1,0},{2,3},{3,2},{4,5},{5,4},{6,7},{7,6},{8,9},{9,8},{10,11... | collective-permute-start | bytes 393224 | tf_op jit(solution)/shard_map/ppermute | solution.py:474
  1.7 2.7 %collective-permute-start = (f32[14,8,256]{2,1,0:T(8,128)S(1)}, f32[14,8,256]{2,1,0:T(8,128)S(1)}, u32[]{:S(2)}, u32[]{:S(2)}) collective-permute-start(f32[14,8,256]{2,1,0:T(8,128)S(1)} %get-tuple-element.15.own_ref), channel_id=1, source_target_pairs={{5,0},{0,5},{7,2},{2,7},{9,4},{4,9},{11,6},{6,11},{13,8},{8,13},{1... | collective-permute-start | bytes 344072 | tf_op jit(solution)/shard_map/ppermute | solution.py:490
  4.3 0.0 collective-permute-done.1.other_ref
  4.4 1.0 %collective-permute-start.2 = (f32[12,8,256]{2,1,0:T(8,128)S(1)}, f32[12,8,256]{2,1,0:T(8,128)S(1)}, u32[]{:S(2)}, u32[]{:S(2)}) collective-permute-start(f32[12,8,256]{2,1,0:T(8,128)S(1)} %slice.4), channel_id=1, source_target_pairs={{5,0},{0,5},{7,2},{2,7},{9,4},{4,9},{11,6},{6,11},{13,8},{8,13},{1... | collective-permute-start | bytes 294920 | tf_op jit(solution)/shard_map/ppermute | solution.py:490
  5.4 1.5 %interior.1 = (f32[8,2,8,256]{3,2,1,0:T(8,128)S(1)}, f32[6,9,8,256]{3,2,1,0:T(8,128)S(1)}, f32[5,8,8,128]{3,2,1,0:T(8,128)S(1)}, f32[3,128]{1,0:T(4,128)S(1)}) custom-call(f32[14,8,256]{2,1,0:T(8,128)S(1)} %get-tuple-element.15.own_ref, f32[4,8,256]{2,1,0:T(8,128)S(1)} %get-tuple-element.17.own_tail, f32[16,8,256]{2,1,0:T(8,128)S(1)} %collective-permute-done.1.other_ref, ...), custom_call_target="tpu_custom_call" | custom-call | tf_op jit(solution)/shard_map/interior/pallas_call | solution.py:524
  6.9 0.0 collective-permute-done.recv_ref
  6.9 1.5 %collective-permute-done.2.recv_other = f32[12,8,256]{2,1,0:T(8,128)S(1)} collective-permute-done((f32[12,8,256]{2,1,0:T(8,128)S(1)}, f32[12,8,256]{2,1,0:T(8,128)S(1)}, u32[]{:S(2)}, u32[]{:S(2)}) %collective-permute-start.2) | collective-permute-done | bytes 98336 | tf_op jit(solution)/shard_map/ppermute | solution.py:490
  8.5 1.1 %edge.1 = (f32[3,8,128]{2,1,0:T(8,128)S(1)}, f32[26,8,128]{2,1,0:T(8,128)S(1)}, f32[5,2,8,128]{3,2,1,0:T(8,128)S(1)}) custom-call(f32[14,8,256]{2,1,0:T(8,128)S(1)} %collective-permute-done.recv_ref, f32[12,8,256]{2,1,0:T(8,128)S(1)} %collective-permute-done.2.recv_other, f32[14,8,256]{2,1,0:T(8,128)S(1)} %get-tuple-element.15.own_ref, ...), custom_call_target="tpu_custom_call" | custom-call | tf_op jit(solution)/shard_map/edge/pallas_call | solution.py:524
  9.5 0.1 collective-permute-start.5
  9.6 1.6 %collective-permute-start.3 = (f32[3,8,128]{2,1,0:T(8,128)S(1)}, f32[3,8,128]{2,1,0:T(8,128)S(1)}, u32[]{:S(2)}, u32[]{:S(2)}) collective-permute-start(f32[3,8,128]{2,1,0:T(8,128)S(1)} %get-tuple-element.21), channel_id=1, source_target_pairs={{0,2},{2,0},{1,3},{3,1},{4,6},{6,4},{5,7},{7,5},{8,10},{10,8},{9,1... | collective-permute-start | bytes 36872 | tf_op jit(solution)/shard_map/ppermute | solution.py:501
  11.2 0.3 %collective-permute-start.4 = (f32[3,8,128]{2,1,0:T(8,128)S(1)}, f32[3,8,128]{2,1,0:T(8,128)S(1)}, u32[]{:S(2)}, u32[]{:S(2)}) collective-permute-start(f32[3,8,128]{2,1,0:T(8,128)S(1)} %get-tuple-element.21), channel_id=1, source_target_pairs={{0,3},{3,0},{1,2},{2,1},{4,7},{7,4},{5,6},{6,5},{8,11},{11,8},{9,1... | collective-permute-start | bytes 36872 | tf_op jit(solution)/shard_map/ppermute | solution.py:507
  11.5 0.0 collective-permute-done.5.other_ref.refs_4_
  11.5 0.3 %base.1.refs_5_ = f32[4,16,256]{2,1,0:T(8,128)S(1)} custom-call(f32[5,8,8,128]{3,2,1,0:T(8,128)S(1)} %get-tuple-element.22.coarse_ref.refs_2_, f32[5,2,8,128]{3,2,1,0:T(8,128)S(1)} %get-tuple-element.23.outer_ref.refs_3_, f32[26,8,128]{2,1,0:T(8,128)S(1)} %get-tuple-element.24.share_ref, f32[26,8,128]{2,1,0:T(8,128)S(1)} %collective-permute-done.5.other_ref.refs_4_), custom_call_target="tpu_custom_call" | custom-call | tf_op jit(solution)/shard_map/base/pallas_call | solution.py:524
  11.8 1.6 %collective-permute-done.3.refs_0_ = f32[3,8,128]{2,1,0:T(8,128)S(1)} collective-permute-done((f32[3,8,128]{2,1,0:T(8,128)S(1)}, f32[3,8,128]{2,1,0:T(8,128)S(1)}, u32[]{:S(2)}, u32[]{:S(2)}) %collective-permute-start.3) | collective-permute-done | bytes 12320 | tf_op jit(solution)/shard_map/ppermute | solution.py:501
  13.4 0.9 %collective-permute-done.4.refs_1_ = f32[3,8,128]{2,1,0:T(8,128)S(1)} collective-permute-done((f32[3,8,128]{2,1,0:T(8,128)S(1)}, f32[3,8,128]{2,1,0:T(8,128)S(1)}, u32[]{:S(2)}, u32[]{:S(2)}) %collective-permute-start.4) | collective-permute-done | bytes 12320 | tf_op jit(solution)/shard_map/ppermute | solution.py:507
  14.3 0.9 %output.1 = f32[1,4,16,256]{3,2,1,0:T(8,128)} custom-call(f32[3,8,128]{2,1,0:T(8,128)S(1)} %collective-permute-done.3.refs_0_, f32[3,8,128]{2,1,0:T(8,128)S(1)} %collective-permute-done.4.refs_1_, f32[5,8,8,128]{3,2,1,0:T(8,128)S(1)} %get-tuple-element.22.coarse_ref.refs_2_, f32[5,2,8,128]{3,2,1,0:T(8,128)S(1)} %get-tuple-element.23.outer_ref.refs_3_, ...), custom_call_target="tpu_custom_call" | custom-call | tf_op jit(solution)/shard_map/output/pallas_call | solution.py:524
  (1 shorter events, 0.0 us)
Async XLA Ops:
  1.1 3.2 %collective-permute-start.1 = (f32[16,8,256]{2,1,0:T(8,128)S(1)}, f32[16,8,256]{2,1,0:T(8,128)S(1)}, u32[]{:S(2)}, u32[]{:S(2)}) collective-permute-start(f32[16,8,256]{2,1,0:T(8,128)S(1)} %get-tuple-element.16), channel_id=1, source_target_pairs={{0,1},{1,0},{2,3},{3,2},{4,5},{5,4},{6,7},{7,6},{8,9},{9,8},{10,11... | collective-permute-start | bytes 393224 | tf_op jit(solution)/shard_map/ppermute | solution.py:474
  1.7 5.3 %collective-permute-start = (f32[14,8,256]{2,1,0:T(8,128)S(1)}, f32[14,8,256]{2,1,0:T(8,128)S(1)}, u32[]{:S(2)}, u32[]{:S(2)}) collective-permute-start(f32[14,8,256]{2,1,0:T(8,128)S(1)} %get-tuple-element.15.own_ref), channel_id=1, source_target_pairs={{5,0},{0,5},{7,2},{2,7},{9,4},{4,9},{11,6},{6,11},{13,8},{8,13},{1... | collective-permute-start | bytes 344072 | tf_op jit(solution)/shard_map/ppermute | solution.py:490
  4.4 4.1 %collective-permute-start.2 = (f32[12,8,256]{2,1,0:T(8,128)S(1)}, f32[12,8,256]{2,1,0:T(8,128)S(1)}, u32[]{:S(2)}, u32[]{:S(2)}) collective-permute-start(f32[12,8,256]{2,1,0:T(8,128)S(1)} %slice.4), channel_id=1, source_target_pairs={{5,0},{0,5},{7,2},{2,7},{9,4},{4,9},{11,6},{6,11},{13,8},{8,13},{1... | collective-permute-start | bytes 294920 | tf_op jit(solution)/shard_map/ppermute | solution.py:490
  9.5 1.9 %collective-permute-start.5 = (f32[26,8,128]{2,1,0:T(8,128)S(1)}, f32[26,8,128]{2,1,0:T(8,128)S(1)}, u32[]{:S(2)}, u32[]{:S(2)}) collective-permute-start(f32[26,8,128]{2,1,0:T(8,128)S(1)} %get-tuple-element.24.share_ref), channel_id=1, source_target_pairs={{0,1},{1,0},{2,3},{3,2},{4,5},{5,4},{6,7},{7,6},{8,9},{9,8},{10,11... | collective-permute-start | bytes 319496 | tf_op jit(solution)/shard_map/ppermute | solution.py:474
  9.6 3.8 %collective-permute-start.3 = (f32[3,8,128]{2,1,0:T(8,128)S(1)}, f32[3,8,128]{2,1,0:T(8,128)S(1)}, u32[]{:S(2)}, u32[]{:S(2)}) collective-permute-start(f32[3,8,128]{2,1,0:T(8,128)S(1)} %get-tuple-element.21), channel_id=1, source_target_pairs={{0,2},{2,0},{1,3},{3,1},{4,6},{6,4},{5,7},{7,5},{8,10},{10,8},{9,1... | collective-permute-start | bytes 36872 | tf_op jit(solution)/shard_map/ppermute | solution.py:501
  11.2 3.1 %collective-permute-start.4 = (f32[3,8,128]{2,1,0:T(8,128)S(1)}, f32[3,8,128]{2,1,0:T(8,128)S(1)}, u32[]{:S(2)}, u32[]{:S(2)}) collective-permute-start(f32[3,8,128]{2,1,0:T(8,128)S(1)} %get-tuple-element.21), channel_id=1, source_target_pairs={{0,3},{3,0},{1,2},{2,1},{4,7},{7,4},{5,6},{6,5},{8,11},{11,8},{9,1... | collective-permute-start | bytes 36872 | tf_op jit(solution)/shard_map/ppermute | solution.py:507

commit v5 on v4

--- a/solution.py
+++ b/solution.py
@@ -125,10 +125,9 @@
     layers = v.shape[0]
     layer = iota(v.shape, 0)
     up, down = layers - layer_gap, layer_gap
-    from_up = jnp.where(layer < layers - layer_gap, pltpu.roll(v, up, 0) - v, 0.0)
-    from_down = jnp.where(layer >= layer_gap, pltpu.roll(v, down, 0) - v, 0.0)
-    z_gain = (k_thick + pltpu.roll(k_thick, up, 0)) * from_up
-    z_gain = z_gain + (k_thick + pltpu.roll(k_thick, down, 0)) * from_down
+    flow = (k_thick + pltpu.roll(k_thick, up, 0)) * (pltpu.roll(v, up, 0) - v)
+    flow = jnp.where(layer < layers - layer_gap, flow, 0.0)
+    z_gain = flow - pltpu.roll(flow, down, 0)
     return ((v + source) + (high - low)) + (z_gain + y_gain(v, k_plane, coefs_beside))
 
 
@@ -277,7 +276,6 @@
     table_ref,
     edge_ref,
     own_coef,
-    rest_ref,
     share_ref,
     coarse_ref,
     v_ref,
@@ -326,18 +324,19 @@
             mask,
         )
 
-    even = iota((layers, LANES), 0) % 2 == 0
-    restricted = []
-    for j in range(HALO - EDGE, HALO + half, 2):
-        restricted.append(0.125 * pair_sum(halves(state[j]) + halves(state[j + 1])))
-    for i in range(0, len(restricted), 2):
-        rest_ref[i // 2] = jnp.where(even, restricted[i], restricted[i + 1])
     for i in range(half):
         share_ref[2 * i] = state[HALO + i][:, :LANES]
         share_ref[2 * i + 1] = state[HALO + i][:, LANES:]
     for k in range(5):
         for i in range(COARSE_STEPS):
             share_ref[2 * half + k * COARSE_STEPS + i] = coarse_ref[k, i]
+    even = iota((layers, LANES), 0) % 2 == 0
+    restricted = []
+    for j in range(HALO - EDGE, HALO + half, 2):
+        restricted.append(0.125 * pair_sum(halves(state[j]) + halves(state[j + 1])))
+    first = share_ref.shape[0] - len(restricted) // 2
+    for i in range(0, len(restricted), 2):
+        share_ref[first + i // 2] = jnp.where(even, restricted[i], restricted[i + 1])
 
 
 def coarse_fields(coarse_ref, outer_ref, other_ref):
@@ -394,25 +393,28 @@
     ]
 
 
-def read_state(refs):
-    if len(refs) == 1:
-        return [refs[0][j] for j in range(refs[0].shape[0])]
-    mine, other = (sum((expand(ref[i]) for i in range(ref.shape[0])), []) for ref in refs)
+def read_state(state_ref, rows):
+    if state_ref.shape[0] == rows:
+        return [state_ref[j] for j in range(rows)]
+    count = state_ref.shape[0] // 2
+    mine, other = (
+        sum((expand(state_ref[i]) for i in range(at, at + count)), []) for at in (0, count)
+    )
     return mine + other[::-1]
 
 
-def unfold_kernel(mine_ref, other_ref, state_ref):
-    for j, row in enumerate(read_state((mine_ref, other_ref))):
+def unfold_kernel(halves_ref, state_ref):
+    for j, row in enumerate(read_state(halves_ref, state_ref.shape[0])):
         state_ref[j] = row
 
 
-def propagated(refs, state_refs=None):
+def propagated(refs, state_ref=None):
     field = coarse_fields(*refs)
     rows = refs[0].shape[1] + 2 * COARSE_STEPS
     state = [field(3, j) for j in range(rows)]
-    if state_refs:
+    if state_ref is not None:
         first = lax.axis_index("tm") == 0
-        state = [jnp.where(first, a, b) for a, b in zip(state, read_state(state_refs))]
+        state = [jnp.where(first, a, b) for a, b in zip(state, read_state(state_ref, rows))]
     return coarse_propagate(state, field, edge_factors(rows))
 
 
@@ -439,11 +441,10 @@
     pl.when(core == 1)(lambda: write(False))
 
 
-def output_kernel(*refs):
-    *state_refs, coarse_ref, outer_ref, other_ref, base_ref, out_ref = refs
+def output_kernel(state_ref, coarse_ref, outer_ref, other_ref, base_ref, out_ref):
     depth, width = base_ref.shape[:2]
     core = lax.axis_index("layer")
-    moved = propagated((coarse_ref, outer_ref, other_ref), state_refs)
+    moved = propagated((coarse_ref, outer_ref, other_ref), state_ref)
     half = iota(moved[0].shape, 1) // 2
 
     def write(mirror):
@@ -461,7 +462,7 @@
 def advance_kernel(state_ref, coarse_ref, outer_ref, share_ref, other_ref, next_ref):
     own = next_ref.shape[0]
     refs = (coarse_ref, outer_ref, other_ref)
-    moved, base = propagated(refs, (state_ref,)), propagated(refs)
+    moved, base = propagated(refs, state_ref), propagated(refs)
     for j in range(own):
         pair = []
         for i in (2 * j, 2 * j + 1):
@@ -567,13 +568,10 @@
         ],
         in_hbm=range(3, 7),
     )
-    rest, share, outer = call(
+    count = (half + EDGE) // 4
+    share, outer = call(
         edge_kernel,
-        (
-            slabs((half + EDGE) // 4),
-            slabs(2 * half + 5 * COARSE_STEPS),
-            slabs(5, COARSE_STEPS),
-        ),
+        (slabs(2 * half + 5 * COARSE_STEPS + count), slabs(5, COARSE_STEPS)),
         *(recv, recv_other, own, tables, levels, own_coef),
         name="edge",
         scratch=[
@@ -585,10 +583,8 @@
 
     slices = lax.axis_size("tm")
     position = lax.axis_index("tm")
-    state = [rest, rest]
-    if slices > 1:
-        state = [time_swap(rest, 0), cross_swap(rest)]
     other_share = layer_swap(share)
+    state = cross_swap(jnp.concatenate([other_share[-count:], share[-count:]], axis=0))
     base = call(
         base_kernel,
         jax.ShapeDtypeStruct((depth, width, length), f32),
@@ -597,22 +593,22 @@
     )
     if slices > 2:
         full = slabs(half + 2 * COARSE_STEPS)
-        state = [call(unfold_kernel, full, *state, name="unfold")]
+        state = call(unfold_kernel, full, state, name="unfold")
     for turn in range(1, slices - 1):
         ended = call(
             advance_kernel,
             slabs(half),
-            *(*state, coarse, outer, share, other_share),
+            *(state, coarse, outer, share, other_share),
             name="advance",
         )
         low = tile_swap(ended[:COARSE_STEPS])
         high = layer_swap(low)
         arrived = time_swap(jnp.concatenate([low[::-1], ended, high], axis=0), turn % 2)
-        state = [jnp.where(position == turn + 1, arrived, state[0])]
+        state = jnp.where(position == turn + 1, arrived, state)
     return call(
         output_kernel,
         jax.ShapeDtypeStruct((1, depth, width, length), f32),
-        *(*state, coarse, outer, other_share, base),
+        *(state, coarse, outer, other_share, base),
         name="output",
     )
 

time: 15.4 us -> 15.2 us (0.987)
  starting transfers between devices: 6.14 us -> 5.53 us
  waiting for transfers between devices: 4.02 us -> 4.56 us
    ppermute x1 -> x0, starting transfers between devices: 1.56 us -> none  [time_swap(): return lax.ppermute(value, ('tm', 'layer'), swap_pairs(pairs))]
    ppermute x1 -> x0, waiting for transfers between devices: 1.55 us -> none  [time_swap(): return lax.ppermute(value, ('tm', 'layer'), swap_pairs(pairs))]
    ppermute x2, waiting for transfers between devices: 0.01 us -> 1.31 us  [layer_swap(): return lax.ppermute(value, 'layer', [(0, 1), (1, 0)])]
    ppermute x1, starting transfers between devices: 0.31 us -> 1.25 us  [cross_swap(): return lax.ppermute(value, ('tm', 'layer'), swap_pairs(pairs))]
    ppermute x1, waiting for transfers between devices: 0.92 us -> 1.66 us  [cross_swap(): return lax.ppermute(value, ('tm', 'layer'), swap_pairs(pairs))]
  transfers between devices with their start and end apart: 6 -> 5, of which waited for: 3 -> 3; matrix products, arithmetic and copies ran while one was open for 0% -> 0% of each run, Pallas kernels for 12% -> 12%
where the time goes in v5:
time: 15.2 us; the launch traced here: 15 us
  starting transfers between devices  5.53 us (36%)
  Pallas kernels  4.88 us (32%)
  waiting for transfers between devices  4.56 us (30%)
    pallas_call x5, Pallas kernels, call(): pl.pallas_call(kernel, out_shape=out_shape, in_specs=[pl.BlockSpec(memory...  4.88 us
    ppermute x2, starting transfers between devices, tile_swap(): return lax.ppermute(value, ('tile', 'tm', 'layer'), swap_pairs(pairs))  3.69 us
    ppermute x1, waiting for transfers between devices, cross_swap(): return lax.ppermute(value, ('tm', 'layer'), swap_pairs(pairs))  1.66 us
    ppermute x2, waiting for transfers between devices, tile_swap(): return lax.ppermute(value, ('tile', 'tm', 'layer'), swap_pairs(pairs))  1.59 us
    ppermute x2, waiting for transfers between devices, layer_swap(): return lax.ppermute(value, 'layer', [(0, 1), (1, 0)])  1.31 us
    ppermute x1, starting transfers between devices, cross_swap(): return lax.ppermute(value, ('tm', 'layer'), swap_pairs(pairs))  1.25 us
    ppermute x2, starting transfers between devices, layer_swap(): return lax.ppermute(value, 'layer', [(0, 1), (1, 0)])  0.59 us
  transfers between devices with their start and end apart: 5, of which 3 were waited for; matrix products, arithmetic and copies ran while one was open for 0% of the time, Pallas kernels for 12%

profile of v5, /device:TPU:0, one launch (start us, length us, event | category | flops | bytes accessed | tf_op | source)
XLA Modules:
  0.0 15.0 jit_solution(4325732971883455531)
XLA Ops:
  0.0 1.1 %pack.1 = (f32[14,8,256]{2,1,0:T(8,128)S(1)}, f32[4,8,256]{2,1,0:T(8,128)S(1)}, f32[16,8,256]{2,1,0:T(8,128)S(1)}) custom-call(f32[4,16,256]{2,1,0:T(8,128)} %bitcast.2, s32[4,16,256]{2,1,0:T(8,128)} %zone_hbm.1, f32[16,256]{1,0:T(8,128)} %bitcast.3), custom_call_target="tpu_custom_call" | custom-call | tf_op jit(solution)/shard_map/pack/pallas_call | solution.py:525
  1.1 0.5 %collective-permute-start.1 = (f32[16,8,256]{2,1,0:T(8,128)S(1)}, f32[16,8,256]{2,1,0:T(8,128)S(1)}, u32[]{:S(2)}, u32[]{:S(2)}) collective-permute-start(f32[16,8,256]{2,1,0:T(8,128)S(1)} %get-tuple-element.15), channel_id=1, source_target_pairs={{0,1},{1,0},{2,3},{3,2},{4,5},{5,4},{6,7},{7,6},{8,9},{9,8},{10,11... | collective-permute-start | bytes 393224 | tf_op jit(solution)/shard_map/ppermute | solution.py:475
  1.7 2.7 %collective-permute-start = (f32[14,8,256]{2,1,0:T(8,128)S(1)}, f32[14,8,256]{2,1,0:T(8,128)S(1)}, u32[]{:S(2)}, u32[]{:S(2)}) collective-permute-start(f32[14,8,256]{2,1,0:T(8,128)S(1)} %get-tuple-element.14.own_ref), channel_id=1, source_target_pairs={{5,0},{0,5},{7,2},{2,7},{9,4},{4,9},{11,6},{6,11},{13,8},{8,13},{1... | collective-permute-start | bytes 344072 | tf_op jit(solution)/shard_map/ppermute | solution.py:491
  4.3 0.0 collective-permute-done.1.other_ref
  4.4 1.0 %collective-permute-start.2 = (f32[12,8,256]{2,1,0:T(8,128)S(1)}, f32[12,8,256]{2,1,0:T(8,128)S(1)}, u32[]{:S(2)}, u32[]{:S(2)}) collective-permute-start(f32[12,8,256]{2,1,0:T(8,128)S(1)} %slice.12), channel_id=1, source_target_pairs={{5,0},{0,5},{7,2},{2,7},{9,4},{4,9},{11,6},{6,11},{13,8},{8,13},{1... | collective-permute-start | bytes 294920 | tf_op jit(solution)/shard_map/ppermute | solution.py:491
  5.4 1.5 %interior.1 = (f32[8,2,8,256]{3,2,1,0:T(8,128)S(1)}, f32[6,9,8,256]{3,2,1,0:T(8,128)S(1)}, f32[5,8,8,128]{3,2,1,0:T(8,128)S(1)}, f32[3,128]{1,0:T(4,128)S(1)}) custom-call(f32[14,8,256]{2,1,0:T(8,128)S(1)} %get-tuple-element.14.own_ref, f32[4,8,256]{2,1,0:T(8,128)S(1)} %get-tuple-element.16.own_tail, f32[16,8,256]{2,1,0:T(8,128)S(1)} %collective-permute-done.1.other_ref, ...), custom_call_target="tpu_custom_call" | custom-call | tf_op jit(solution)/shard_map/interior/pallas_call | solution.py:525
  6.9 0.0 collective-permute-done.recv_ref
  6.9 1.6 %collective-permute-done.2.recv_other = f32[12,8,256]{2,1,0:T(8,128)S(1)} collective-permute-done((f32[12,8,256]{2,1,0:T(8,128)S(1)}, f32[12,8,256]{2,1,0:T(8,128)S(1)}, u32[]{:S(2)}, u32[]{:S(2)}) %collective-permute-start.2) | collective-permute-done | bytes 98336 | tf_op jit(solution)/shard_map/ppermute | solution.py:491
  8.5 1.0 %edge.1 = (f32[29,8,128]{2,1,0:T(8,128)S(1)}, f32[5,2,8,128]{3,2,1,0:T(8,128)S(1)}) custom-call(f32[14,8,256]{2,1,0:T(8,128)S(1)} %collective-permute-done.recv_ref, f32[12,8,256]{2,1,0:T(8,128)S(1)} %collective-permute-done.2.recv_other, f32[14,8,256]{2,1,0:T(8,128)S(1)} %get-tuple-element.14.own_ref, f32[3,128]{1,0:T(4,128)S(1)} %get-tuple-element.17.table_ref, ...), custom_call_target="tpu_custom_call" | custom-call | tf_op jit(solution)/shard_map/edge/pallas_call | solution.py:525
  9.5 0.1 collective-permute-start.3
  9.5 1.3 %collective-permute-done.3.other_ref = f32[29,8,128]{2,1,0:T(8,128)S(1)} collective-permute-done((f32[29,8,128]{2,1,0:T(8,128)S(1)}, f32[29,8,128]{2,1,0:T(8,128)S(1)}, u32[]{:S(2)}, u32[]{:S(2)}) %collective-permute-start.3) | collective-permute-done | bytes 118816 | tf_op jit(solution)/shard_map/ppermute | solution.py:475
  10.9 1.2 %collective-permute-start.4 = (f32[6,8,128]{2,1,0:T(8,128)S(1)}, f32[6,8,128]{2,1,0:T(8,128)S(1)}, u32[]{:S(2)}, u32[]{:S(2)}) collective-permute-start(f32[6,8,128]{2,1,0:T(8,128)S(1)} %pad_maximum_fusion), channel_id=1, source_target_pairs={{0,3},{3,0},{1,2},{2,1},{4,7},{7,4},{5,6},{6,5},{8,11},{11,8},{9,1... | collective-permute-start | bytes 73736 | tf_op jit(solution)/shard_map/ppermute | solution.py:508
  12.1 0.3 %base.1.base_ref = f32[4,16,256]{2,1,0:T(8,128)S(1)} custom-call(f32[5,8,8,128]{3,2,1,0:T(8,128)S(1)} %get-tuple-element.21.coarse_ref, f32[5,2,8,128]{3,2,1,0:T(8,128)S(1)} %get-tuple-element.22.outer_ref, f32[29,8,128]{2,1,0:T(8,128)S(1)} %get-tuple-element.20.share_ref, f32[29,8,128]{2,1,0:T(8,128)S(1)} %collective-permute-done.3.other_ref), custom_call_target="tpu_custom_call" | custom-call | tf_op jit(solution)/shard_map/base/pallas_call | solution.py:525
  12.4 1.7 %collective-permute-done.4.state_ref = f32[6,8,128]{2,1,0:T(8,128)S(1)} collective-permute-done((f32[6,8,128]{2,1,0:T(8,128)S(1)}, f32[6,8,128]{2,1,0:T(8,128)S(1)}, u32[]{:S(2)}, u32[]{:S(2)}) %collective-permute-start.4) | collective-permute-done | bytes 24608 | tf_op jit(solution)/shard_map/ppermute | solution.py:508
  14.1 0.9 %output.1 = f32[1,4,16,256]{3,2,1,0:T(8,128)} custom-call(f32[6,8,128]{2,1,0:T(8,128)S(1)} %collective-permute-done.4.state_ref, f32[5,8,8,128]{3,2,1,0:T(8,128)S(1)} %get-tuple-element.21.coarse_ref, f32[5,2,8,128]{3,2,1,0:T(8,128)S(1)} %get-tuple-element.22.outer_ref, f32[29,8,128]{2,1,0:T(8,128)S(1)} %collective-permute-done.3.other_ref, ...), custom_call_target="tpu_custom_call" | custom-call | tf_op jit(solution)/shard_map/output/pallas_call | solution.py:525
  (4 shorter events, 0.0 us)
Async XLA Ops:
  1.1 3.2 %collective-permute-start.1 = (f32[16,8,256]{2,1,0:T(8,128)S(1)}, f32[16,8,256]{2,1,0:T(8,128)S(1)}, u32[]{:S(2)}, u32[]{:S(2)}) collective-permute-start(f32[16,8,256]{2,1,0:T(8,128)S(1)} %get-tuple-element.15), channel_id=1, source_target_pairs={{0,1},{1,0},{2,3},{3,2},{4,5},{5,4},{6,7},{7,6},{8,9},{9,8},{10,11... | collective-permute-start | bytes 393224 | tf_op jit(solution)/shard_map/ppermute | solution.py:475
  1.7 5.2 %collective-permute-start = (f32[14,8,256]{2,1,0:T(8,128)S(1)}, f32[14,8,256]{2,1,0:T(8,128)S(1)}, u32[]{:S(2)}, u32[]{:S(2)}) collective-permute-start(f32[14,8,256]{2,1,0:T(8,128)S(1)} %get-tuple-element.14.own_ref), channel_id=1, source_target_pairs={{5,0},{0,5},{7,2},{2,7},{9,4},{4,9},{11,6},{6,11},{13,8},{8,13},{1... | collective-permute-start | bytes 344072 | tf_op jit(solution)/shard_map/ppermute | solution.py:491
  4.4 4.1 %collective-permute-start.2 = (f32[12,8,256]{2,1,0:T(8,128)S(1)}, f32[12,8,256]{2,1,0:T(8,128)S(1)}, u32[]{:S(2)}, u32[]{:S(2)}) collective-permute-start(f32[12,8,256]{2,1,0:T(8,128)S(1)} %slice.12), channel_id=1, source_target_pairs={{5,0},{0,5},{7,2},{2,7},{9,4},{4,9},{11,6},{6,11},{13,8},{8,13},{1... | collective-permute-start | bytes 294920 | tf_op jit(solution)/shard_map/ppermute | solution.py:491
  9.5 1.4 %collective-permute-start.3 = (f32[29,8,128]{2,1,0:T(8,128)S(1)}, f32[29,8,128]{2,1,0:T(8,128)S(1)}, u32[]{:S(2)}, u32[]{:S(2)}) collective-permute-start(f32[29,8,128]{2,1,0:T(8,128)S(1)} %get-tuple-element.20.share_ref), channel_id=1, source_target_pairs={{0,1},{1,0},{2,3},{3,2},{4,5},{5,4},{6,7},{7,6},{8,9},{9,8},{10,11... | collective-permute-start | bytes 356360 | tf_op jit(solution)/shard_map/ppermute | solution.py:475
  10.9 3.3 %collective-permute-start.4 = (f32[6,8,128]{2,1,0:T(8,128)S(1)}, f32[6,8,128]{2,1,0:T(8,128)S(1)}, u32[]{:S(2)}, u32[]{:S(2)}) collective-permute-start(f32[6,8,128]{2,1,0:T(8,128)S(1)} %pad_maximum_fusion), channel_id=1, source_target_pairs={{0,3},{3,0},{1,2},{2,1},{4,7},{7,4},{5,6},{6,5},{8,11},{11,8},{9,1... | collective-permute-start | bytes 73736 | tf_op jit(solution)/shard_map/ppermute | solution.py:508

commit v6 on v5

--- a/solution.py
+++ b/solution.py
@@ -55,8 +55,13 @@
 def pack_kernel(
     u_hbm, zone_hbm, flux_hbm, head_ref, tail_ref, turned_ref, u_ref, zone_ref, flux_ref, sems
 ):
-    copies = start_copies((u_hbm, zone_hbm, flux_hbm), (u_ref, zone_ref, flux_ref), sems)
     width = u_ref.shape[1]
+    parts = [
+        (source.at[:, pl.ds(row, 8)], target.at[:, pl.ds(row, 8)])
+        for row in range(0, width, 8)
+        for source, target in ((u_hbm, u_ref), (zone_hbm, zone_ref))
+    ]
+    copies = start_copies(*zip(*parts, (flux_hbm, flux_ref)), sems)
 
     def fill(mirror):
         for i in range(width):
@@ -276,6 +281,7 @@
     table_ref,
     edge_ref,
     own_coef,
+    rest_ref,
     share_ref,
     coarse_ref,
     v_ref,
@@ -334,9 +340,8 @@
     restricted = []
     for j in range(HALO - EDGE, HALO + half, 2):
         restricted.append(0.125 * pair_sum(halves(state[j]) + halves(state[j + 1])))
-    first = share_ref.shape[0] - len(restricted) // 2
     for i in range(0, len(restricted), 2):
-        share_ref[first + i // 2] = jnp.where(even, restricted[i], restricted[i + 1])
+        rest_ref[i // 2] = jnp.where(even, restricted[i], restricted[i + 1])
 
 
 def coarse_fields(coarse_ref, outer_ref, other_ref):
@@ -542,7 +547,7 @@
             pltpu.VMEM(u_own.shape, f32),
             pltpu.VMEM(zone_of_cell.shape, jnp.int32),
             pltpu.VMEM(flux.shape[1:], f32),
-            pltpu.SemaphoreType.DMA((3,)),
+            pltpu.SemaphoreType.DMA((2 * (width // 8) + 1,)),
         ],
         in_hbm=range(3),
     )
@@ -568,10 +573,13 @@
         ],
         in_hbm=range(3, 7),
     )
-    count = (half + EDGE) // 4
-    share, outer = call(
+    rest, share, outer = call(
         edge_kernel,
-        (slabs(2 * half + 5 * COARSE_STEPS + count), slabs(5, COARSE_STEPS)),
+        (
+            slabs((half + EDGE) // 4),
+            slabs(2 * half + 5 * COARSE_STEPS),
+            slabs(5, COARSE_STEPS),
+        ),
         *(recv, recv_other, own, tables, levels, own_coef),
         name="edge",
         scratch=[
@@ -583,8 +591,8 @@
 
     slices = lax.axis_size("tm")
     position = lax.axis_index("tm")
-    other_share = layer_swap(share)
-    state = cross_swap(jnp.concatenate([other_share[-count:], share[-count:]], axis=0))
+    other_rest, other_share = layer_swap(rest), layer_swap(share)
+    state = cross_swap(jnp.concatenate([other_rest, rest], axis=0))
     base = call(
         base_kernel,
         jax.ShapeDtypeStruct((depth, width, length), f32),

time: 15.2 us -> 15.1 us (level)
  waiting for transfers between devices: 4.56 us -> 3.91 us
  starting transfers between devices: 5.53 us -> 6.04 us
    ppermute x2 -> x3, waiting for transfers between devices: 1.31 us -> 0.67 us  [layer_swap(): return lax.ppermute(value, 'layer', [(0, 1), (1, 0)])]
    ppermute x2 -> x3, starting transfers between devices: 0.59 us -> 1.09 us  [layer_swap(): return lax.ppermute(value, 'layer', [(0, 1), (1, 0)])]
  transfers between devices with their start and end apart: 5 -> 6, of which waited for: 3 -> 3; matrix products, arithmetic and copies ran while one was open for 0% -> 0% of each run, Pallas kernels for 12% -> 12%
where the time goes in v6:
time: 15.1 us; the launch traced here: 14.8 us
  starting transfers between devices  6.04 us (40%)
  Pallas kernels  4.83 us (32%)
  waiting for transfers between devices  3.91 us (26%)
    pallas_call x5, Pallas kernels, call(): pl.pallas_call(kernel, out_shape=out_shape, in_specs=[pl.BlockSpec(memory...  4.83 us
    ppermute x2, starting transfers between devices, tile_swap(): return lax.ppermute(value, ('tile', 'tm', 'layer'), swap_pairs(pairs))  3.69 us
    ppermute x1, waiting for transfers between devices, cross_swap(): return lax.ppermute(value, ('tm', 'layer'), swap_pairs(pairs))  1.64 us
    ppermute x2, waiting for transfers between devices, tile_swap(): return lax.ppermute(value, ('tile', 'tm', 'layer'), swap_pairs(pairs))  1.59 us
    ppermute x1, starting transfers between devices, cross_swap(): return lax.ppermute(value, ('tm', 'layer'), swap_pairs(pairs))  1.26 us
    ppermute x3, starting transfers between devices, layer_swap(): return lax.ppermute(value, 'layer', [(0, 1), (1, 0)])  1.09 us
    ppermute x3, waiting for transfers between devices, layer_swap(): return lax.ppermute(value, 'layer', [(0, 1), (1, 0)])  0.67 us
  transfers between devices with their start and end apart: 6, of which 3 were waited for; matrix products, arithmetic and copies ran while one was open for 0% of the time, Pallas kernels for 12%

profile of v6, /device:TPU:0, one launch (start us, length us, event | category | flops | bytes accessed | tf_op | source)
XLA Modules:
  0.0 14.8 jit_solution(15389380511127196269)
XLA Ops:
  0.0 1.1 %pack.1 = (f32[14,8,256]{2,1,0:T(8,128)S(1)}, f32[4,8,256]{2,1,0:T(8,128)S(1)}, f32[16,8,256]{2,1,0:T(8,128)S(1)}) custom-call(f32[4,16,256]{2,1,0:T(8,128)} %bitcast.2, s32[4,16,256]{2,1,0:T(8,128)} %zone_hbm.1, f32[16,256]{1,0:T(8,128)} %bitcast.3), custom_call_target="tpu_custom_call" | custom-call | tf_op jit(solution)/shard_map/pack/pallas_call | solution.py:530
  1.1 0.5 %collective-permute-start.1 = (f32[16,8,256]{2,1,0:T(8,128)S(1)}, f32[16,8,256]{2,1,0:T(8,128)S(1)}, u32[]{:S(2)}, u32[]{:S(2)}) collective-permute-start(f32[16,8,256]{2,1,0:T(8,128)S(1)} %get-tuple-element.16), channel_id=1, source_target_pairs={{0,1},{1,0},{2,3},{3,2},{4,5},{5,4},{6,7},{7,6},{8,9},{9,8},{10,11... | collective-permute-start | bytes 393224 | tf_op jit(solution)/shard_map/ppermute | solution.py:480
  1.6 2.7 %collective-permute-start = (f32[14,8,256]{2,1,0:T(8,128)S(1)}, f32[14,8,256]{2,1,0:T(8,128)S(1)}, u32[]{:S(2)}, u32[]{:S(2)}) collective-permute-start(f32[14,8,256]{2,1,0:T(8,128)S(1)} %get-tuple-element.15.own_ref), channel_id=1, source_target_pairs={{5,0},{0,5},{7,2},{2,7},{9,4},{4,9},{11,6},{6,11},{13,8},{8,13},{1... | collective-permute-start | bytes 344072 | tf_op jit(solution)/shard_map/ppermute | solution.py:496
  4.3 0.0 collective-permute-done.1.other_ref
  4.3 1.0 %collective-permute-start.2 = (f32[12,8,256]{2,1,0:T(8,128)S(1)}, f32[12,8,256]{2,1,0:T(8,128)S(1)}, u32[]{:S(2)}, u32[]{:S(2)}) collective-permute-start(f32[12,8,256]{2,1,0:T(8,128)S(1)} %slice.4), channel_id=1, source_target_pairs={{5,0},{0,5},{7,2},{2,7},{9,4},{4,9},{11,6},{6,11},{13,8},{8,13},{1... | collective-permute-start | bytes 294920 | tf_op jit(solution)/shard_map/ppermute | solution.py:496
  5.3 1.5 %interior.1 = (f32[8,2,8,256]{3,2,1,0:T(8,128)S(1)}, f32[6,9,8,256]{3,2,1,0:T(8,128)S(1)}, f32[5,8,8,128]{3,2,1,0:T(8,128)S(1)}, f32[3,128]{1,0:T(4,128)S(1)}) custom-call(f32[14,8,256]{2,1,0:T(8,128)S(1)} %get-tuple-element.15.own_ref, f32[4,8,256]{2,1,0:T(8,128)S(1)} %get-tuple-element.17.own_tail, f32[16,8,256]{2,1,0:T(8,128)S(1)} %collective-permute-done.1.other_ref, ...), custom_call_target="tpu_custom_call" | custom-call | tf_op jit(solution)/shard_map/interior/pallas_call | solution.py:530
  6.8 0.0 collective-permute-done.recv_ref
  6.8 1.6 %collective-permute-done.2.recv_other = f32[12,8,256]{2,1,0:T(8,128)S(1)} collective-permute-done((f32[12,8,256]{2,1,0:T(8,128)S(1)}, f32[12,8,256]{2,1,0:T(8,128)S(1)}, u32[]{:S(2)}, u32[]{:S(2)}) %collective-permute-start.2) | collective-permute-done | bytes 98336 | tf_op jit(solution)/shard_map/ppermute | solution.py:496
  8.4 1.0 %edge.1 = (f32[3,8,128]{2,1,0:T(8,128)S(1)}, f32[26,8,128]{2,1,0:T(8,128)S(1)}, f32[5,2,8,128]{3,2,1,0:T(8,128)S(1)}) custom-call(f32[14,8,256]{2,1,0:T(8,128)S(1)} %collective-permute-done.recv_ref, f32[12,8,256]{2,1,0:T(8,128)S(1)} %collective-permute-done.2.recv_other, f32[14,8,256]{2,1,0:T(8,128)S(1)} %get-tuple-element.15.own_ref, ...), custom_call_target="tpu_custom_call" | custom-call | tf_op jit(solution)/shard_map/edge/pallas_call | solution.py:530
  9.4 0.1 collective-permute-start.3
  9.5 0.5 %collective-permute-start.5 = (f32[26,8,128]{2,1,0:T(8,128)S(1)}, f32[26,8,128]{2,1,0:T(8,128)S(1)}, u32[]{:S(2)}, u32[]{:S(2)}) collective-permute-start(f32[26,8,128]{2,1,0:T(8,128)S(1)} %get-tuple-element.24.share_ref), channel_id=1, source_target_pairs={{0,1},{1,0},{2,3},{3,2},{4,5},{5,4},{6,7},{7,6},{8,9},{9,8},{10,11... | collective-permute-start | bytes 319496 | tf_op jit(solution)/shard_map/ppermute | solution.py:480
  10.0 0.7 %collective-permute-done.3 = f32[3,8,128]{2,1,0:T(8,128)S(1)} collective-permute-done((f32[3,8,128]{2,1,0:T(8,128)S(1)}, f32[3,8,128]{2,1,0:T(8,128)S(1)}, u32[]{:S(2)}, u32[]{:S(2)}) %collective-permute-start.3) | collective-permute-done | bytes 12320 | tf_op jit(solution)/shard_map/ppermute | solution.py:480
  10.7 1.3 %collective-permute-start.4 = (f32[6,8,128]{2,1,0:T(8,128)S(1)}, f32[6,8,128]{2,1,0:T(8,128)S(1)}, u32[]{:S(2)}, u32[]{:S(2)}) collective-permute-start(f32[6,8,128]{2,1,0:T(8,128)S(1)} %pad_maximum_fusion), channel_id=1, source_target_pairs={{0,3},{3,0},{1,2},{2,1},{4,7},{7,4},{5,6},{6,5},{8,11},{11,8},{9,1... | collective-permute-start | bytes 73736 | tf_op jit(solution)/shard_map/ppermute | solution.py:513
  11.9 0.0 collective-permute-done.5.other_ref
  11.9 0.3 %base.1.base_ref = f32[4,16,256]{2,1,0:T(8,128)S(1)} custom-call(f32[5,8,8,128]{3,2,1,0:T(8,128)S(1)} %get-tuple-element.22.coarse_ref, f32[5,2,8,128]{3,2,1,0:T(8,128)S(1)} %get-tuple-element.23.outer_ref, f32[26,8,128]{2,1,0:T(8,128)S(1)} %get-tuple-element.24.share_ref, f32[26,8,128]{2,1,0:T(8,128)S(1)} %collective-permute-done.5.other_ref), custom_call_target="tpu_custom_call" | custom-call | tf_op jit(solution)/shard_map/base/pallas_call | solution.py:530
  12.3 1.6 %collective-permute-done.4.state_ref = f32[6,8,128]{2,1,0:T(8,128)S(1)} collective-permute-done((f32[6,8,128]{2,1,0:T(8,128)S(1)}, f32[6,8,128]{2,1,0:T(8,128)S(1)}, u32[]{:S(2)}, u32[]{:S(2)}) %collective-permute-start.4) | collective-permute-done | bytes 24608 | tf_op jit(solution)/shard_map/ppermute | solution.py:513
  13.9 0.9 %output.1 = f32[1,4,16,256]{3,2,1,0:T(8,128)} custom-call(f32[6,8,128]{2,1,0:T(8,128)S(1)} %collective-permute-done.4.state_ref, f32[5,8,8,128]{3,2,1,0:T(8,128)S(1)} %get-tuple-element.22.coarse_ref, f32[5,2,8,128]{3,2,1,0:T(8,128)S(1)} %get-tuple-element.23.outer_ref, f32[26,8,128]{2,1,0:T(8,128)S(1)} %collective-permute-done.5.other_ref, ...), custom_call_target="tpu_custom_call" | custom-call | tf_op jit(solution)/shard_map/output/pallas_call | solution.py:530
  (2 shorter events, 0.0 us)
Async XLA Ops:
  1.1 3.2 %collective-permute-start.1 = (f32[16,8,256]{2,1,0:T(8,128)S(1)}, f32[16,8,256]{2,1,0:T(8,128)S(1)}, u32[]{:S(2)}, u32[]{:S(2)}) collective-permute-start(f32[16,8,256]{2,1,0:T(8,128)S(1)} %get-tuple-element.16), channel_id=1, source_target_pairs={{0,1},{1,0},{2,3},{3,2},{4,5},{5,4},{6,7},{7,6},{8,9},{9,8},{10,11... | collective-permute-start | bytes 393224 | tf_op jit(solution)/shard_map/ppermute | solution.py:480
  1.6 5.2 %collective-permute-start = (f32[14,8,256]{2,1,0:T(8,128)S(1)}, f32[14,8,256]{2,1,0:T(8,128)S(1)}, u32[]{:S(2)}, u32[]{:S(2)}) collective-permute-start(f32[14,8,256]{2,1,0:T(8,128)S(1)} %get-tuple-element.15.own_ref), channel_id=1, source_target_pairs={{5,0},{0,5},{7,2},{2,7},{9,4},{4,9},{11,6},{6,11},{13,8},{8,13},{1... | collective-permute-start | bytes 344072 | tf_op jit(solution)/shard_map/ppermute | solution.py:496
  4.3 4.1 %collective-permute-start.2 = (f32[12,8,256]{2,1,0:T(8,128)S(1)}, f32[12,8,256]{2,1,0:T(8,128)S(1)}, u32[]{:S(2)}, u32[]{:S(2)}) collective-permute-start(f32[12,8,256]{2,1,0:T(8,128)S(1)} %slice.4), channel_id=1, source_target_pairs={{5,0},{0,5},{7,2},{2,7},{9,4},{4,9},{11,6},{6,11},{13,8},{8,13},{1... | collective-permute-start | bytes 294920 | tf_op jit(solution)/shard_map/ppermute | solution.py:496
  9.4 1.2 %collective-permute-start.3 = (f32[3,8,128]{2,1,0:T(8,128)S(1)}, f32[3,8,128]{2,1,0:T(8,128)S(1)}, u32[]{:S(2)}, u32[]{:S(2)}) collective-permute-start(f32[3,8,128]{2,1,0:T(8,128)S(1)} %get-tuple-element.21), channel_id=1, source_target_pairs={{0,1},{1,0},{2,3},{3,2},{4,5},{5,4},{6,7},{7,6},{8,9},{9,8},{10,11... | collective-permute-start | bytes 36872 | tf_op jit(solution)/shard_map/ppermute | solution.py:480
  9.5 2.4 %collective-permute-start.5 = (f32[26,8,128]{2,1,0:T(8,128)S(1)}, f32[26,8,128]{2,1,0:T(8,128)S(1)}, u32[]{:S(2)}, u32[]{:S(2)}) collective-permute-start(f32[26,8,128]{2,1,0:T(8,128)S(1)} %get-tuple-element.24.share_ref), channel_id=1, source_target_pairs={{0,1},{1,0},{2,3},{3,2},{4,5},{5,4},{6,7},{7,6},{8,9},{9,8},{10,11... | collective-permute-start | bytes 319496 | tf_op jit(solution)/shard_map/ppermute | solution.py:480
  10.7 3.3 %collective-permute-start.4 = (f32[6,8,128]{2,1,0:T(8,128)S(1)}, f32[6,8,128]{2,1,0:T(8,128)S(1)}, u32[]{:S(2)}, u32[]{:S(2)}) collective-permute-start(f32[6,8,128]{2,1,0:T(8,128)S(1)} %pad_maximum_fusion), channel_id=1, source_target_pairs={{0,3},{3,0},{1,2},{2,1},{4,7},{7,4},{5,6},{6,5},{8,11},{11,8},{9,1... | collective-permute-start | bytes 73736 | tf_op jit(solution)/shard_map/ppermute | solution.py:513

commit v7 on v6

--- a/solution.py
+++ b/solution.py
@@ -362,10 +362,11 @@
     flux = {j: field(4, j) for j in range(1, count - 1)}
     plane = [field(0, j) for j in range(count)]
     thick = [field(1, j) for j in range(count)]
-    soft = [field(2, j) for j in range(count)]
+    plane_slope = [field(2, j) * plane[j] for j in range(count)]
+    thick_slope = [field(2, j) * thick[j] for j in range(count)]
     for step in range(1, COARSE_STEPS + 1):
         k_plane = {
-            j: plane[j] * (1.0 + soft[j] * state[j]) for j in range(step - 1, count - step + 1)
+            j: plane[j] + plane_slope[j] * state[j] for j in range(step - 1, count - step + 1)
         }
         flows = {}
         for j in range(step - 1, count - step):
@@ -373,7 +374,7 @@
             flows[j] = flow * masks[j] if j in masks else flow
         fresh = list(state)
         for j in range(step, count - step):
-            k_thick = thick[j] * (1.0 + soft[j] * state[j])
+            k_thick = thick[j] + thick_slope[j] * state[j]
             fresh[j] = step_row(
                 state[j], flows[j - 1], flows[j], k_plane[j], k_thick, flux[j], coarse_y, 2
             )

time: 15.1 us -> 15.1 us (level)
  no operation moved by 1% of the time
where the time goes in v7:
time: 15.1 us; the launch traced here: 14.8 us
  starting transfers between devices  6.04 us (40%)
  Pallas kernels  4.83 us (32%)
  waiting for transfers between devices  3.9 us (26%)
    pallas_call x5, Pallas kernels, call(): pl.pallas_call(kernel, out_shape=out_shape, in_specs=[pl.BlockSpec(memory...  4.83 us
    ppermute x2, starting transfers between devices, tile_swap(): return lax.ppermute(value, ('tile', 'tm', 'layer'), swap_pairs(pairs))  3.69 us
    ppermute x1, waiting for transfers between devices, cross_swap(): return lax.ppermute(value, ('tm', 'layer'), swap_pairs(pairs))  1.64 us
    ppermute x2, waiting for transfers between devices, tile_swap(): return lax.ppermute(value, ('tile', 'tm', 'layer'), swap_pairs(pairs))  1.59 us
    ppermute x1, starting transfers between devices, cross_swap(): return lax.ppermute(value, ('tm', 'layer'), swap_pairs(pairs))  1.26 us
    ppermute x3, starting transfers between devices, layer_swap(): return lax.ppermute(value, 'layer', [(0, 1), (1, 0)])  1.09 us
    ppermute x3, waiting for transfers between devices, layer_swap(): return lax.ppermute(value, 'layer', [(0, 1), (1, 0)])  0.67 us
  transfers between devices with their start and end apart: 6, of which 3 were waited for; matrix products, arithmetic and copies ran while one was open for 0% of the time, Pallas kernels for 12%

profile of v7, /device:TPU:0, one launch (start us, length us, event | category | flops | bytes accessed | tf_op | source)
XLA Modules:
  0.0 14.8 jit_solution(1647383394880610242)
XLA Ops:
  0.0 1.1 %pack.1 = (f32[14,8,256]{2,1,0:T(8,128)S(1)}, f32[4,8,256]{2,1,0:T(8,128)S(1)}, f32[16,8,256]{2,1,0:T(8,128)S(1)}) custom-call(f32[4,16,256]{2,1,0:T(8,128)} %bitcast.2, s32[4,16,256]{2,1,0:T(8,128)} %zone_hbm.1, f32[16,256]{1,0:T(8,128)} %bitcast.3), custom_call_target="tpu_custom_call" | custom-call | tf_op jit(solution)/shard_map/pack/pallas_call | solution.py:531
  1.1 0.5 %collective-permute-start.1 = (f32[16,8,256]{2,1,0:T(8,128)S(1)}, f32[16,8,256]{2,1,0:T(8,128)S(1)}, u32[]{:S(2)}, u32[]{:S(2)}) collective-permute-start(f32[16,8,256]{2,1,0:T(8,128)S(1)} %get-tuple-element.16), channel_id=1, source_target_pairs={{0,1},{1,0},{2,3},{3,2},{4,5},{5,4},{6,7},{7,6},{8,9},{9,8},{10,11... | collective-permute-start | bytes 393224 | tf_op jit(solution)/shard_map/ppermute | solution.py:481
  1.6 2.7 %collective-permute-start = (f32[14,8,256]{2,1,0:T(8,128)S(1)}, f32[14,8,256]{2,1,0:T(8,128)S(1)}, u32[]{:S(2)}, u32[]{:S(2)}) collective-permute-start(f32[14,8,256]{2,1,0:T(8,128)S(1)} %get-tuple-element.15.own_ref), channel_id=1, source_target_pairs={{5,0},{0,5},{7,2},{2,7},{9,4},{4,9},{11,6},{6,11},{13,8},{8,13},{1... | collective-permute-start | bytes 344072 | tf_op jit(solution)/shard_map/ppermute | solution.py:497
  4.3 0.0 collective-permute-done.1.other_ref
  4.3 1.0 %collective-permute-start.2 = (f32[12,8,256]{2,1,0:T(8,128)S(1)}, f32[12,8,256]{2,1,0:T(8,128)S(1)}, u32[]{:S(2)}, u32[]{:S(2)}) collective-permute-start(f32[12,8,256]{2,1,0:T(8,128)S(1)} %slice.4), channel_id=1, source_target_pairs={{5,0},{0,5},{7,2},{2,7},{9,4},{4,9},{11,6},{6,11},{13,8},{8,13},{1... | collective-permute-start | bytes 294920 | tf_op jit(solution)/shard_map/ppermute | solution.py:497
  5.3 1.5 %interior.1 = (f32[8,2,8,256]{3,2,1,0:T(8,128)S(1)}, f32[6,9,8,256]{3,2,1,0:T(8,128)S(1)}, f32[5,8,8,128]{3,2,1,0:T(8,128)S(1)}, f32[3,128]{1,0:T(4,128)S(1)}) custom-call(f32[14,8,256]{2,1,0:T(8,128)S(1)} %get-tuple-element.15.own_ref, f32[4,8,256]{2,1,0:T(8,128)S(1)} %get-tuple-element.17.own_tail, f32[16,8,256]{2,1,0:T(8,128)S(1)} %collective-permute-done.1.other_ref, ...), custom_call_target="tpu_custom_call" | custom-call | tf_op jit(solution)/shard_map/interior/pallas_call | solution.py:531
  6.8 0.0 collective-permute-done.recv_ref
  6.8 1.6 %collective-permute-done.2.recv_other = f32[12,8,256]{2,1,0:T(8,128)S(1)} collective-permute-done((f32[12,8,256]{2,1,0:T(8,128)S(1)}, f32[12,8,256]{2,1,0:T(8,128)S(1)}, u32[]{:S(2)}, u32[]{:S(2)}) %collective-permute-start.2) | collective-permute-done | bytes 98336 | tf_op jit(solution)/shard_map/ppermute | solution.py:497
  8.4 1.0 %edge.1 = (f32[3,8,128]{2,1,0:T(8,128)S(1)}, f32[26,8,128]{2,1,0:T(8,128)S(1)}, f32[5,2,8,128]{3,2,1,0:T(8,128)S(1)}) custom-call(f32[14,8,256]{2,1,0:T(8,128)S(1)} %collective-permute-done.recv_ref, f32[12,8,256]{2,1,0:T(8,128)S(1)} %collective-permute-done.2.recv_other, f32[14,8,256]{2,1,0:T(8,128)S(1)} %get-tuple-element.15.own_ref, ...), custom_call_target="tpu_custom_call" | custom-call | tf_op jit(solution)/shard_map/edge/pallas_call | solution.py:531
  9.4 0.1 collective-permute-start.3
  9.5 0.5 %collective-permute-start.5 = (f32[26,8,128]{2,1,0:T(8,128)S(1)}, f32[26,8,128]{2,1,0:T(8,128)S(1)}, u32[]{:S(2)}, u32[]{:S(2)}) collective-permute-start(f32[26,8,128]{2,1,0:T(8,128)S(1)} %get-tuple-element.24.share_ref), channel_id=1, source_target_pairs={{0,1},{1,0},{2,3},{3,2},{4,5},{5,4},{6,7},{7,6},{8,9},{9,8},{10,11... | collective-permute-start | bytes 319496 | tf_op jit(solution)/shard_map/ppermute | solution.py:481
  10.0 0.7 %collective-permute-done.3 = f32[3,8,128]{2,1,0:T(8,128)S(1)} collective-permute-done((f32[3,8,128]{2,1,0:T(8,128)S(1)}, f32[3,8,128]{2,1,0:T(8,128)S(1)}, u32[]{:S(2)}, u32[]{:S(2)}) %collective-permute-start.3) | collective-permute-done | bytes 12320 | tf_op jit(solution)/shard_map/ppermute | solution.py:481
  10.7 1.3 %collective-permute-start.4 = (f32[6,8,128]{2,1,0:T(8,128)S(1)}, f32[6,8,128]{2,1,0:T(8,128)S(1)}, u32[]{:S(2)}, u32[]{:S(2)}) collective-permute-start(f32[6,8,128]{2,1,0:T(8,128)S(1)} %pad_maximum_fusion), channel_id=1, source_target_pairs={{0,3},{3,0},{1,2},{2,1},{4,7},{7,4},{5,6},{6,5},{8,11},{11,8},{9,1... | collective-permute-start | bytes 73736 | tf_op jit(solution)/shard_map/ppermute | solution.py:514
  11.9 0.0 collective-permute-done.5.other_ref
  11.9 0.3 %base.1.base_ref = f32[4,16,256]{2,1,0:T(8,128)S(1)} custom-call(f32[5,8,8,128]{3,2,1,0:T(8,128)S(1)} %get-tuple-element.22.coarse_ref, f32[5,2,8,128]{3,2,1,0:T(8,128)S(1)} %get-tuple-element.23.outer_ref, f32[26,8,128]{2,1,0:T(8,128)S(1)} %get-tuple-element.24.share_ref, f32[26,8,128]{2,1,0:T(8,128)S(1)} %collective-permute-done.5.other_ref), custom_call_target="tpu_custom_call" | custom-call | tf_op jit(solution)/shard_map/base/pallas_call | solution.py:531
  12.3 1.6 %collective-permute-done.4.state_ref = f32[6,8,128]{2,1,0:T(8,128)S(1)} collective-permute-done((f32[6,8,128]{2,1,0:T(8,128)S(1)}, f32[6,8,128]{2,1,0:T(8,128)S(1)}, u32[]{:S(2)}, u32[]{:S(2)}) %collective-permute-start.4) | collective-permute-done | bytes 24608 | tf_op jit(solution)/shard_map/ppermute | solution.py:514
  13.9 0.9 %output.1 = f32[1,4,16,256]{3,2,1,0:T(8,128)} custom-call(f32[6,8,128]{2,1,0:T(8,128)S(1)} %collective-permute-done.4.state_ref, f32[5,8,8,128]{3,2,1,0:T(8,128)S(1)} %get-tuple-element.22.coarse_ref, f32[5,2,8,128]{3,2,1,0:T(8,128)S(1)} %get-tuple-element.23.outer_ref, f32[26,8,128]{2,1,0:T(8,128)S(1)} %collective-permute-done.5.other_ref, ...), custom_call_target="tpu_custom_call" | custom-call | tf_op jit(solution)/shard_map/output/pallas_call | solution.py:531
  (2 shorter events, 0.0 us)
Async XLA Ops:
  1.1 3.2 %collective-permute-start.1 = (f32[16,8,256]{2,1,0:T(8,128)S(1)}, f32[16,8,256]{2,1,0:T(8,128)S(1)}, u32[]{:S(2)}, u32[]{:S(2)}) collective-permute-start(f32[16,8,256]{2,1,0:T(8,128)S(1)} %get-tuple-element.16), channel_id=1, source_target_pairs={{0,1},{1,0},{2,3},{3,2},{4,5},{5,4},{6,7},{7,6},{8,9},{9,8},{10,11... | collective-permute-start | bytes 393224 | tf_op jit(solution)/shard_map/ppermute | solution.py:481
  1.6 5.2 %collective-permute-start = (f32[14,8,256]{2,1,0:T(8,128)S(1)}, f32[14,8,256]{2,1,0:T(8,128)S(1)}, u32[]{:S(2)}, u32[]{:S(2)}) collective-permute-start(f32[14,8,256]{2,1,0:T(8,128)S(1)} %get-tuple-element.15.own_ref), channel_id=1, source_target_pairs={{5,0},{0,5},{7,2},{2,7},{9,4},{4,9},{11,6},{6,11},{13,8},{8,13},{1... | collective-permute-start | bytes 344072 | tf_op jit(solution)/shard_map/ppermute | solution.py:497
  4.3 4.1 %collective-permute-start.2 = (f32[12,8,256]{2,1,0:T(8,128)S(1)}, f32[12,8,256]{2,1,0:T(8,128)S(1)}, u32[]{:S(2)}, u32[]{:S(2)}) collective-permute-start(f32[12,8,256]{2,1,0:T(8,128)S(1)} %slice.4), channel_id=1, source_target_pairs={{5,0},{0,5},{7,2},{2,7},{9,4},{4,9},{11,6},{6,11},{13,8},{8,13},{1... | collective-permute-start | bytes 294920 | tf_op jit(solution)/shard_map/ppermute | solution.py:497
  9.4 1.2 %collective-permute-start.3 = (f32[3,8,128]{2,1,0:T(8,128)S(1)}, f32[3,8,128]{2,1,0:T(8,128)S(1)}, u32[]{:S(2)}, u32[]{:S(2)}) collective-permute-start(f32[3,8,128]{2,1,0:T(8,128)S(1)} %get-tuple-element.21), channel_id=1, source_target_pairs={{0,1},{1,0},{2,3},{3,2},{4,5},{5,4},{6,7},{7,6},{8,9},{9,8},{10,11... | collective-permute-start | bytes 36872 | tf_op jit(solution)/shard_map/ppermute | solution.py:481
  9.5 2.4 %collective-permute-start.5 = (f32[26,8,128]{2,1,0:T(8,128)S(1)}, f32[26,8,128]{2,1,0:T(8,128)S(1)}, u32[]{:S(2)}, u32[]{:S(2)}) collective-permute-start(f32[26,8,128]{2,1,0:T(8,128)S(1)} %get-tuple-element.24.share_ref), channel_id=1, source_target_pairs={{0,1},{1,0},{2,3},{3,2},{4,5},{5,4},{6,7},{7,6},{8,9},{9,8},{10,11... | collective-permute-start | bytes 319496 | tf_op jit(solution)/shard_map/ppermute | solution.py:481
  10.7 3.3 %collective-permute-start.4 = (f32[6,8,128]{2,1,0:T(8,128)S(1)}, f32[6,8,128]{2,1,0:T(8,128)S(1)}, u32[]{:S(2)}, u32[]{:S(2)}) collective-permute-start(f32[6,8,128]{2,1,0:T(8,128)S(1)} %pad_maximum_fusion), channel_id=1, source_target_pairs={{0,3},{3,0},{1,2},{2,1},{4,7},{7,4},{5,6},{6,5},{8,11},{11,8},{9,1... | collective-permute-start | bytes 73736 | tf_op jit(solution)/shard_map/ppermute | solution.py:514

commit v8 on v7

--- a/solution.py
+++ b/solution.py
@@ -53,7 +53,7 @@
 
 
 def pack_kernel(
-    u_hbm, zone_hbm, flux_hbm, head_ref, tail_ref, turned_ref, u_ref, zone_ref, flux_ref, sems
+    u_hbm, zone_hbm, flux_hbm, head_ref, tail_ref, turned_head, turned_tail, u_ref, zone_ref, flux_ref, sems
 ):
     width = u_ref.shape[1]
     parts = [
@@ -70,7 +70,11 @@
                 [u_ref[:, row, :], zone_ref[:, row, :].astype(jnp.float32)], axis=0
             )
             slab = split_lanes(slab)
-            turned_ref[width - 1 - i] = slab
+            at = width - 1 - i
+            if at < HALO:
+                turned_head[at] = slab
+            else:
+                turned_tail[at - HALO] = slab
             if i < HALO:
                 head_ref[i] = slab
             else:
@@ -218,6 +222,7 @@
     own_ref,
     own_tail,
     other_ref,
+    other_tail,
     row_hbm,
     plane_hbm,
     thick_hbm,
@@ -246,7 +251,10 @@
     def gather():
         rows = []
         for i in range(width):
-            a, b = own_ref[i] if i < HALO else own_tail[i - HALO], other_ref[i]
+            a, b = (
+                head[i] if i < HALO else tail[i - HALO]
+                for head, tail in ((own_ref, own_tail), (other_ref, other_tail))
+            )
             v, zone = join_layers(jnp.where(first, a, b), jnp.where(first, b, a))
             coefs = look_up(table_ref, zone)
             v_ref[i] = v
@@ -539,9 +547,9 @@
         )(*operands)
 
     u_own = u_start[0]
-    own, own_tail, turned = call(
+    own, own_tail, turned, turned_tail = call(
         pack_kernel,
-        (wide(HALO + width // 8), wide(width - HALO), wide(width)),
+        (wide(HALO + width // 8), wide(width - HALO), wide(HALO), wide(width - HALO)),
         *(u_own, zone_of_cell, flux[0]),
         name="pack",
         scratch=[
@@ -552,8 +560,8 @@
         ],
         in_hbm=range(3),
     )
-    other = layer_swap(turned)
-    recv, recv_other = tile_swap(own), tile_swap(other[:HALO])
+    other, other_tail = layer_swap(turned), layer_swap(turned_tail)
+    recv, recv_other = tile_swap(own), tile_swap(other)
 
     levels, own_coef, coarse, tables = call(
         interior_kernel,
@@ -563,7 +571,7 @@
             slabs(5, half),
             jax.ShapeDtypeStruct((3, LANES), f32),
         ),
-        *(own, own_tail, other, zone_row, plane_rate, thick_rate, soften),
+        *(own, own_tail, other, other_tail, zone_row, plane_rate, thick_rate, soften),
         name="interior",
         scratch=[
             pltpu.VMEM((width, layers, length), f32),
@@ -572,7 +580,7 @@
             *[pltpu.SMEM(plane_rate.shape, f32)] * 3,
             pltpu.SemaphoreType.DMA((4,)),
         ],
-        in_hbm=range(3, 7),
+        in_hbm=range(4, 8),
     )
     rest, share, outer = call(
         edge_kernel,

time: 15.1 us -> 15 us (level)
    ppermute x2, waiting for transfers between devices: 1.59 us -> 0.38 us  [tile_swap(): return lax.ppermute(value, ('tile', 'tm', 'layer'), swap_pairs(pairs))]
    ppermute x3 -> x4, waiting for transfers between devices: 0.67 us -> 1.85 us  [layer_swap(): return lax.ppermute(value, 'layer', [(0, 1), (1, 0)])]
    ppermute x3 -> x4, starting transfers between devices: 1.09 us -> 1.12 us  [layer_swap(): return lax.ppermute(value, 'layer', [(0, 1), (1, 0)])]
  transfers between devices with their start and end apart: 6 -> 7, of which waited for: 3 -> 4; matrix products, arithmetic and copies ran while one was open for 0% -> 0% of each run, Pallas kernels for 12% -> 12%
where the time goes in v8:
time: 15 us; the launch traced here: 14.8 us
  starting transfers between devices  6 us (40%)
  Pallas kernels  4.83 us (32%)
  waiting for transfers between devices  3.87 us (26%)
    pallas_call x5, Pallas kernels, call(): pl.pallas_call(kernel, out_shape=out_shape, in_specs=[pl.BlockSpec(memory...  4.83 us
    ppermute x2, starting transfers between devices, tile_swap(): return lax.ppermute(value, ('tile', 'tm', 'layer'), swap_pairs(pairs))  3.63 us
    ppermute x4, waiting for transfers between devices, layer_swap(): return lax.ppermute(value, 'layer', [(0, 1), (1, 0)])  1.85 us
    ppermute x1, waiting for transfers between devices, cross_swap(): return lax.ppermute(value, ('tm', 'layer'), swap_pairs(pairs))  1.64 us
    ppermute x1, starting transfers between devices, cross_swap(): return lax.ppermute(value, ('tm', 'layer'), swap_pairs(pairs))  1.26 us
    ppermute x4, starting transfers between devices, layer_swap(): return lax.ppermute(value, 'layer', [(0, 1), (1, 0)])  1.12 us
    ppermute x2, waiting for transfers between devices, tile_swap(): return lax.ppermute(value, ('tile', 'tm', 'layer'), swap_pairs(pairs))  0.38 us
  transfers between devices with their start and end apart: 7, of which 4 were waited for; matrix products, arithmetic and copies ran while one was open for 0% of the time, Pallas kernels for 12%

profile of v8, /device:TPU:0, one launch (start us, length us, event | category | flops | bytes accessed | tf_op | source)
XLA Modules:
  0.0 14.8 jit_solution(15359736597024734785)
XLA Ops:
  0.0 1.1 %pack.1 = (f32[14,8,256]{2,1,0:T(8,128)S(1)}, f32[4,8,256]{2,1,0:T(8,128)S(1)}, f32[12,8,256]{2,1,0:T(8,128)S(1)}, f32[4,8,256]{2,1,0:T(8,128)S(1)}) custom-call(f32[4,16,256]{2,1,0:T(8,128)} %bitcast.2, s32[4,16,256]{2,1,0:T(8,128)} %zone_hbm.1, f32[16,256]{1,0:T(8,128)} %bitcast.3), custom_call_target="tpu_custom_call" | custom-call | tf_op jit(solution)/shard_map/pack/pallas_call | solution.py:539
  1.1 0.5 %collective-permute-start.1 = (f32[12,8,256]{2,1,0:T(8,128)S(1)}, f32[12,8,256]{2,1,0:T(8,128)S(1)}, u32[]{:S(2)}, u32[]{:S(2)}) collective-permute-start(f32[12,8,256]{2,1,0:T(8,128)S(1)} %get-tuple-element.17), channel_id=1, source_target_pairs={{0,1},{1,0},{2,3},{3,2},{4,5},{5,4},{6,7},{7,6},{8,9},{9,8},{10,11... | collective-permute-start | bytes 294920 | tf_op jit(solution)/shard_map/ppermute | solution.py:489
  1.6 2.7 %collective-permute-start = (f32[14,8,256]{2,1,0:T(8,128)S(1)}, f32[14,8,256]{2,1,0:T(8,128)S(1)}, u32[]{:S(2)}, u32[]{:S(2)}) collective-permute-start(f32[14,8,256]{2,1,0:T(8,128)S(1)} %get-tuple-element.16.own_ref), channel_id=1, source_target_pairs={{5,0},{0,5},{7,2},{2,7},{9,4},{4,9},{11,6},{6,11},{13,8},{8,13},{1... | collective-permute-start | bytes 344072 | tf_op jit(solution)/shard_map/ppermute | solution.py:505
  4.3 0.0 collective-permute-done.1.other_ref
  4.3 0.9 %collective-permute-start.2 = (f32[12,8,256]{2,1,0:T(8,128)S(1)}, f32[12,8,256]{2,1,0:T(8,128)S(1)}, u32[]{:S(2)}, u32[]{:S(2)}) collective-permute-start(f32[12,8,256]{2,1,0:T(8,128)S(1)} %collective-permute-done.1.other_ref), channel_id=1, source_target_pairs={{5,0},{0,5},{7,2},{2,7},{9,4},{4,9},{11,6},{6,11},{13,8},{8,13},{1... | collective-permute-start | bytes 294920 | tf_op jit(solution)/shard_map/ppermute | solution.py:505
  5.2 0.0 collective-permute-start.3
  5.3 1.2 %collective-permute-done.3.other_tail = f32[4,8,256]{2,1,0:T(8,128)S(1)} collective-permute-done((f32[4,8,256]{2,1,0:T(8,128)S(1)}, f32[4,8,256]{2,1,0:T(8,128)S(1)}, u32[]{:S(2)}, u32[]{:S(2)}) %collective-permute-start.3) | collective-permute-done | bytes 32800 | tf_op jit(solution)/shard_map/ppermute | solution.py:489
  6.4 1.5 %interior.1 = (f32[8,2,8,256]{3,2,1,0:T(8,128)S(1)}, f32[6,9,8,256]{3,2,1,0:T(8,128)S(1)}, f32[5,8,8,128]{3,2,1,0:T(8,128)S(1)}, f32[3,128]{1,0:T(4,128)S(1)}) custom-call(f32[14,8,256]{2,1,0:T(8,128)S(1)} %get-tuple-element.16.own_ref, f32[4,8,256]{2,1,0:T(8,128)S(1)} %get-tuple-element.18.own_tail, f32[12,8,256]{2,1,0:T(8,128)S(1)} %collective-permute-done.1.other_ref, ...), custom_call_target="tpu_custom_call" | custom-call | tf_op jit(solution)/shard_map/interior/pallas_call | solution.py:539
  8.0 0.0 collective-permute-done.recv_ref
  8.0 0.4 %collective-permute-done.2.recv_other = f32[12,8,256]{2,1,0:T(8,128)S(1)} collective-permute-done((f32[12,8,256]{2,1,0:T(8,128)S(1)}, f32[12,8,256]{2,1,0:T(8,128)S(1)}, u32[]{:S(2)}, u32[]{:S(2)}) %collective-permute-start.2) | collective-permute-done | bytes 98336 | tf_op jit(solution)/shard_map/ppermute | solution.py:505
  8.3 1.0 %edge.1 = (f32[3,8,128]{2,1,0:T(8,128)S(1)}, f32[26,8,128]{2,1,0:T(8,128)S(1)}, f32[5,2,8,128]{3,2,1,0:T(8,128)S(1)}) custom-call(f32[14,8,256]{2,1,0:T(8,128)S(1)} %collective-permute-done.recv_ref, f32[12,8,256]{2,1,0:T(8,128)S(1)} %collective-permute-done.2.recv_other, f32[14,8,256]{2,1,0:T(8,128)S(1)} %get-tuple-element.16.own_ref, ...), custom_call_target="tpu_custom_call" | custom-call | tf_op jit(solution)/shard_map/edge/pallas_call | solution.py:539
  9.3 0.1 collective-permute-start.4
  9.4 0.5 %collective-permute-start.6 = (f32[26,8,128]{2,1,0:T(8,128)S(1)}, f32[26,8,128]{2,1,0:T(8,128)S(1)}, u32[]{:S(2)}, u32[]{:S(2)}) collective-permute-start(f32[26,8,128]{2,1,0:T(8,128)S(1)} %get-tuple-element.26.share_ref), channel_id=1, source_target_pairs={{0,1},{1,0},{2,3},{3,2},{4,5},{5,4},{6,7},{7,6},{8,9},{9,8},{10,11... | collective-permute-start | bytes 319496 | tf_op jit(solution)/shard_map/ppermute | solution.py:489
  9.9 0.7 %collective-permute-done.4 = f32[3,8,128]{2,1,0:T(8,128)S(1)} collective-permute-done((f32[3,8,128]{2,1,0:T(8,128)S(1)}, f32[3,8,128]{2,1,0:T(8,128)S(1)}, u32[]{:S(2)}, u32[]{:S(2)}) %collective-permute-start.4) | collective-permute-done | bytes 12320 | tf_op jit(solution)/shard_map/ppermute | solution.py:489
  10.6 1.3 %collective-permute-start.5 = (f32[6,8,128]{2,1,0:T(8,128)S(1)}, f32[6,8,128]{2,1,0:T(8,128)S(1)}, u32[]{:S(2)}, u32[]{:S(2)}) collective-permute-start(f32[6,8,128]{2,1,0:T(8,128)S(1)} %pad_maximum_fusion), channel_id=1, source_target_pairs={{0,3},{3,0},{1,2},{2,1},{4,7},{7,4},{5,6},{6,5},{8,11},{11,8},{9,1... | collective-permute-start | bytes 73736 | tf_op jit(solution)/shard_map/ppermute | solution.py:522
  11.8 0.0 collective-permute-done.6.other_ref
  11.8 0.3 %base.1.base_ref = f32[4,16,256]{2,1,0:T(8,128)S(1)} custom-call(f32[5,8,8,128]{3,2,1,0:T(8,128)S(1)} %get-tuple-element.24.coarse_ref, f32[5,2,8,128]{3,2,1,0:T(8,128)S(1)} %get-tuple-element.25.outer_ref, f32[26,8,128]{2,1,0:T(8,128)S(1)} %get-tuple-element.26.share_ref, f32[26,8,128]{2,1,0:T(8,128)S(1)} %collective-permute-done.6.other_ref), custom_call_target="tpu_custom_call" | custom-call | tf_op jit(solution)/shard_map/base/pallas_call | solution.py:539
  12.2 1.6 %collective-permute-done.5.state_ref = f32[6,8,128]{2,1,0:T(8,128)S(1)} collective-permute-done((f32[6,8,128]{2,1,0:T(8,128)S(1)}, f32[6,8,128]{2,1,0:T(8,128)S(1)}, u32[]{:S(2)}, u32[]{:S(2)}) %collective-permute-start.5) | collective-permute-done | bytes 24608 | tf_op jit(solution)/shard_map/ppermute | solution.py:522
  13.8 0.9 %output.1 = f32[1,4,16,256]{3,2,1,0:T(8,128)} custom-call(f32[6,8,128]{2,1,0:T(8,128)S(1)} %collective-permute-done.5.state_ref, f32[5,8,8,128]{3,2,1,0:T(8,128)S(1)} %get-tuple-element.24.coarse_ref, f32[5,2,8,128]{3,2,1,0:T(8,128)S(1)} %get-tuple-element.25.outer_ref, f32[26,8,128]{2,1,0:T(8,128)S(1)} %collective-permute-done.6.other_ref, ...), custom_call_target="tpu_custom_call" | custom-call | tf_op jit(solution)/shard_map/output/pallas_call | solution.py:539
  (1 shorter events, 0.0 us)
Async XLA Ops:
  1.1 3.2 %collective-permute-start.1 = (f32[12,8,256]{2,1,0:T(8,128)S(1)}, f32[12,8,256]{2,1,0:T(8,128)S(1)}, u32[]{:S(2)}, u32[]{:S(2)}) collective-permute-start(f32[12,8,256]{2,1,0:T(8,128)S(1)} %get-tuple-element.17), channel_id=1, source_target_pairs={{0,1},{1,0},{2,3},{3,2},{4,5},{5,4},{6,7},{7,6},{8,9},{9,8},{10,11... | collective-permute-start | bytes 294920 | tf_op jit(solution)/shard_map/ppermute | solution.py:489
  1.6 6.3 %collective-permute-start = (f32[14,8,256]{2,1,0:T(8,128)S(1)}, f32[14,8,256]{2,1,0:T(8,128)S(1)}, u32[]{:S(2)}, u32[]{:S(2)}) collective-permute-start(f32[14,8,256]{2,1,0:T(8,128)S(1)} %get-tuple-element.16.own_ref), channel_id=1, source_target_pairs={{5,0},{0,5},{7,2},{2,7},{9,4},{4,9},{11,6},{6,11},{13,8},{8,13},{1... | collective-permute-start | bytes 344072 | tf_op jit(solution)/shard_map/ppermute | solution.py:505
  4.3 4.0 %collective-permute-start.2 = (f32[12,8,256]{2,1,0:T(8,128)S(1)}, f32[12,8,256]{2,1,0:T(8,128)S(1)}, u32[]{:S(2)}, u32[]{:S(2)}) collective-permute-start(f32[12,8,256]{2,1,0:T(8,128)S(1)} %collective-permute-done.1.other_ref), channel_id=1, source_target_pairs={{5,0},{0,5},{7,2},{2,7},{9,4},{4,9},{11,6},{6,11},{13,8},{8,13},{1... | collective-permute-start | bytes 294920 | tf_op jit(solution)/shard_map/ppermute | solution.py:505
  5.2 1.2 %collective-permute-start.3 = (f32[4,8,256]{2,1,0:T(8,128)S(1)}, f32[4,8,256]{2,1,0:T(8,128)S(1)}, u32[]{:S(2)}, u32[]{:S(2)}) collective-permute-start(f32[4,8,256]{2,1,0:T(8,128)S(1)} %get-tuple-element.19), channel_id=1, source_target_pairs={{0,1},{1,0},{2,3},{3,2},{4,5},{5,4},{6,7},{7,6},{8,9},{9,8},{10,11... | collective-permute-start | bytes 98312 | tf_op jit(solution)/shard_map/ppermute | solution.py:489
  9.3 1.2 %collective-permute-start.4 = (f32[3,8,128]{2,1,0:T(8,128)S(1)}, f32[3,8,128]{2,1,0:T(8,128)S(1)}, u32[]{:S(2)}, u32[]{:S(2)}) collective-permute-start(f32[3,8,128]{2,1,0:T(8,128)S(1)} %get-tuple-element.23), channel_id=1, source_target_pairs={{0,1},{1,0},{2,3},{3,2},{4,5},{5,4},{6,7},{7,6},{8,9},{9,8},{10,11... | collective-permute-start | bytes 36872 | tf_op jit(solution)/shard_map/ppermute | solution.py:489
  9.4 2.4 %collective-permute-start.6 = (f32[26,8,128]{2,1,0:T(8,128)S(1)}, f32[26,8,128]{2,1,0:T(8,128)S(1)}, u32[]{:S(2)}, u32[]{:S(2)}) collective-permute-start(f32[26,8,128]{2,1,0:T(8,128)S(1)} %get-tuple-element.26.share_ref), channel_id=1, source_target_pairs={{0,1},{1,0},{2,3},{3,2},{4,5},{5,4},{6,7},{7,6},{8,9},{9,8},{10,11... | collective-permute-start | bytes 319496 | tf_op jit(solution)/shard_map/ppermute | solution.py:489
  10.6 3.3 %collective-permute-start.5 = (f32[6,8,128]{2,1,0:T(8,128)S(1)}, f32[6,8,128]{2,1,0:T(8,128)S(1)}, u32[]{:S(2)}, u32[]{:S(2)}) collective-permute-start(f32[6,8,128]{2,1,0:T(8,128)S(1)} %pad_maximum_fusion), channel_id=1, source_target_pairs={{0,3},{3,0},{1,2},{2,1},{4,7},{7,4},{5,6},{6,5},{8,11},{11,8},{9,1... | collective-permute-start | bytes 73736 | tf_op jit(solution)/shard_map/ppermute | solution.py:522

commit v9 on v8

--- a/solution.py
+++ b/solution.py
@@ -66,6 +66,9 @@
     def fill(mirror):
         for i in range(width):
             row = width - 1 - i if mirror else i
+            if i % 8 == 0:
+                for copy in copies[row // 8 * 2 : row // 8 * 2 + 2]:
+                    copy.wait()
             slab = jnp.concatenate(
                 [u_ref[:, row, :], zone_ref[:, row, :].astype(jnp.float32)], axis=0
             )
@@ -79,13 +82,12 @@
                 head_ref[i] = slab
             else:
                 tail_ref[i - HALO] = slab
+        copies[-1].wait()
         flux = split_lanes(flux_ref[...])
         for i in range(width):
             row = width - 1 - i if mirror else i
             head_ref[HALO + i // 8, i % 8 : i % 8 + 1, :] = flux[row : row + 1]
 
-    for copy in copies:
-        copy.wait()
     core = lax.axis_index("layer")
     pl.when(core == 0)(lambda: fill(True))
     pl.when(core == 1)(lambda: fill(False))

time: 15 us -> 15.1 us (level)
  no operation moved by 1% of the time
where the time goes in v9:
time: 15.1 us; the launch traced here: 14.9 us
  starting transfers between devices  6 us (40%)
  Pallas kernels  4.98 us (33%)
  waiting for transfers between devices  3.87 us (26%)
    pallas_call x5, Pallas kernels, call(): pl.pallas_call(kernel, out_shape=out_shape, in_specs=[pl.BlockSpec(memory...  4.98 us
    ppermute x2, starting transfers between devices, tile_swap(): return lax.ppermute(value, ('tile', 'tm', 'layer'), swap_pairs(pairs))  3.66 us
    ppermute x4, waiting for transfers between devices, layer_swap(): return lax.ppermute(value, 'layer', [(0, 1), (1, 0)])  1.85 us
    ppermute x1, waiting for transfers between devices, cross_swap(): return lax.ppermute(value, ('tm', 'layer'), swap_pairs(pairs))  1.64 us
    ppermute x1, starting transfers between devices, cross_swap(): return lax.ppermute(value, ('tm', 'layer'), swap_pairs(pairs))  1.26 us
    ppermute x4, starting transfers between devices, layer_swap(): return lax.ppermute(value, 'layer', [(0, 1), (1, 0)])  1.08 us
    ppermute x2, waiting for transfers between devices, tile_swap(): return lax.ppermute(value, ('tile', 'tm', 'layer'), swap_pairs(pairs))  0.38 us
  transfers between devices with their start and end apart: 7, of which 4 were waited for; matrix products, arithmetic and copies ran while one was open for 0% of the time, Pallas kernels for 12%

profile of v9, /device:TPU:0, one launch (start us, length us, event | category | flops | bytes accessed | tf_op | source)
XLA Modules:
  0.0 14.9 jit_solution(3131640689883026769)
XLA Ops:
  0.0 1.2 %pack.1 = (f32[14,8,256]{2,1,0:T(8,128)S(1)}, f32[4,8,256]{2,1,0:T(8,128)S(1)}, f32[12,8,256]{2,1,0:T(8,128)S(1)}, f32[4,8,256]{2,1,0:T(8,128)S(1)}) custom-call(f32[4,16,256]{2,1,0:T(8,128)} %bitcast.2, s32[4,16,256]{2,1,0:T(8,128)} %zone_hbm.1, f32[16,256]{1,0:T(8,128)} %bitcast.3), custom_call_target="tpu_custom_call" | custom-call | tf_op jit(solution)/shard_map/pack/pallas_call | solution.py:541
  1.2 0.5 %collective-permute-start.1 = (f32[12,8,256]{2,1,0:T(8,128)S(1)}, f32[12,8,256]{2,1,0:T(8,128)S(1)}, u32[]{:S(2)}, u32[]{:S(2)}) collective-permute-start(f32[12,8,256]{2,1,0:T(8,128)S(1)} %get-tuple-element.17), channel_id=1, source_target_pairs={{0,1},{1,0},{2,3},{3,2},{4,5},{5,4},{6,7},{7,6},{8,9},{9,8},{10,11... | collective-permute-start | bytes 294920 | tf_op jit(solution)/shard_map/ppermute | solution.py:491
  1.7 2.7 %collective-permute-start = (f32[14,8,256]{2,1,0:T(8,128)S(1)}, f32[14,8,256]{2,1,0:T(8,128)S(1)}, u32[]{:S(2)}, u32[]{:S(2)}) collective-permute-start(f32[14,8,256]{2,1,0:T(8,128)S(1)} %get-tuple-element.16.own_ref), channel_id=1, source_target_pairs={{5,0},{0,5},{7,2},{2,7},{9,4},{4,9},{11,6},{6,11},{13,8},{8,13},{1... | collective-permute-start | bytes 344072 | tf_op jit(solution)/shard_map/ppermute | solution.py:507
  4.4 0.0 collective-permute-done.1.other_ref
  4.4 0.9 %collective-permute-start.2 = (f32[12,8,256]{2,1,0:T(8,128)S(1)}, f32[12,8,256]{2,1,0:T(8,128)S(1)}, u32[]{:S(2)}, u32[]{:S(2)}) collective-permute-start(f32[12,8,256]{2,1,0:T(8,128)S(1)} %collective-permute-done.1.other_ref), channel_id=1, source_target_pairs={{5,0},{0,5},{7,2},{2,7},{9,4},{4,9},{11,6},{6,11},{13,8},{8,13},{1... | collective-permute-start | bytes 294920 | tf_op jit(solution)/shard_map/ppermute | solution.py:507
  5.4 0.0 collective-permute-start.3
  5.4 1.2 %collective-permute-done.3.other_tail = f32[4,8,256]{2,1,0:T(8,128)S(1)} collective-permute-done((f32[4,8,256]{2,1,0:T(8,128)S(1)}, f32[4,8,256]{2,1,0:T(8,128)S(1)}, u32[]{:S(2)}, u32[]{:S(2)}) %collective-permute-start.3) | collective-permute-done | bytes 32800 | tf_op jit(solution)/shard_map/ppermute | solution.py:491
  6.6 1.5 %interior.1 = (f32[8,2,8,256]{3,2,1,0:T(8,128)S(1)}, f32[6,9,8,256]{3,2,1,0:T(8,128)S(1)}, f32[5,8,8,128]{3,2,1,0:T(8,128)S(1)}, f32[3,128]{1,0:T(4,128)S(1)}) custom-call(f32[14,8,256]{2,1,0:T(8,128)S(1)} %get-tuple-element.16.own_ref, f32[4,8,256]{2,1,0:T(8,128)S(1)} %get-tuple-element.18.own_tail, f32[12,8,256]{2,1,0:T(8,128)S(1)} %collective-permute-done.1.other_ref, ...), custom_call_target="tpu_custom_call" | custom-call | tf_op jit(solution)/shard_map/interior/pallas_call | solution.py:541
  8.1 0.0 collective-permute-done.recv_ref
  8.1 0.4 %collective-permute-done.2.recv_other = f32[12,8,256]{2,1,0:T(8,128)S(1)} collective-permute-done((f32[12,8,256]{2,1,0:T(8,128)S(1)}, f32[12,8,256]{2,1,0:T(8,128)S(1)}, u32[]{:S(2)}, u32[]{:S(2)}) %collective-permute-start.2) | collective-permute-done | bytes 98336 | tf_op jit(solution)/shard_map/ppermute | solution.py:507
  8.5 1.0 %edge.1 = (f32[3,8,128]{2,1,0:T(8,128)S(1)}, f32[26,8,128]{2,1,0:T(8,128)S(1)}, f32[5,2,8,128]{3,2,1,0:T(8,128)S(1)}) custom-call(f32[14,8,256]{2,1,0:T(8,128)S(1)} %collective-permute-done.recv_ref, f32[12,8,256]{2,1,0:T(8,128)S(1)} %collective-permute-done.2.recv_other, f32[14,8,256]{2,1,0:T(8,128)S(1)} %get-tuple-element.16.own_ref, ...), custom_call_target="tpu_custom_call" | custom-call | tf_op jit(solution)/shard_map/edge/pallas_call | solution.py:541
  9.5 0.1 collective-permute-start.4
  9.6 0.5 %collective-permute-start.6 = (f32[26,8,128]{2,1,0:T(8,128)S(1)}, f32[26,8,128]{2,1,0:T(8,128)S(1)}, u32[]{:S(2)}, u32[]{:S(2)}) collective-permute-start(f32[26,8,128]{2,1,0:T(8,128)S(1)} %get-tuple-element.26.share_ref), channel_id=1, source_target_pairs={{0,1},{1,0},{2,3},{3,2},{4,5},{5,4},{6,7},{7,6},{8,9},{9,8},{10,11... | collective-permute-start | bytes 319496 | tf_op jit(solution)/shard_map/ppermute | solution.py:491
  10.1 0.7 %collective-permute-done.4 = f32[3,8,128]{2,1,0:T(8,128)S(1)} collective-permute-done((f32[3,8,128]{2,1,0:T(8,128)S(1)}, f32[3,8,128]{2,1,0:T(8,128)S(1)}, u32[]{:S(2)}, u32[]{:S(2)}) %collective-permute-start.4) | collective-permute-done | bytes 12320 | tf_op jit(solution)/shard_map/ppermute | solution.py:491
  10.7 1.3 %collective-permute-start.5 = (f32[6,8,128]{2,1,0:T(8,128)S(1)}, f32[6,8,128]{2,1,0:T(8,128)S(1)}, u32[]{:S(2)}, u32[]{:S(2)}) collective-permute-start(f32[6,8,128]{2,1,0:T(8,128)S(1)} %pad_maximum_fusion), channel_id=1, source_target_pairs={{0,3},{3,0},{1,2},{2,1},{4,7},{7,4},{5,6},{6,5},{8,11},{11,8},{9,1... | collective-permute-start | bytes 73736 | tf_op jit(solution)/shard_map/ppermute | solution.py:524
  12.0 0.0 collective-permute-done.6.other_ref
  12.0 0.3 %base.1.base_ref = f32[4,16,256]{2,1,0:T(8,128)S(1)} custom-call(f32[5,8,8,128]{3,2,1,0:T(8,128)S(1)} %get-tuple-element.24.coarse_ref, f32[5,2,8,128]{3,2,1,0:T(8,128)S(1)} %get-tuple-element.25.outer_ref, f32[26,8,128]{2,1,0:T(8,128)S(1)} %get-tuple-element.26.share_ref, f32[26,8,128]{2,1,0:T(8,128)S(1)} %collective-permute-done.6.other_ref), custom_call_target="tpu_custom_call" | custom-call | tf_op jit(solution)/shard_map/base/pallas_call | solution.py:541
  12.3 1.6 %collective-permute-done.5.state_ref = f32[6,8,128]{2,1,0:T(8,128)S(1)} collective-permute-done((f32[6,8,128]{2,1,0:T(8,128)S(1)}, f32[6,8,128]{2,1,0:T(8,128)S(1)}, u32[]{:S(2)}, u32[]{:S(2)}) %collective-permute-start.5) | collective-permute-done | bytes 24608 | tf_op jit(solution)/shard_map/ppermute | solution.py:524
  14.0 0.9 %output.1 = f32[1,4,16,256]{3,2,1,0:T(8,128)} custom-call(f32[6,8,128]{2,1,0:T(8,128)S(1)} %collective-permute-done.5.state_ref, f32[5,8,8,128]{3,2,1,0:T(8,128)S(1)} %get-tuple-element.24.coarse_ref, f32[5,2,8,128]{3,2,1,0:T(8,128)S(1)} %get-tuple-element.25.outer_ref, f32[26,8,128]{2,1,0:T(8,128)S(1)} %collective-permute-done.6.other_ref, ...), custom_call_target="tpu_custom_call" | custom-call | tf_op jit(solution)/shard_map/output/pallas_call | solution.py:541
  (1 shorter events, 0.0 us)
Async XLA Ops:
  1.2 3.2 %collective-permute-start.1 = (f32[12,8,256]{2,1,0:T(8,128)S(1)}, f32[12,8,256]{2,1,0:T(8,128)S(1)}, u32[]{:S(2)}, u32[]{:S(2)}) collective-permute-start(f32[12,8,256]{2,1,0:T(8,128)S(1)} %get-tuple-element.17), channel_id=1, source_target_pairs={{0,1},{1,0},{2,3},{3,2},{4,5},{5,4},{6,7},{7,6},{8,9},{9,8},{10,11... | collective-permute-start | bytes 294920 | tf_op jit(solution)/shard_map/ppermute | solution.py:491
  1.7 6.4 %collective-permute-start = (f32[14,8,256]{2,1,0:T(8,128)S(1)}, f32[14,8,256]{2,1,0:T(8,128)S(1)}, u32[]{:S(2)}, u32[]{:S(2)}) collective-permute-start(f32[14,8,256]{2,1,0:T(8,128)S(1)} %get-tuple-element.16.own_ref), channel_id=1, source_target_pairs={{5,0},{0,5},{7,2},{2,7},{9,4},{4,9},{11,6},{6,11},{13,8},{8,13},{1... | collective-permute-start | bytes 344072 | tf_op jit(solution)/shard_map/ppermute | solution.py:507
  4.4 4.0 %collective-permute-start.2 = (f32[12,8,256]{2,1,0:T(8,128)S(1)}, f32[12,8,256]{2,1,0:T(8,128)S(1)}, u32[]{:S(2)}, u32[]{:S(2)}) collective-permute-start(f32[12,8,256]{2,1,0:T(8,128)S(1)} %collective-permute-done.1.other_ref), channel_id=1, source_target_pairs={{5,0},{0,5},{7,2},{2,7},{9,4},{4,9},{11,6},{6,11},{13,8},{8,13},{1... | collective-permute-start | bytes 294920 | tf_op jit(solution)/shard_map/ppermute | solution.py:507
  5.4 1.2 %collective-permute-start.3 = (f32[4,8,256]{2,1,0:T(8,128)S(1)}, f32[4,8,256]{2,1,0:T(8,128)S(1)}, u32[]{:S(2)}, u32[]{:S(2)}) collective-permute-start(f32[4,8,256]{2,1,0:T(8,128)S(1)} %get-tuple-element.19), channel_id=1, source_target_pairs={{0,1},{1,0},{2,3},{3,2},{4,5},{5,4},{6,7},{7,6},{8,9},{9,8},{10,11... | collective-permute-start | bytes 98312 | tf_op jit(solution)/shard_map/ppermute | solution.py:491
  9.5 1.2 %collective-permute-start.4 = (f32[3,8,128]{2,1,0:T(8,128)S(1)}, f32[3,8,128]{2,1,0:T(8,128)S(1)}, u32[]{:S(2)}, u32[]{:S(2)}) collective-permute-start(f32[3,8,128]{2,1,0:T(8,128)S(1)} %get-tuple-element.23), channel_id=1, source_target_pairs={{0,1},{1,0},{2,3},{3,2},{4,5},{5,4},{6,7},{7,6},{8,9},{9,8},{10,11... | collective-permute-start | bytes 36872 | tf_op jit(solution)/shard_map/ppermute | solution.py:491
  9.6 2.4 %collective-permute-start.6 = (f32[26,8,128]{2,1,0:T(8,128)S(1)}, f32[26,8,128]{2,1,0:T(8,128)S(1)}, u32[]{:S(2)}, u32[]{:S(2)}) collective-permute-start(f32[26,8,128]{2,1,0:T(8,128)S(1)} %get-tuple-element.26.share_ref), channel_id=1, source_target_pairs={{0,1},{1,0},{2,3},{3,2},{4,5},{5,4},{6,7},{7,6},{8,9},{9,8},{10,11... | collective-permute-start | bytes 319496 | tf_op jit(solution)/shard_map/ppermute | solution.py:491
  10.7 3.3 %collective-permute-start.5 = (f32[6,8,128]{2,1,0:T(8,128)S(1)}, f32[6,8,128]{2,1,0:T(8,128)S(1)}, u32[]{:S(2)}, u32[]{:S(2)}) collective-permute-start(f32[6,8,128]{2,1,0:T(8,128)S(1)} %pad_maximum_fusion), channel_id=1, source_target_pairs={{0,3},{3,0},{1,2},{2,1},{4,7},{7,4},{5,6},{6,5},{8,11},{11,8},{9,1... | collective-permute-start | bytes 73736 | tf_op jit(solution)/shard_map/ppermute | solution.py:524
